TPU v7x, 32 devices: a whole 2x2x4 slice. The times are simulated.
32 devices in a mesh: ctx: 8 (over z, x), fsdp: 4 (over y, core).
Axes of the slice: x: 2, y: 2, z: 4, core: 2. Of those that a mesh axis runs over, the one named last changes fastest.
Arguments:
- hidden: bfloat16 [4, 1024, 768], P('fsdp', 'ctx'), may hold values from -6 to 6
- project_in: bfloat16 [768, 2304], P('fsdp', 'ctx'), may hold values from -0.21875 to 0.21875
- project_out: bfloat16 [768, 768], P('fsdp', 'ctx'), may hold values from -3.5 to 3.5
- expand_weight: bfloat16 [768, 3072], P('fsdp', 'ctx'), may hold values from -0.21875 to 0.21875
- shrink_weight: bfloat16 [3072, 768], P('fsdp', 'ctx'), may hold values from -0.109375 to 0.109375
- biases: bfloat16 [6, 768], P(None, 'ctx'), may hold values from -3 to 3
- gains: bfloat16 [2, 768], P(None, 'ctx'), may hold values from 0.5 to 1.5
- expand_bias: bfloat16 [3072], P('ctx'), may hold values from -3 to 3
- random_blocks: int32 [4, 16, 3], P('fsdp', 'ctx'), may hold values from 0 to 15
- global_blocks: int32 [4, 2], P('fsdp'), may hold values from 0 to 15
- document_lengths: int32 [4, 8], P('fsdp'), may hold values from 1 to 897, as said below
- cotangent: bfloat16 [4, 1024, 768], P('fsdp', 'ctx'), may hold values from -6 to 6
Outputs:
- output: bfloat16 [4, 1024, 768], P('fsdp', 'ctx')
- grad_hidden: bfloat16 [4, 1024, 768], P('fsdp', 'ctx')
- grad_project_in: float32 [768, 2304], P('fsdp', 'ctx')
- grad_project_out: float32 [768, 768], P('fsdp', 'ctx')
- grad_expand: float32 [768, 3072], P('fsdp', 'ctx')
- grad_shrink: float32 [3072, 768], P('fsdp', 'ctx')
- grad_biases: float32 [6, 768], P(None, 'ctx')
- grad_gains: float32 [2, 768], P(None, 'ctx')
- grad_expand_bias: float32 [3072], P('ctx')
Inputs may be any that keep to these rules, and one draw needn't show every extreme that they name: `document_lengths`: each sequence's 8 lengths add up to 1024; exactly one document has the largest length, 897, and the others together have 128 - 1 tokens.
All inputs are finite; a program needn't handle non-finite values.
Results may differ from a plain program's by a relative error of at most 0.015.
Values may be sent and summed in bfloat16 or wider, within the bound.
A program may use at most 192 MiB of HBM per device.

v0:
```python
import jax
import jax.numpy as jnp
from jax import lax
from jax.sharding import PartitionSpec as P

HEAD_DIM = 64
BLOCK = 64


def segment_of(positions, bounds):
    return jnp.sum((positions[..., None] >= bounds).astype(jnp.int32), axis=-1)


def layer_norm_parts(values, gain_row, shift_row):
    centre = values - jnp.mean(values, axis=-1, keepdims=True)
    inverse = lax.rsqrt(jnp.mean(centre * centre, axis=-1, keepdims=True) + 1e-05)
    normed = centre * inverse
    return (normed * gain_row + shift_row, normed, inverse)


def layer_norm_back(upstream, normed, inverse, gain_row):
    scaled = upstream * gain_row
    return inverse * (
        scaled
        - jnp.mean(scaled, axis=-1, keepdims=True)
        - normed * jnp.mean(scaled * normed, axis=-1, keepdims=True)
    )


def matmul(left_side, right_side):
    return jnp.dot(left_side, right_side, preferred_element_type=jnp.float32)


def matmul_left_t(left_side, right_side):
    return lax.dot_general(
        left_side, right_side, (((0,), (0,)), ((), ())), preferred_element_type=jnp.float32
    )


def matmul_right_t(left_side, right_side):
    return lax.dot_general(
        left_side, right_side, (((1,), (1,)), ((), ())), preferred_element_type=jnp.float32
    )


def over_cols(qkv_grad, out_grad, expand_grad, shrink_grad, vector_grad, gain_grad, inner_grad):
    return (
        lax.psum_scatter(qkv_grad, "ctx", scatter_dimension=1, tiled=True),
        lax.psum_scatter(out_grad, "ctx", scatter_dimension=1, tiled=True),
        lax.psum_scatter(expand_grad, "ctx", scatter_dimension=1, tiled=True),
        lax.psum_scatter(shrink_grad, "ctx", scatter_dimension=1, tiled=True),
        lax.psum_scatter(vector_grad, "ctx", scatter_dimension=1, tiled=True),
        lax.psum_scatter(gain_grad, "ctx", scatter_dimension=1, tiled=True),
        lax.psum_scatter(inner_grad, "ctx", scatter_dimension=1, tiled=True),
    )


def over_rows(qkv_grad, out_grad, expand_grad, shrink_grad):
    return (
        lax.psum_scatter(
            qkv_grad.astype(jnp.bfloat16), "fsdp", scatter_dimension=0, tiled=True
        ).astype(jnp.float32),
        lax.psum_scatter(
            out_grad.astype(jnp.bfloat16), "fsdp", scatter_dimension=0, tiled=True
        ).astype(jnp.float32),
        lax.psum_scatter(
            expand_grad.astype(jnp.bfloat16), "fsdp", scatter_dimension=0, tiled=True
        ).astype(jnp.float32),
        lax.psum_scatter(
            shrink_grad.astype(jnp.bfloat16), "fsdp", scatter_dimension=0, tiled=True
        ).astype(jnp.float32),
    )


def scatter_rows(link_ids, link_grads, row_count, feature_width):
    block_count = row_count // BLOCK
    inside = (link_ids >= 0) & (link_ids < block_count)
    target = jnp.where(inside, link_ids, block_count).reshape(-1)
    partial_value = jnp.zeros((block_count, BLOCK, feature_width), jnp.float32)
    partial_value = partial_value.at[target].add(
        link_grads.reshape(-1, BLOCK, feature_width), mode="drop"
    )
    return partial_value.reshape(row_count, feature_width)


def shards(
    hidden,
    project_in,
    project_out,
    expand_weight,
    shrink_weight,
    biases,
    gains,
    expand_bias,
    random_blocks,
    global_blocks,
    document_lengths,
    cotangent,
):
    inputs = hidden[0]
    tokens_here = inputs.shape[0]
    width = inputs.shape[1]
    head_count = width // HEAD_DIM
    blocks_here = tokens_here // BLOCK
    rand_count = random_blocks.shape[2]
    link_count = 3 + rand_count + global_blocks.shape[1]
    ctx_rank = lax.axis_index("ctx")
    last_block = tokens_here * lax.axis_size("ctx") // BLOCK - 1
    col_full = (
        lax.all_gather(project_in, "ctx", axis=1, tiled=True),
        lax.all_gather(project_out, "ctx", axis=1, tiled=True),
        lax.all_gather(expand_weight, "ctx", axis=1, tiled=True),
        lax.all_gather(shrink_weight, "ctx", axis=1, tiled=True),
        lax.all_gather(biases, "ctx", axis=1, tiled=True),
        lax.all_gather(gains, "ctx", axis=1, tiled=True),
        lax.all_gather(expand_bias.reshape(1, -1), "ctx", axis=1, tiled=True),
    )
    full_qkv, full_out, full_expand, full_shrink = (
        lax.all_gather(col_full[0], "fsdp", axis=0, tiled=True),
        lax.all_gather(col_full[1], "fsdp", axis=0, tiled=True),
        lax.all_gather(col_full[2], "fsdp", axis=0, tiled=True),
        lax.all_gather(col_full[3], "fsdp", axis=0, tiled=True),
    )
    vectors = col_full[4].astype(jnp.float32)
    gain_rows = col_full[5].astype(jnp.float32)
    inner_bias = col_full[6][0].astype(jnp.float32)
    block_ids = ctx_rank * blocks_here + jnp.arange(blocks_here, dtype=jnp.int32)
    window = jnp.stack(
        [jnp.maximum(block_ids - 1, 0), block_ids, jnp.minimum(block_ids + 1, last_block)], axis=1
    )
    global_links = jnp.broadcast_to(
        global_blocks[0][None, :], (blocks_here, global_blocks.shape[1])
    )
    linked_ids = jnp.concatenate([window, random_blocks[0], global_links], axis=1)
    bounds = jnp.cumsum(document_lengths[0])[:-1]
    query_pos = (ctx_rank * tokens_here + jnp.arange(tokens_here, dtype=jnp.int32)).reshape(
        blocks_here, BLOCK
    )
    query_seg = segment_of(query_pos, bounds)
    key_pos = linked_ids[:, :, None] * BLOCK + jnp.arange(BLOCK, dtype=jnp.int32)[None, None, :]
    key_seg = segment_of(key_pos, bounds).reshape(blocks_here, -1)
    allowed = query_seg[:, None, :, None] == key_seg[:, None, None, :]
    zero_row = jnp.zeros((width,), jnp.float32)
    mixed_qkv = (
        matmul(inputs, full_qkv) + jnp.concatenate([vectors[0], zero_row, vectors[1]])
    ).astype(jnp.bfloat16)
    queries = mixed_qkv[:, :width]
    keyvals = mixed_qkv[:, width:]
    blank_slots = jnp.zeros((blocks_here, link_count, BLOCK, 2 * width), jnp.bfloat16)
    shard_piece = lax.all_gather(keyvals, "ctx", axis=0, tiled=True)
    block_count = shard_piece.shape[0] // BLOCK
    stacked = shard_piece.reshape(block_count, BLOCK, shard_piece.shape[1])
    inside = (linked_ids >= 0) & (linked_ids < block_count)
    fetched = jnp.take(
        stacked, jnp.clip(linked_ids, 0, block_count - 1).reshape(-1), axis=0
    ).reshape(blank_slots.shape)
    linked = jnp.where(inside[:, :, None, None], fetched, blank_slots)
    query_heads = queries.reshape(blocks_here, BLOCK, head_count, HEAD_DIM)
    key_heads = linked[..., :width].reshape(blocks_here, link_count * BLOCK, head_count, HEAD_DIM)
    value_heads = linked[..., width:].reshape(blocks_here, link_count * BLOCK, head_count, HEAD_DIM)

    def score_parts():
        raw_scores = (
            jnp.einsum(
                "bqhd,bkhd->bhqk", query_heads, key_heads, preferred_element_type=jnp.float32
            )
            * 0.125
        )
        return jnp.where(allowed, raw_scores, -1e30)

    scores = score_parts()
    top_score = jnp.max(scores, axis=-1, keepdims=True)
    exp_total = jnp.sum(jnp.exp(scores - top_score), axis=-1, keepdims=True)
    attention = jnp.exp(scores - top_score) / exp_total
    attended = jnp.einsum(
        "bhqk,bkhd->bqhd",
        attention.astype(jnp.bfloat16),
        value_heads,
        preferred_element_type=jnp.float32,
    )
    attended = attended.reshape(tokens_here, width).astype(jnp.bfloat16)
    residual_one = inputs.astype(jnp.float32) + matmul(attended, full_out) + vectors[2]
    hidden_one, normed_one, inverse_one = layer_norm_parts(residual_one, gain_rows[0], vectors[3])
    hidden_low = hidden_one.astype(jnp.bfloat16)
    inner_pre = matmul(hidden_low, full_expand) + inner_bias
    activated, gelu_pull = jax.vjp(
        lambda argument: jax.nn.gelu(argument, approximate=False), inner_pre
    )
    active_low = activated.astype(jnp.bfloat16)
    residual_two = hidden_one + matmul(active_low, full_shrink) + vectors[4]
    result, normed_two, inverse_two = layer_norm_parts(residual_two, gain_rows[1], vectors[5])
    upstream = cotangent[0].astype(jnp.float32)
    grad_gain_two = jnp.sum(upstream * normed_two, axis=0)
    grad_shift_two = jnp.sum(upstream, axis=0)
    grad_two = layer_norm_back(upstream, normed_two, inverse_two, gain_rows[1])
    grad_bias_back = jnp.sum(grad_two, axis=0)
    grad_two_low = grad_two.astype(jnp.bfloat16)
    again_cols = (
        lax.all_gather(project_in, "ctx", axis=1, tiled=True),
        lax.all_gather(project_out, "ctx", axis=1, tiled=True),
        lax.all_gather(expand_weight, "ctx", axis=1, tiled=True),
        lax.all_gather(shrink_weight, "ctx", axis=1, tiled=True),
    )
    back_weights = (
        lax.all_gather(again_cols[0], "fsdp", axis=0, tiled=True),
        lax.all_gather(again_cols[1], "fsdp", axis=0, tiled=True),
        lax.all_gather(again_cols[2], "fsdp", axis=0, tiled=True),
        lax.all_gather(again_cols[3], "fsdp", axis=0, tiled=True),
    )
    back_qkv, back_out, back_expand, back_shrink = back_weights
    grad_shrink_w = matmul_left_t(active_low, grad_two_low)
    grad_active = matmul_right_t(grad_two_low, back_shrink)
    grad_inner = gelu_pull(grad_active)[0]
    grad_inner_bias = jnp.sum(grad_inner, axis=0)
    grad_inner_low = grad_inner.astype(jnp.bfloat16)
    grad_expand_w = matmul_left_t(hidden_low, grad_inner_low)
    grad_hidden_one = grad_two + matmul_right_t(grad_inner_low, back_expand)
    grad_gain_one = jnp.sum(grad_hidden_one * normed_one, axis=0)
    grad_shift_one = jnp.sum(grad_hidden_one, axis=0)
    grad_one = layer_norm_back(grad_hidden_one, normed_one, inverse_one, gain_rows[0])
    grad_bias_out = jnp.sum(grad_one, axis=0)
    grad_one_low = grad_one.astype(jnp.bfloat16)
    grad_out_w = matmul_left_t(attended, grad_one_low)
    grad_attended = matmul_right_t(grad_one_low, back_out).astype(jnp.bfloat16)
    grad_attended = grad_attended.reshape(blocks_here, BLOCK, head_count, HEAD_DIM)
    scores = score_parts()
    attention = jnp.exp(scores - top_score) / exp_total
    grad_attention = jnp.einsum(
        "bqhd,bkhd->bhqk", grad_attended, value_heads, preferred_element_type=jnp.float32
    )
    grad_values = jnp.einsum(
        "bhqk,bqhd->bkhd",
        attention.astype(jnp.bfloat16),
        grad_attended,
        preferred_element_type=jnp.float32,
    )
    row_inner = jnp.sum(attention * grad_attention, axis=-1, keepdims=True)
    grad_scores = (attention * (grad_attention - row_inner) * 0.125).astype(jnp.bfloat16)
    grad_queries = jnp.einsum(
        "bhqk,bkhd->bqhd", grad_scores, key_heads, preferred_element_type=jnp.float32
    ).reshape(tokens_here, width)
    grad_keys = jnp.einsum(
        "bhqk,bqhd->bkhd", grad_scores, query_heads, preferred_element_type=jnp.float32
    )
    slot_grads = jnp.concatenate(
        [
            grad_keys.reshape(blocks_here, link_count, BLOCK, width),
            grad_values.reshape(blocks_here, link_count, BLOCK, width),
        ],
        axis=-1,
    )
    grad_keyvals = lax.psum_scatter(
        scatter_rows(linked_ids, slot_grads, tokens_here * lax.axis_size("ctx"), 2 * width),
        "ctx",
        scatter_dimension=0,
        tiled=True,
    )
    grad_mixed = jnp.concatenate([grad_queries, grad_keyvals], axis=1)
    grad_bias_query = jnp.sum(grad_queries, axis=0)
    grad_bias_value = jnp.sum(grad_keyvals[:, width:], axis=0)
    grad_mixed_low = grad_mixed.astype(jnp.bfloat16)
    grad_qkv_w = matmul_left_t(inputs, grad_mixed_low)
    grad_inputs = grad_one + matmul_right_t(grad_mixed_low, back_qkv)
    grad_vectors = jnp.stack(
        [
            grad_bias_query,
            grad_bias_value,
            grad_bias_out,
            grad_shift_one,
            grad_bias_back,
            grad_shift_two,
        ]
    )
    grad_gain_rows = jnp.stack([grad_gain_one, grad_gain_two])
    grad_inner_row = grad_inner_bias[None, :]
    reduced = over_cols(
        grad_qkv_w,
        grad_out_w,
        grad_expand_w,
        grad_shrink_w,
        grad_vectors,
        grad_gain_rows,
        grad_inner_row,
    )
    sum_qkv, sum_out, sum_expand, sum_shrink = over_rows(
        reduced[0], reduced[1], reduced[2], reduced[3]
    )
    final_vectors, final_gains, final_inner = lax.psum((reduced[4], reduced[5], reduced[6]), "fsdp")
    return (
        result.astype(jnp.bfloat16)[None],
        grad_inputs.astype(jnp.bfloat16)[None],
        sum_qkv,
        sum_out,
        sum_expand,
        sum_shrink,
        final_vectors,
        final_gains,
        final_inner.reshape(-1),
    )


def solution(mesh):
    return jax.shard_map(
        shards,
        mesh=mesh,
        in_specs=(
            P("fsdp", "ctx", None),
            P("fsdp", "ctx"),
            P("fsdp", "ctx"),
            P("fsdp", "ctx"),
            P("fsdp", "ctx"),
            P(None, "ctx"),
            P(None, "ctx"),
            P("ctx"),
            P("fsdp", "ctx", None),
            P("fsdp", None),
            P("fsdp", None),
            P("fsdp", "ctx", None),
        ),
        out_specs=(
            P("fsdp", "ctx", None),
            P("fsdp", "ctx", None),
            P("fsdp", "ctx"),
            P("fsdp", "ctx"),
            P("fsdp", "ctx"),
            P("fsdp", "ctx"),
            P(None, "ctx"),
            P(None, "ctx"),
            P("ctx"),
        ),
        check_vma=False,
    )
```

profile of v0, /device:TPU:0, one launch (start us, length us, event | category | flops | bytes accessed | tf_op | source)
XLA Modules:
  0.0 1371.1 jit_solution(5716698652214751825)
XLA Ops:
  8.2 35.3 %all_gather.44 = bf16[192,2304]{0,1:T(8,128)(2,1)S(1)} all-gather(bf16[192,288]{0,1:T(8,128)(2,1)S(1)} %copy.125), channel_id=1, replica_groups=mesh['ctx'=8,'fsdp'=4] {'ctx'}, dimensions={1}, use_global_device_ids=true | all-gather | bytes 995328 | tf_op jit(solution)/shard_map/all_gather | solution.py:110
  46.5 26.0 %all-gather.1 = bf16[8,96,6]{1,2,0:T(8,128)(2,1)S(1)} all-gather(bf16[1,96,6]{1,2,0:T(8,128)(2,1)S(1)} %bitcast.130), channel_id=1, replica_groups=mesh['ctx'=8,'fsdp'=4] {'ctx'}, dimensions={0}, use_global_device_ids=true | all-gather | bytes 10368 | tf_op jit(solution)/shard_map/all_gather | solution.py:114
  80.0 31.7 %all_gather.48 = bf16[192,768]{0,1:T(8,128)(2,1)S(1)} all-gather(bf16[192,96]{0,1:T(8,128)(2,1)S(1)} %copy.133), channel_id=1, replica_groups=mesh['ctx'=8,'fsdp'=4] {'ctx'}, dimensions={1}, use_global_device_ids=true | all-gather | bytes 331776 | tf_op jit(solution)/shard_map/all_gather | solution.py:111
  112.7 8.1 all-gather.18.cloned.1.call-done
  120.8 42.5 %all-gather.22.cloned.1.call-done = bf16[768,768]{0,1:T(8,128)(2,1)} async-done(((bf16[768,96]{0,1:T(8,128)(2,1)}), bf16[768,768]{0,1:T(8,128)(2,1)}) %all-gather.22.cloned.1.call-update) | async-done | bytes 1179664 | tf_op jit(solution)/shard_map/all_gather | solution.py:113
  163.7 18.2 %all-gather.2 = bf16[8,96,2]{1,2,0:T(2,128)(2,1)S(1)} all-gather(bf16[1,96,2]{1,2,0:T(2,128)(2,1)S(1)} %bitcast.132), channel_id=1, replica_groups=mesh['ctx'=8,'fsdp'=4] {'ctx'}, dimensions={0}, use_global_device_ids=true | all-gather | bytes 3456 | tf_op jit(solution)/shard_map/all_gather | solution.py:115
  182.4 26.3 %all-gather.3 = bf16[8,1,384]{2,1,0:T(2,128)(2,1)S(1)} all-gather(bf16[1,1,384]{2,1,0:T(2,128)(2,1)S(1)} %reshape.367), channel_id=2, replica_groups=mesh['ctx'=8,'fsdp'=4] {'ctx'}, dimensions={0}, use_global_device_ids=true | all-gather | bytes 6912 | tf_op jit(solution)/shard_map/all_gather | solution.py:116
  211.0 13.7 %all-gather.14.cloned.1.call-done = bf16[1024,1536]{1,0:T(8,128)(2,1)} async-done(((bf16[128,1536]{1,0:T(8,128)(2,1)}), bf16[1024,1536]{1,0:T(8,128)(2,1)}) %all-gather.14.cloned.1.call-update) | async-done | bytes 3145744 | tf_op jit(solution)/shard_map/all_gather | solution.py:150
  252.2 29.6 %all-gather.20.cloned.1.call-done = bf16[768,3072]{1,0:T(8,128)(2,1)} async-done(((bf16[192,3072]{1,0:T(8,128)(2,1)}), bf16[768,3072]{1,0:T(8,128)(2,1)}) %all-gather.20.cloned.1.call-update) | async-done | bytes 4718608 | tf_op jit(solution)/shard_map/all_gather | solution.py:121
  281.8 7.6 multiply_convert_fusion.1
  289.4 31.4 %all-gather.24.cloned.1.call-done = bf16[3072,768]{0,1:T(8,128)(2,1)} async-done(((bf16[768,768]{0,1:T(8,128)(2,1)}), bf16[3072,768]{0,1:T(8,128)(2,1)}) %all-gather.24.cloned.1.call-update) | async-done | bytes 4718608 | tf_op jit(solution)/shard_map/all_gather | solution.py:122
  342.3 15.3 %fusion.13 = f32[2,512,12,64]{1,3,2,0:T(8,128)} fusion(bf16[2,64,12,64]{1,3,2,0:T(8,128)(2,1)S(1)} %copy-done.22, f32[2,12,64,512]{3,2,1,0:T(8,128)} %fusion.88, f32[2,12,64,512]{3,2,1,0:T(8,128)} %get-tuple-element.104, f32[2,12,64]{2,1,0:T(8,128)S(1)} %get-tuple-element.103), kind=kOutput, calls=%fused_computation.19 | convolution fusion | flops 106170368 | bytes 9639936 | tf_op jit(solution)/shard_map/bhqk,bqhd->bkhd/dot_general | solution.py:242
  366.1 6.7 concatenate.40
  372.9 5.2 concatenate.41
  378.1 12.3 pad_maximum_fusion
  390.4 9.8 copy.143
  403.6 15.0 %scatter_fusion = f32[16,64,1536]{2,1,0:T(8,128)} fusion(f32[16,64,1536]{2,1,0:T(8,128)} %broadcast_in_dim.86, s32[16]{0:T(128)S(1)} %copy-done.34, f32[16,64,1536]{2,1,0:T(8,128)} %copy.143), kind=kCustom, calls=%fused_computation.1 | custom fusion | flops 1572864 | bytes 18874432 | tf_op jit(solution)/shard_map/scatter-add | solution.py:80
  422.7 5.2 fusion.46
  435.6 13.3 fusion.81
  449.5 87.5 %reduce-scatter.23.cloned.1.call-done = f32[128,1536]{1,0:T(8,128)} async-done(((f32[1024,1536]{1,0:T(8,128)}), f32[128,1536]{1,0:T(8,128)}) %reduce-scatter.23.cloned.1.call-update) | async-done | bytes 786448 | tf_op jit(solution)/shard_map/reduce_scatter | solution.py:252
  546.7 61.9 %reduce-scatter.27.cloned.1.call-done = f32[768,96]{0,1:T(8,128)} async-done(((f32[768,768]{0,1:T(8,128)}), f32[768,96]{0,1:T(8,128)}) %reduce-scatter.27.cloned.1.call-update) | async-done | bytes 294928 | tf_op jit(solution)/shard_map/reduce_scatter | solution.py:49
  611.7 162.8 %reduce-scatter.29.cloned.1.call-done = f32[768,384]{1,0:T(8,128)} async-done(((f32[768,3072]{1,0:T(8,128)}), f32[768,384]{1,0:T(8,128)}) %reduce-scatter.29.cloned.1.call-update) | async-done | bytes 1179664 | tf_op jit(solution)/shard_map/reduce_scatter | solution.py:50
  776.7 163.9 %reduce-scatter.33.cloned.1.call-done = f32[3072,96]{0,1:T(8,128)} async-done(((f32[3072,768]{0,1:T(8,128)}), f32[3072,96]{0,1:T(8,128)}) %reduce-scatter.33.cloned.1.call-update) | async-done | bytes 1179664 | tf_op jit(solution)/shard_map/reduce_scatter | solution.py:51
  942.9 129.4 %reduce-scatter.25.cloned.1.call-done = f32[768,288]{0,1:T(8,128)} async-done(((f32[768,2304]{0,1:T(8,128)}), f32[768,288]{0,1:T(8,128)}) %reduce-scatter.25.cloned.1.call-update) | async-done | bytes 884752 | tf_op jit(solution)/shard_map/reduce_scatter | solution.py:48
  1076.4 60.0 %reduce-scatter.43.cloned.1.call-done = f32[96,2]{1,0:T(8,128)} async-done(((f32[768,2]{1,0:T(8,128)}), f32[96,2]{1,0:T(8,128)}) %reduce-scatter.43.cloned.1.call-update) | async-done | bytes 784
  1137.3 66.7 %reduce-scatter.45.cloned.1.call-done = f32[384,1]{1,0:T(8,128)} async-done(((f32[3072,1]{1,0:T(8,128)}), f32[384,1]{1,0:T(8,128)}) %reduce-scatter.45.cloned.1.call-update) | async-done | bytes 1552
  1205.1 20.4 %reduce-scatter.39.cloned.1.call-done = bf16[192,96]{1,0:T(8,128)(2,1)} async-done(((bf16[768,96]{1,0:T(8,128)(2,1)}), bf16[192,96]{1,0:T(8,128)(2,1)}) %reduce-scatter.39.cloned.1.call-update) | async-done | bytes 36880
  1231.7 58.3 %reduce-scatter.41.cloned.1.call-done = f32[96,6]{1,0:T(8,128)} async-done(((f32[768,6]{1,0:T(8,128)}), f32[96,6]{1,0:T(8,128)}) %reduce-scatter.41.cloned.1.call-update) | async-done | bytes 2320
  1290.9 6.3 all-reduce
  1297.2 16.3 %reduce-scatter.31.cloned.1.call-done = bf16[192,384]{1,0:T(8,128)(2,1)} async-done(((bf16[768,384]{1,0:T(8,128)(2,1)}), bf16[192,384]{1,0:T(8,128)(2,1)}) %reduce-scatter.31.cloned.1.call-update) | async-done | bytes 147472 | tf_op jit(solution)/shard_map/reduce_scatter | solution.py:66
  1315.1 22.8 %reduce-scatter.35.cloned.1.call-done = bf16[768,96]{0,1:T(8,128)(2,1)} async-done(((bf16[3072,96]{0,1:T(8,128)(2,1)}), bf16[768,96]{0,1:T(8,128)(2,1)}) %reduce-scatter.35.cloned.1.call-update) | async-done | bytes 147472 | tf_op jit(solution)/shard_map/reduce_scatter | solution.py:69
  1339.5 22.9 %reduce-scatter.37.cloned.1.call-done = bf16[192,288]{1,0:T(8,128)(2,1)} async-done(((bf16[768,288]{1,0:T(8,128)(2,1)}), bf16[192,288]{1,0:T(8,128)(2,1)}) %reduce-scatter.37.cloned.1.call-update) | async-done | bytes 110608
  (243 shorter events, 123.7 us)
Async XLA Ops:
  7.2 69.2 %all-gather.12.cloned.1.call-start = ((), (), s32[]{:S(2)}) async-start(), calls=%async_computation.12 | async-start | bytes 4423680 | tf_op jit(solution)/shard_map/all_gather | solution.py:119
  44.9 75.9 %all-gather.18.cloned.1.call-start = ((), (), s32[]{:S(2)}) async-start(), calls=%async_computation.15 | async-start | bytes 1327104 | tf_op jit(solution)/shard_map/all_gather | solution.py:112
  45.7 117.7 %all-gather.22.cloned.1.call-start = ((), (), s32[]{:S(2)}) async-start(), calls=%async_computation.17 | async-start | bytes 1327104 | tf_op jit(solution)/shard_map/all_gather | solution.py:113
  46.4 178.4 %all-gather.14.cloned.1.call-start = ((), (), s32[]{:S(2)}) async-start(), calls=%async_computation.13 | async-start | bytes 3538944 | tf_op jit(solution)/shard_map/all_gather | solution.py:150
  79.9 170.2 %all-gather.16.cloned.1.call-start = ((), (), s32[]{:S(2)}) async-start(), calls=%async_computation.14 | async-start | bytes 1474560 | tf_op jit(solution)/shard_map/all_gather | solution.py:120
  111.7 51.8 %copy-start.36 = (s32[1,2]{1,0:T(1,128)S(1)}, s32[1,2]{1,0:T(1,128)}, u32[]{:S(2)}) copy-start(s32[1,2]{1,0:T(1,128)} %param.21) | copy-start | bytes 28
  111.7 51.8 %copy-start.33 = (s32[1,2,3]{2,1,0:T(2,128)S(1)}, s32[1,2,3]{2,1,0:T(2,128)}, u32[]{:S(2)}) copy-start(s32[1,2,3]{2,1,0:T(2,128)} %param.20) | copy-start | bytes 76
  111.7 52.0 %copy-start.35 = (bf16[2,96]{1,0:T(2,128)(2,1)S(1)}, bf16[2,96]{1,0:T(2,128)(2,1)}, u32[]{:S(2)}) copy-start(bf16[2,96]{1,0:T(2,128)(2,1)} %param.18) | copy-start | bytes 1156
  111.7 70.3 %copy-start.37 = (s32[1,8]{1,0:T(1,128)S(1)}, s32[1,8]{1,0:T(1,128)}, u32[]{:S(2)}) copy-start(s32[1,8]{1,0:T(1,128)} %param.22) | copy-start | bytes 100
  112.6 169.2 %all-gather.20.cloned.1.call-start = ((), (), s32[]{:S(2)}) async-start(), calls=%async_computation.16 | async-start | bytes 5898240 | tf_op jit(solution)/shard_map/all_gather | solution.py:121
  120.8 200.1 %all-gather.24.cloned.1.call-start = ((), (), s32[]{:S(2)}) async-start(), calls=%async_computation.18 | async-start | bytes 5898240 | tf_op jit(solution)/shard_map/all_gather | solution.py:122
  163.3 373.7 %reduce-scatter.23.cloned.1.call-start = ((), (), s32[]{:S(2)}) async-start(), calls=%async_computation.19 | async-start | bytes 7077888 | tf_op jit(solution)/shard_map/reduce_scatter | solution.py:252
  246.8 95.4 %copy-start.39 = (f32[2,12,64]{2,1,0:T(8,128)}, f32[2,12,64]{2,1,0:T(8,128)S(1)}, u32[]{:S(2)}) copy-start(f32[2,12,64]{2,1,0:T(8,128)S(1)} %get-tuple-element.103) | copy-start | bytes 18436
  252.1 82.3 %copy-start.28 = (f32[128]{0:T(128)}, f32[128]{0:T(128)S(1)}, u32[]{:S(2)}) copy-start(f32[128]{0:T(128)S(1)} %add_rsqrt_fusion.1) | copy-start | bytes 1540
  418.6 190.0 %reduce-scatter.27.cloned.1.call-start = ((), (), s32[]{:S(2)}) async-start(), calls=%async_computation.21 | async-start | bytes 2654208 | tf_op jit(solution)/shard_map/reduce_scatter | solution.py:49
  421.6 352.9 %reduce-scatter.29.cloned.1.call-start = ((), (), s32[]{:S(2)}) async-start(), calls=%async_computation.22 | async-start | bytes 10616832 | tf_op jit(solution)/shard_map/reduce_scatter | solution.py:50
  427.9 512.7 %reduce-scatter.33.cloned.1.call-start = ((), (), s32[]{:S(2)}) async-start(), calls=%async_computation.24 | async-start | bytes 10616832 | tf_op jit(solution)/shard_map/reduce_scatter | solution.py:51
  434.2 638.1 %reduce-scatter.25.cloned.1.call-start = ((), (), s32[]{:S(2)}) async-start(), calls=%async_computation.20 | async-start | bytes 7962624 | tf_op jit(solution)/shard_map/reduce_scatter | solution.py:48
  448.9 90.0 %copy-start.14 = (bf16[1,128,768]{2,1,0:T(8,128)(2,1)S(1)}, bf16[1,128,768]{2,1,0:T(8,128)(2,1)}, u32[]{:S(2)}) copy-start(bf16[1,128,768]{2,1,0:T(8,128)(2,1)} %param.12) | copy-start | bytes 589828
  449.5 93.4 %copy-start.18 = (bf16[128,768]{1,0:T(8,128)(2,1)}, bf16[128,768]{1,0:T(8,128)(2,1)S(1)}, u32[]{:S(2)}) copy-start(bf16[128,768]{1,0:T(8,128)(2,1)S(1)} %reshape.372) | copy-start | bytes 589828
  543.0 593.4 %reduce-scatter.43.cloned.1.call-start = ((), (), s32[]{:S(2)}) async-start(), calls=%async_computation.29 | async-start | bytes 442368
  544.7 659.3 %reduce-scatter.45.cloned.1.call-start = ((), (), s32[]{:S(2)}) async-start(), calls=%async_computation.30 | async-start | bytes 1769472
  546.6 63.8 %copy-start.17 = (bf16[1,128,768]{2,1,0:T(8,128)(2,1)S(1)}, bf16[1,128,768]{2,1,0:T(8,128)(2,1)}, u32[]{:S(2)}) copy-start(bf16[1,128,768]{2,1,0:T(8,128)(2,1)} %param.23) | copy-start | bytes 589828
  546.6 63.9 %copy-start.26 = (f32[768]{0:T(1024)S(1)}, f32[768]{0:T(1024)}, u32[]{:S(2)}) copy-start(f32[768]{0:T(1024)} %get-tuple-element.77) | copy-start | bytes 9220
  546.6 63.9 %copy-start.24 = (f32[768]{0:T(1024)S(1)}, f32[768]{0:T(1024)}, u32[]{:S(2)}) copy-start(f32[768]{0:T(1024)} %get-tuple-element.92) | copy-start | bytes 9220
  546.6 64.0 %copy-start.15 = (f32[128,1536]{1,0:T(8,128)S(1)}, f32[128,1536]{1,0:T(8,128)}, u32[]{:S(2)}) copy-start(f32[128,1536]{1,0:T(8,128)} %reduce-scatter.23.cloned.1.call-done) | copy-start | bytes 2359300
  546.6 678.9 %reduce-scatter.39.cloned.1.call-start = ((), (), s32[]{:S(2)}) async-start(), calls=%async_computation.27 | async-start | bytes 245760
  610.4 679.6 %reduce-scatter.41.cloned.1.call-start = ((), (), s32[]{:S(2)}) async-start(), calls=%async_computation.28 | async-start | bytes 442368
  611.7 701.8 %reduce-scatter.31.cloned.1.call-start = ((), (), s32[]{:S(2)}) async-start(), calls=%async_computation.23 | async-start | bytes 737280 | tf_op jit(solution)/shard_map/reduce_scatter | solution.py:66
  776.7 561.2 %reduce-scatter.35.cloned.1.call-start = ((), (), s32[]{:S(2)}) async-start(), calls=%async_computation.25 | async-start | bytes 737280 | tf_op jit(solution)/shard_map/reduce_scatter | solution.py:69
  942.8 285.7 %copy-start = (bf16[768,2304]{1,0:T(8,128)(2,1)S(1)}, bf16[768,2304]{1,0:T(8,128)(2,1)}, u32[]{:S(2)}) copy-start(bf16[768,2304]{1,0:T(8,128)(2,1)} %all-gather.12.cloned.1.call-done) | copy-start | bytes 10616836
  942.8 419.7 %reduce-scatter.37.cloned.1.call-start = ((), (), s32[]{:S(2)}) async-start(), calls=%async_computation.26 | async-start | bytes 737280
  (33 other events, 232.7 us)
Sparse Core Ops, SparseCore 0:
  45.0 31.3 all-gather.11
  78.4 42.2 all-gather.17
  123.0 40.3 all-gather.21
  165.4 59.3 all-gather.13
  226.8 16.0 all-gather.15
  244.3 37.4 all-gather.19
  283.4 37.4 all-gather.23
  418.7 118.2 reduce-scatter.22
  540.5 67.9 reduce-scatter.26
  612.0 162.5 reduce-scatter.28
  778.1 162.4 reduce-scatter.32
  944.2 128.0 reduce-scatter.24
  1075.9 60.4 reduce-scatter.42
  1140.1 63.8 reduce-scatter.44
  1206.9 18.5 reduce-scatter.38
  1228.6 61.3 reduce-scatter.40
  1292.3 21.0 reduce-scatter.30
  1315.8 22.0 reduce-scatter.34
  1340.4 22.0 reduce-scatter.36
where the time goes:
time: 1380 us; the launch traced here: 1370 us
  waiting for transfers between devices  1000 us (72%)
  blocking collectives  144 us (10%)
  matrix products  83.9 us (6%)
  local copies, waits for them, and re-layouts  80.4 us (6%)
  other arithmetic  43.5 us (3%)
  between operations  14.8 us (1%)
    unnamed x24, waiting for transfers between devices  230 us
    reduce_scatter x1, waiting for transfers between devices, over_cols(): lax.psum_scatter(shrink_grad, 'ctx', scatter_dimension=1, tiled=True)  164 us
    reduce_scatter x1, waiting for transfers between devices, over_cols(): lax.psum_scatter(expand_grad, 'ctx', scatter_dimension=1, tiled=True)  163 us
    reduce_scatter x1, waiting for transfers between devices, over_cols(): lax.psum_scatter(qkv_grad, 'ctx', scatter_dimension=1, tiled=True)  129 us
    reduce_scatter x1, waiting for transfers between devices, shards(): lax.psum_scatter(scatter_rows(linked_ids, slot_grads, tokens_here * lax.a...  87.5 us
    reduce_scatter x1, waiting for transfers between devices, over_cols(): lax.psum_scatter(out_grad, 'ctx', scatter_dimension=1, tiled=True)  61.9 us
    all_gather x1, waiting for transfers between devices, shards(): lax.all_gather(shrink_weight, 'ctx', axis=1, tiled=True)  42.5 us
    all_gather x1, blocking collectives, shards(): lax.all_gather(project_in, 'ctx', axis=1, tiled=True)  35.3 us
  transfers between devices with their start and end apart: 19, of which 18 were waited for; matrix products, arithmetic and copies ran while one was open for 7% of the time, Pallas kernels for 0%

commit v1 on v0

--- a/solution.py
+++ b/solution.py
@@ -132,7 +132,11 @@
         global_blocks[0][None, :], (blocks_here, global_blocks.shape[1])
     )
     linked_ids = jnp.concatenate([window, random_blocks[0], global_links], axis=1)
-    bounds = jnp.cumsum(document_lengths[0])[:-1]
+    lengths = document_lengths[0]
+    doc_order = jnp.arange(lengths.shape[0], dtype=jnp.int32)
+    bounds = jnp.sum(
+        jnp.where(doc_order[None, :] <= doc_order[:-1, None], lengths[None, :], 0), axis=1
+    )
     query_pos = (ctx_rank * tokens_here + jnp.arange(tokens_here, dtype=jnp.int32)).reshape(
         blocks_here, BLOCK
     )
@@ -146,15 +150,15 @@
     ).astype(jnp.bfloat16)
     queries = mixed_qkv[:, :width]
     keyvals = mixed_qkv[:, width:]
-    blank_slots = jnp.zeros((blocks_here, link_count, BLOCK, 2 * width), jnp.bfloat16)
     shard_piece = lax.all_gather(keyvals, "ctx", axis=0, tiled=True)
     block_count = shard_piece.shape[0] // BLOCK
     stacked = shard_piece.reshape(block_count, BLOCK, shard_piece.shape[1])
-    inside = (linked_ids >= 0) & (linked_ids < block_count)
-    fetched = jnp.take(
-        stacked, jnp.clip(linked_ids, 0, block_count - 1).reshape(-1), axis=0
-    ).reshape(blank_slots.shape)
-    linked = jnp.where(inside[:, :, None, None], fetched, blank_slots)
+    picks = (
+        linked_ids.reshape(-1)[:, None] == jnp.arange(block_count, dtype=jnp.int32)[None, :]
+    ).astype(jnp.bfloat16)
+    linked = jnp.einsum("lb,bkd->lkd", picks, stacked).reshape(
+        blocks_here, link_count, BLOCK, 2 * width
+    )
     query_heads = queries.reshape(blocks_here, BLOCK, head_count, HEAD_DIM)
     key_heads = linked[..., :width].reshape(blocks_here, link_count * BLOCK, head_count, HEAD_DIM)
     value_heads = linked[..., width:].reshape(blocks_here, link_count * BLOCK, head_count, HEAD_DIM)

time: 1380 us -> 1380 us (level)
  no operation moved by 1% of the time
where the time goes in v1:
time: 1380 us; the launch traced here: 1370 us
  waiting for transfers between devices  1000 us (72%)
  blocking collectives  144 us (10%)
  matrix products  88.5 us (6%)
  local copies, waits for them, and re-layouts  78.7 us (6%)
  other arithmetic  43.3 us (3%)
  between operations  14.9 us (1%)
    unnamed x24, waiting for transfers between devices  230 us
    reduce_scatter x1, waiting for transfers between devices, over_cols(): lax.psum_scatter(shrink_grad, 'ctx', scatter_dimension=1, tiled=True)  164 us
    reduce_scatter x1, waiting for transfers between devices, over_cols(): lax.psum_scatter(expand_grad, 'ctx', scatter_dimension=1, tiled=True)  163 us
    reduce_scatter x1, waiting for transfers between devices, over_cols(): lax.psum_scatter(qkv_grad, 'ctx', scatter_dimension=1, tiled=True)  129 us
    reduce_scatter x1, waiting for transfers between devices, shards(): lax.psum_scatter(scatter_rows(linked_ids, slot_grads, tokens_here * lax.a...  87 us
    reduce_scatter x1, waiting for transfers between devices, over_cols(): lax.psum_scatter(out_grad, 'ctx', scatter_dimension=1, tiled=True)  62 us
    all_gather x1, waiting for transfers between devices, shards(): lax.all_gather(shrink_weight, 'ctx', axis=1, tiled=True)  42.5 us
    all_gather x1, blocking collectives, shards(): lax.all_gather(project_in, 'ctx', axis=1, tiled=True)  35.3 us
  transfers between devices with their start and end apart: 19, of which 18 were waited for; matrix products, arithmetic and copies ran while one was open for 7% of the time, Pallas kernels for 0%

profile of v1, /device:TPU:0, one launch (start us, length us, event | category | flops | bytes accessed | tf_op | source)
XLA Modules:
  0.0 1370.7 jit_solution(4215923019688839348)
XLA Ops:
  8.2 35.3 %all_gather.44 = bf16[192,2304]{0,1:T(8,128)(2,1)S(1)} all-gather(bf16[192,288]{0,1:T(8,128)(2,1)S(1)} %copy.132), channel_id=1, replica_groups=mesh['ctx'=8,'fsdp'=4] {'ctx'}, dimensions={1}, use_global_device_ids=true | all-gather | bytes 995328 | tf_op jit(solution)/shard_map/all_gather | solution.py:110
  46.5 26.0 %all-gather.1 = bf16[8,96,6]{1,2,0:T(8,128)(2,1)S(1)} all-gather(bf16[1,96,6]{1,2,0:T(8,128)(2,1)S(1)} %bitcast.134), channel_id=1, replica_groups=mesh['ctx'=8,'fsdp'=4] {'ctx'}, dimensions={0}, use_global_device_ids=true | all-gather | bytes 10368 | tf_op jit(solution)/shard_map/all_gather | solution.py:114
  80.0 31.7 %all_gather.48 = bf16[192,768]{0,1:T(8,128)(2,1)S(1)} all-gather(bf16[192,96]{0,1:T(8,128)(2,1)S(1)} %copy.141), channel_id=1, replica_groups=mesh['ctx'=8,'fsdp'=4] {'ctx'}, dimensions={1}, use_global_device_ids=true | all-gather | bytes 331776 | tf_op jit(solution)/shard_map/all_gather | solution.py:111
  112.7 8.1 all-gather.18.cloned.1.call-done
  120.8 42.5 %all-gather.22.cloned.1.call-done = bf16[768,768]{0,1:T(8,128)(2,1)} async-done(((bf16[768,96]{0,1:T(8,128)(2,1)}), bf16[768,768]{0,1:T(8,128)(2,1)}) %all-gather.22.cloned.1.call-update) | async-done | bytes 1179664 | tf_op jit(solution)/shard_map/all_gather | solution.py:113
  163.7 18.2 %all-gather.2 = bf16[8,96,2]{1,2,0:T(2,128)(2,1)S(1)} all-gather(bf16[1,96,2]{1,2,0:T(2,128)(2,1)S(1)} %bitcast.136), channel_id=1, replica_groups=mesh['ctx'=8,'fsdp'=4] {'ctx'}, dimensions={0}, use_global_device_ids=true | all-gather | bytes 3456 | tf_op jit(solution)/shard_map/all_gather | solution.py:115
  182.4 26.4 %all-gather.3 = bf16[8,1,384]{2,1,0:T(2,128)(2,1)S(1)} all-gather(bf16[1,1,384]{2,1,0:T(2,128)(2,1)S(1)} %reshape.276), channel_id=2, replica_groups=mesh['ctx'=8,'fsdp'=4] {'ctx'}, dimensions={0}, use_global_device_ids=true | all-gather | bytes 6912 | tf_op jit(solution)/shard_map/all_gather | solution.py:116
  211.1 13.5 all-gather.14.cloned.1.call-done
  254.6 27.0 %all-gather.20.cloned.1.call-done = bf16[768,3072]{1,0:T(8,128)(2,1)} async-done(((bf16[192,3072]{1,0:T(8,128)(2,1)}), bf16[768,3072]{1,0:T(8,128)(2,1)}) %all-gather.20.cloned.1.call-update) | async-done | bytes 4718608 | tf_op jit(solution)/shard_map/all_gather | solution.py:121
  281.6 7.7 multiply_convert_fusion.1
  289.3 31.4 %all-gather.24.cloned.1.call-done = bf16[3072,768]{0,1:T(8,128)(2,1)} async-done(((bf16[768,768]{0,1:T(8,128)(2,1)}), bf16[3072,768]{0,1:T(8,128)(2,1)}) %all-gather.24.cloned.1.call-update) | async-done | bytes 4718608 | tf_op jit(solution)/shard_map/all_gather | solution.py:122
  342.1 15.3 %fusion.16 = f32[2,512,12,64]{1,3,2,0:T(8,128)} fusion(bf16[2,64,12,64]{1,3,2,0:T(8,128)(2,1)S(1)} %copy-done.22, f32[2,12,64,512]{3,2,1,0:T(8,128)} %fusion.93, f32[2,12,64,512]{3,2,1,0:T(8,128)} %get-tuple-element.100, f32[2,12,64]{2,1,0:T(8,128)S(1)} %get-tuple-element.99), kind=kOutput, calls=%fused_computation.20 | convolution fusion | flops 106170368 | bytes 9639936 | tf_op jit(solution)/shard_map/bhqk,bqhd->bkhd/dot_general | solution.py:246
  366.0 6.7 concatenate.27
  377.7 12.3 pad_maximum_fusion
  390.0 9.8 copy.151
  403.2 15.3 %scatter_fusion = f32[16,64,1536]{2,1,0:T(8,128)} fusion(f32[16,64,1536]{2,1,0:T(8,128)} %broadcast_in_dim.86, s32[16]{0:T(128)S(1)} %copy-done.34, f32[16,64,1536]{2,1,0:T(8,128)} %copy.151), kind=kCustom, calls=%fused_computation | custom fusion | flops 1572864 | bytes 18874432 | tf_op jit(solution)/shard_map/scatter-add | solution.py:80
  422.6 5.2 fusion.49
  429.0 5.1 fusion.61
  435.6 13.3 fusion.86
  449.5 87.0 %reduce-scatter.23.cloned.1.call-done = f32[128,1536]{1,0:T(8,128)} async-done(((f32[1024,1536]{1,0:T(8,128)}), f32[128,1536]{1,0:T(8,128)}) %reduce-scatter.23.cloned.1.call-update) | async-done | bytes 786448 | tf_op jit(solution)/shard_map/reduce_scatter | solution.py:256
  546.2 62.0 %reduce-scatter.27.cloned.1.call-done = f32[768,96]{0,1:T(8,128)} async-done(((f32[768,768]{0,1:T(8,128)}), f32[768,96]{0,1:T(8,128)}) %reduce-scatter.27.cloned.1.call-update) | async-done | bytes 294928 | tf_op jit(solution)/shard_map/reduce_scatter | solution.py:49
  611.3 162.6 %reduce-scatter.29.cloned.1.call-done = f32[768,384]{1,0:T(8,128)} async-done(((f32[768,3072]{1,0:T(8,128)}), f32[768,384]{1,0:T(8,128)}) %reduce-scatter.29.cloned.1.call-update) | async-done | bytes 1179664 | tf_op jit(solution)/shard_map/reduce_scatter | solution.py:50
  776.1 163.9 %reduce-scatter.33.cloned.1.call-done = f32[3072,96]{0,1:T(8,128)} async-done(((f32[3072,768]{0,1:T(8,128)}), f32[3072,96]{0,1:T(8,128)}) %reduce-scatter.33.cloned.1.call-update) | async-done | bytes 1179664 | tf_op jit(solution)/shard_map/reduce_scatter | solution.py:51
  942.3 129.4 %reduce-scatter.25.cloned.1.call-done = f32[768,288]{0,1:T(8,128)} async-done(((f32[768,2304]{0,1:T(8,128)}), f32[768,288]{0,1:T(8,128)}) %reduce-scatter.25.cloned.1.call-update) | async-done | bytes 884752 | tf_op jit(solution)/shard_map/reduce_scatter | solution.py:48
  1075.8 60.0 %reduce-scatter.43.cloned.1.call-done = f32[96,2]{1,0:T(8,128)} async-done(((f32[768,2]{1,0:T(8,128)}), f32[96,2]{1,0:T(8,128)}) %reduce-scatter.43.cloned.1.call-update) | async-done | bytes 784
  1136.7 66.7 %reduce-scatter.45.cloned.1.call-done = f32[384,1]{1,0:T(8,128)} async-done(((f32[3072,1]{1,0:T(8,128)}), f32[384,1]{1,0:T(8,128)}) %reduce-scatter.45.cloned.1.call-update) | async-done | bytes 1552
  1204.5 20.5 %reduce-scatter.39.cloned.1.call-done = bf16[192,96]{1,0:T(8,128)(2,1)} async-done(((bf16[768,96]{1,0:T(8,128)(2,1)}), bf16[192,96]{1,0:T(8,128)(2,1)}) %reduce-scatter.39.cloned.1.call-update) | async-done | bytes 36880
  1231.2 58.3 %reduce-scatter.41.cloned.1.call-done = f32[96,6]{1,0:T(8,128)} async-done(((f32[768,6]{1,0:T(8,128)}), f32[96,6]{1,0:T(8,128)}) %reduce-scatter.41.cloned.1.call-update) | async-done | bytes 2320
  1290.3 6.3 all-reduce
  1296.7 16.3 %reduce-scatter.31.cloned.1.call-done = bf16[192,384]{1,0:T(8,128)(2,1)} async-done(((bf16[768,384]{1,0:T(8,128)(2,1)}), bf16[192,384]{1,0:T(8,128)(2,1)}) %reduce-scatter.31.cloned.1.call-update) | async-done | bytes 147472 | tf_op jit(solution)/shard_map/reduce_scatter | solution.py:66
  1314.6 22.8 %reduce-scatter.35.cloned.1.call-done = bf16[768,96]{0,1:T(8,128)(2,1)} async-done(((bf16[3072,96]{0,1:T(8,128)(2,1)}), bf16[768,96]{0,1:T(8,128)(2,1)}) %reduce-scatter.35.cloned.1.call-update) | async-done | bytes 147472 | tf_op jit(solution)/shard_map/reduce_scatter | solution.py:69
  1339.1 23.0 %reduce-scatter.37.cloned.1.call-done = bf16[192,288]{1,0:T(8,128)(2,1)} async-done(((bf16[768,288]{1,0:T(8,128)(2,1)}), bf16[192,288]{1,0:T(8,128)(2,1)}) %reduce-scatter.37.cloned.1.call-update) | async-done | bytes 110608
  (240 shorter events, 126.3 us)
Async XLA Ops:
  7.2 69.2 %all-gather.12.cloned.1.call-start = ((), (), s32[]{:S(2)}) async-start(), calls=%async_computation.12 | async-start | bytes 4423680 | tf_op jit(solution)/shard_map/all_gather | solution.py:119
  44.9 75.9 %all-gather.18.cloned.1.call-start = ((), (), s32[]{:S(2)}) async-start(), calls=%async_computation.15 | async-start | bytes 1327104 | tf_op jit(solution)/shard_map/all_gather | solution.py:112
  45.7 117.7 %all-gather.22.cloned.1.call-start = ((), (), s32[]{:S(2)}) async-start(), calls=%async_computation.17 | async-start | bytes 1327104 | tf_op jit(solution)/shard_map/all_gather | solution.py:113
  46.4 178.2 %all-gather.14.cloned.1.call-start = ((), (), s32[]{:S(2)}) async-start(), calls=%async_computation.13 | async-start | bytes 3538944 | tf_op jit(solution)/shard_map/all_gather | solution.py:153
  79.9 172.5 %all-gather.16.cloned.1.call-start = ((), (), s32[]{:S(2)}) async-start(), calls=%async_computation.14 | async-start | bytes 1474560 | tf_op jit(solution)/shard_map/all_gather | solution.py:120
  111.7 51.8 %copy-start.36 = (s32[1,2]{1,0:T(1,128)S(1)}, s32[1,2]{1,0:T(1,128)}, u32[]{:S(2)}) copy-start(s32[1,2]{1,0:T(1,128)} %param.21) | copy-start | bytes 28
  111.7 51.8 %copy-start.33 = (s32[1,2,3]{2,1,0:T(2,128)S(1)}, s32[1,2,3]{2,1,0:T(2,128)}, u32[]{:S(2)}) copy-start(s32[1,2,3]{2,1,0:T(2,128)} %param.20) | copy-start | bytes 76
  111.7 52.0 %copy-start.35 = (bf16[2,96]{1,0:T(2,128)(2,1)S(1)}, bf16[2,96]{1,0:T(2,128)(2,1)}, u32[]{:S(2)}) copy-start(bf16[2,96]{1,0:T(2,128)(2,1)} %param.18) | copy-start | bytes 1156
  111.7 70.3 %copy-start.37 = (s32[1,8]{1,0:T(1,128)S(1)}, s32[1,8]{1,0:T(1,128)}, u32[]{:S(2)}) copy-start(s32[1,8]{1,0:T(1,128)} %param.22) | copy-start | bytes 100
  112.6 169.0 %all-gather.20.cloned.1.call-start = ((), (), s32[]{:S(2)}) async-start(), calls=%async_computation.16 | async-start | bytes 5898240 | tf_op jit(solution)/shard_map/all_gather | solution.py:121
  120.8 199.9 %all-gather.24.cloned.1.call-start = ((), (), s32[]{:S(2)}) async-start(), calls=%async_computation.18 | async-start | bytes 5898240 | tf_op jit(solution)/shard_map/all_gather | solution.py:122
  163.3 373.1 %reduce-scatter.23.cloned.1.call-start = ((), (), s32[]{:S(2)}) async-start(), calls=%async_computation.19 | async-start | bytes 7077888 | tf_op jit(solution)/shard_map/reduce_scatter | solution.py:256
  248.9 93.2 %copy-start.39 = (f32[2,12,64]{2,1,0:T(8,128)}, f32[2,12,64]{2,1,0:T(8,128)S(1)}, u32[]{:S(2)}) copy-start(f32[2,12,64]{2,1,0:T(8,128)S(1)} %get-tuple-element.99) | copy-start | bytes 18436
  254.6 79.7 %copy-start.28 = (f32[128]{0:T(128)}, f32[128]{0:T(128)S(1)}, u32[]{:S(2)}) copy-start(f32[128]{0:T(128)S(1)} %add_rsqrt_fusion.1) | copy-start | bytes 1540
  418.5 189.6 %reduce-scatter.27.cloned.1.call-start = ((), (), s32[]{:S(2)}) async-start(), calls=%async_computation.21 | async-start | bytes 2654208 | tf_op jit(solution)/shard_map/reduce_scatter | solution.py:49
  421.5 352.4 %reduce-scatter.29.cloned.1.call-start = ((), (), s32[]{:S(2)}) async-start(), calls=%async_computation.22 | async-start | bytes 10616832 | tf_op jit(solution)/shard_map/reduce_scatter | solution.py:50
  427.8 512.3 %reduce-scatter.33.cloned.1.call-start = ((), (), s32[]{:S(2)}) async-start(), calls=%async_computation.24 | async-start | bytes 10616832 | tf_op jit(solution)/shard_map/reduce_scatter | solution.py:51
  434.1 637.6 %reduce-scatter.25.cloned.1.call-start = ((), (), s32[]{:S(2)}) async-start(), calls=%async_computation.20 | async-start | bytes 7962624 | tf_op jit(solution)/shard_map/reduce_scatter | solution.py:48
  448.9 89.5 %copy-start.14 = (bf16[1,128,768]{2,1,0:T(8,128)(2,1)S(1)}, bf16[1,128,768]{2,1,0:T(8,128)(2,1)}, u32[]{:S(2)}) copy-start(bf16[1,128,768]{2,1,0:T(8,128)(2,1)} %param.12) | copy-start | bytes 589828
  449.4 93.0 %copy-start.18 = (bf16[128,768]{1,0:T(8,128)(2,1)}, bf16[128,768]{1,0:T(8,128)(2,1)S(1)}, u32[]{:S(2)}) copy-start(bf16[128,768]{1,0:T(8,128)(2,1)S(1)} %reshape.283) | copy-start | bytes 589828
  542.4 593.4 %reduce-scatter.43.cloned.1.call-start = ((), (), s32[]{:S(2)}) async-start(), calls=%async_computation.29 | async-start | bytes 442368
  544.1 659.3 %reduce-scatter.45.cloned.1.call-start = ((), (), s32[]{:S(2)}) async-start(), calls=%async_computation.30 | async-start | bytes 1769472
  546.1 63.9 %copy-start.17 = (bf16[1,128,768]{2,1,0:T(8,128)(2,1)S(1)}, bf16[1,128,768]{2,1,0:T(8,128)(2,1)}, u32[]{:S(2)}) copy-start(bf16[1,128,768]{2,1,0:T(8,128)(2,1)} %param.23) | copy-start | bytes 589828
  546.1 64.0 %copy-start.26 = (f32[768]{0:T(1024)S(1)}, f32[768]{0:T(1024)}, u32[]{:S(2)}) copy-start(f32[768]{0:T(1024)} %get-tuple-element.77) | copy-start | bytes 9220
  546.1 64.0 %copy-start.24 = (f32[768]{0:T(1024)S(1)}, f32[768]{0:T(1024)}, u32[]{:S(2)}) copy-start(f32[768]{0:T(1024)} %get-tuple-element.92) | copy-start | bytes 9220
  546.1 64.1 %copy-start.15 = (f32[128,1536]{1,0:T(8,128)S(1)}, f32[128,1536]{1,0:T(8,128)}, u32[]{:S(2)}) copy-start(f32[128,1536]{1,0:T(8,128)} %reduce-scatter.23.cloned.1.call-done) | copy-start | bytes 2359300
  546.1 678.8 %reduce-scatter.39.cloned.1.call-start = ((), (), s32[]{:S(2)}) async-start(), calls=%async_computation.27 | async-start | bytes 245760
  609.9 679.6 %reduce-scatter.41.cloned.1.call-start = ((), (), s32[]{:S(2)}) async-start(), calls=%async_computation.28 | async-start | bytes 442368
  611.2 701.7 %reduce-scatter.31.cloned.1.call-start = ((), (), s32[]{:S(2)}) async-start(), calls=%async_computation.23 | async-start | bytes 737280 | tf_op jit(solution)/shard_map/reduce_scatter | solution.py:66
  776.1 561.3 %reduce-scatter.35.cloned.1.call-start = ((), (), s32[]{:S(2)}) async-start(), calls=%async_computation.25 | async-start | bytes 737280 | tf_op jit(solution)/shard_map/reduce_scatter | solution.py:69
  942.2 285.8 %copy-start = (bf16[768,2304]{1,0:T(8,128)(2,1)S(1)}, bf16[768,2304]{1,0:T(8,128)(2,1)}, u32[]{:S(2)}) copy-start(bf16[768,2304]{1,0:T(8,128)(2,1)} %all-gather.12.cloned.1.call-done) | copy-start | bytes 10616836
  942.3 419.8 %reduce-scatter.37.cloned.1.call-start = ((), (), s32[]{:S(2)}) async-start(), calls=%async_computation.26 | async-start | bytes 737280
  (33 other events, 230.2 us)
Sparse Core Ops, SparseCore 0:
  45.0 31.3 all-gather.11
  78.4 42.2 all-gather.17
  123.0 40.3 all-gather.21
  165.4 59.2 all-gather.13
  226.6 16.0 all-gather.15
  244.1 37.4 all-gather.19
  283.2 37.4 all-gather.23
  418.6 117.7 reduce-scatter.22
  539.9 68.1 reduce-scatter.26
  611.5 162.3 reduce-scatter.28
  777.5 162.5 reduce-scatter.32
  943.6 128.0 reduce-scatter.24
  1075.3 60.4 reduce-scatter.42
  1139.5 63.8 reduce-scatter.44
  1206.3 18.6 reduce-scatter.38
  1228.1 61.3 reduce-scatter.40
  1291.8 21.1 reduce-scatter.30
  1315.3 22.0 reduce-scatter.34
  1339.9 22.0 reduce-scatter.36

commit v2 on v1

--- a/solution.py
+++ b/solution.py
@@ -1,6 +1,8 @@
 import jax
 import jax.numpy as jnp
 from jax import lax
+from jax.experimental import pallas as pl
+from jax.experimental.pallas import tpu as pltpu
 from jax.sharding import PartitionSpec as P
 
 HEAD_DIM = 64
@@ -303,9 +305,756 @@
     )
 
 
+MESH = pl.DeviceIdType.MESH
+BF = jnp.bfloat16
+F32 = jnp.float32
+SENDS = 128
+RECVS = 128
+NEG = -1e30
+
+
+def dot_nn(a, b):
+    return jnp.dot(a, b, preferred_element_type=F32)
+
+
+def dot_nt(a, b):
+    return lax.dot_general(a, b, (((1,), (1,)), ((), ())), preferred_element_type=F32)
+
+
+def dot_tn(a, b):
+    return lax.dot_general(a, b, (((0,), (0,)), ((), ())), preferred_element_type=F32)
+
+
+def row_sum(values):
+    return jnp.sum(values, axis=0, keepdims=True)
+
+
+def layer_kernel(
+    rand_ref, glob_ref, doc_ref, hid, cot, win, wout, wexp, wshr, bia, gai, ebi,
+    o_out, o_gh, o_win, o_wout, o_wexp, o_wshr, o_gb, o_gg, o_ge,
+    win3, xg, eo, ms, mg, ps, par, win_p, wout_p, wexp_f, wshr_p, w_in, w_out, w_shr, prm,
+    q_s, kv, kh, vh, bias_s, p_s, a_f, a_b, a_all, hg, h1_s, n1_s, r1_s, dge, g_s, ysum, yb,
+    rs1, d2_s, dg, du_s, dh_b, rs2, beg, d1_s, d1g, dab, da, ds_s, dkv, dkb, dkr, dz, dx_b, rs3,
+    gs, rs_c, t_shr, rs_y, fsb, fs, ge, re_c, t_exp, re_y, te_f, te_b, re_z,
+    go, ro_c, tob, ro_y, tob2, fo, gi, ri_c, tib, ri_y, ti2, fi,
+    vg, vr, vs1, vc, vs2, vy, qb_s, vb_s, ob, ohr, ghb, ghr,
+    ssem, rsem,
+):
+    ctx = lax.axis_index("ctx")
+    seq = lax.axis_index("fsdp")
+    z, x = ctx // 2, ctx % 2
+    y, c = seq // 2, seq % 2
+    zh, zl = z // 2, z % 2
+    r = 2 * zl + x
+    f = seq
+
+    def dev(px, py, pz, pc):
+        return (2 * pz + px, 2 * py + pc)
+
+    def flip(v, on):
+        return v + on - 2 * v * on
+
+    def peer(j):
+        return dev(flip(x, j % 2), y, 2 * zh + flip(zl, j // 2), c)
+
+    def peer_rank(j):
+        return 2 * flip(zl, j // 2) + flip(x, j % 2)
+
+    core_mate = dev(x, y, z, 1 - c)
+    y_mate = dev(x, 1 - y, z, c)
+    z_mate = dev(x, y, 2 * (1 - zh) + zl, c)
+    home = dev(x, y, 2 * c + zl, zh)
+
+    pending = []
+    counts = {"s": 0, "r": 0}
+
+    def recvs(n):
+        first = counts["r"]
+        counts["r"] = first + n
+        assert counts["r"] <= RECVS
+        return first
+
+    def sends(n):
+        first = counts["s"]
+        counts["s"] = first + n
+        assert counts["s"] <= SENDS
+        return first
+
+    def copy_to(src, dst, si, ri, to):
+        return pltpu.make_async_remote_copy(
+            src_ref=src, dst_ref=dst, send_sem=ssem.at[si], recv_sem=rsem.at[ri],
+            device_id=to, device_id_type=MESH,
+        )
+
+    def send(src, dst, ri, to):
+        cp = copy_to(src, dst, sends(1), ri, to)
+        cp.start()
+        pending.append(cp.wait_send)
+
+    def send_or_keep(src, dst, ri, to):
+        si = sends(1)
+        away = jnp.logical_or(to[0] != ctx, to[1] != seq)
+
+        @pl.when(away)
+        def _():
+            copy_to(src, dst, si, ri, to).start()
+
+        @pl.when(jnp.logical_not(away))
+        def _():
+            pltpu.make_async_copy(src, dst, rsem.at[ri]).start()
+
+        def finish():
+            @pl.when(away)
+            def _():
+                copy_to(src, dst, si, ri, to).wait_send()
+
+        pending.append(finish)
+
+    def arrived(dst, ri):
+        pltpu.make_async_copy(dst, dst, rsem.at[ri]).wait()
+
+    barrier = pltpu.get_barrier_semaphore()
+    place = 2 * ctx + c
+    for d in range(1, 16):
+        other = (place + d) % 16
+        pl.semaphore_signal(
+            barrier, inc=1, device_id=(other // 2, 2 * y + other % 2), device_id_type=MESH
+        )
+    pl.semaphore_signal(barrier, inc=1, device_id=y_mate, device_id_type=MESH)
+
+    lane = lax.broadcasted_iota(jnp.int32, (1, 128), 1)
+    for i in range(2):
+        block = 2 * ctx + i
+        links = [jnp.maximum(block - 1, 0), block, jnp.minimum(block + 1, 15)]
+        links += [rand_ref[i, k] for k in range(3)] + [glob_ref[0, k] for k in range(2)]
+        count = jnp.zeros((1, 128), F32)
+        for link in links:
+            count += jnp.where(lane == link, 1.0, 0.0)
+        ms[i : i + 1, :] = count
+    edge = doc_ref[0, 0]
+    edges = jnp.zeros((1, 128), F32)
+    for k in range(7):
+        edges += jnp.where(lane == k, edge.astype(F32), 0.0)
+        edge = edge + doc_ref[0, k + 1]
+    ms[2:3, :] = edges
+    ms[3:8, :] = jnp.zeros((5, 128), F32)
+    for j in range(3):
+        win3[j] = win[:, 96 * j : 96 * j + 96]
+    ps[...] = jnp.zeros((16, 128), F32)
+    ps[0:6, 0:96] = bia[...].astype(F32)
+    ps[6:8, 0:96] = gai[...].astype(F32)
+    ps[8:11, :] = ebi[...].astype(F32)
+
+    pl.semaphore_wait(barrier, 16)
+
+    k_x, k_m, k_e = recvs(4), recvs(4), recvs(1)
+    send_or_keep(hid, xg.at[r], k_x, home)
+    send_or_keep(ms, mg.at[r], k_m, home)
+    k_par = recvs(8)
+    k_win = recvs(6)
+    for j in range(3):
+        unit = 3 * ctx + j
+        rank = (unit % 8) // 2
+        slot = 2 * (unit // 8) + unit % 2
+        for half in range(2):
+            send_or_keep(
+                win3.at[j], win_p.at[f, slot], k_win + slot, dev(rank % 2, y, 2 * half + rank // 2, c)
+            )
+    for d in range(1, 8):
+        other = (ctx + d) % 8
+        send(ps, par.at[ctx], k_par + d, (other, seq))
+    par[ctx] = ps[...]
+
+    arrived(xg.at[r], k_x)
+    arrived(mg.at[r], k_m)
+    for j in range(1, 4):
+        send(mg.at[r], mg.at[r], k_m + j, peer(j))
+        send(xg.at[r], xg.at[r], k_x + j, peer(j))
+    send_or_keep(cot, eo, k_e, home)
+
+    k_wout = recvs(8)
+    for d in range(8):
+        other = (ctx + d) % 8
+        if d == 0:
+            pltpu.make_async_copy(wout, wout_p.at[f, ctx], rsem.at[k_wout]).start()
+        else:
+            send(wout, wout_p.at[f, ctx], k_wout + d, (other, seq))
+    k_wexp = recvs(2)
+    mine_exp = wexp_f.at[f, :, pl.ds(pl.multiple_of(384 * zh, 128), 384)]
+    pltpu.make_async_copy(wexp, mine_exp, rsem.at[k_wexp]).start()
+    send(wexp, mine_exp, k_wexp + 1, z_mate)
+    k_wshr = recvs(4)
+    for sub in range(2):
+        for half in range(2):
+            send_or_keep(
+                wshr.at[sub], wshr_p.at[y, x, 2 * zh + zl], k_wshr + 2 * zh + zl,
+                dev(sub, y, 2 * half + c, x),
+            )
+
+    k_win_y, k_win_c = recvs(1), recvs(2)
+    for slot in range(6):
+        arrived(win_p.at[f, slot], k_win + slot)
+    send(win_p.at[f], win_p.at[f], k_win_y, y_mate)
+    send(win_p.at[f], win_p.at[f], k_win_c, core_mate)
+    f_y = 2 * (1 - y) + c
+    arrived(win_p.at[f_y], k_win_y)
+    send(win_p.at[f_y], win_p.at[f_y], k_win_c + 1, core_mate)
+
+    for j in range(1, 4):
+        arrived(mg.at[peer_rank(j)], k_m + j)
+    counted = jnp.concatenate([mg[k, 0:2, :] for k in range(4)], axis=0)
+    spread = (
+        lax.broadcasted_iota(jnp.int32, (128, 1024), 1) // 64
+        == lax.broadcasted_iota(jnp.int32, (128, 1024), 0)
+    ).astype(BF)
+    counted = dot_nn(counted.astype(BF), spread)
+    logs = jnp.where(counted > 0.5, jnp.log(jnp.maximum(counted, 1.0)), NEG)
+    key_pos = lax.broadcasted_iota(jnp.int32, (1, 1024), 1).astype(F32)
+    row_pos = (lax.broadcasted_iota(jnp.int32, (512, 1), 0) + 512 * c).astype(F32)
+    key_seg = jnp.zeros((1, 1024), F32)
+    row_seg = jnp.zeros((512, 1), F32)
+    for k in range(7):
+        at = mg[0, 2:3, k : k + 1]
+        key_seg += jnp.where(key_pos >= at, 1.0, 0.0)
+        row_seg += jnp.where(row_pos >= at, 1.0, 0.0)
+    for i in range(8):
+        bias_s[i // 2, 64 * (i % 2) : 64 * (i % 2) + 64, :] = jnp.where(
+            row_seg[64 * i : 64 * i + 64] == key_seg, logs[i : i + 1, :], NEG
+        )
+
+    for d in range(1, 8):
+        arrived(par.at[(ctx + 8 - d) % 8], k_par + d)
+    prm[...] = jnp.concatenate([par[b, 0:8, 0:96] for b in range(8)], axis=1)
+    be = jnp.concatenate(
+        [par[r, 8 + i : 9 + i, :] for i in range(3)] + [par[4 + r, 8 + i : 9 + i, :] for i in range(3)],
+        axis=1,
+    )
+    zrow = jnp.zeros((1, 192), F32)
+    z_bias = jnp.concatenate(
+        [par[2 * r, 0:1, 0:96], par[2 * r + 1, 0:1, 0:96], zrow, par[2 * r, 1:2, 0:96], par[2 * r + 1, 1:2, 0:96]],
+        axis=1,
+    )
+
+
+    arrived(win_p.at[2 * y + 1 - c], k_win_c)
+    arrived(win_p.at[2 * (1 - y) + 1 - c], k_win_c + 1)
+    for k in range(4):
+        w_in[192 * k : 192 * k + 192, :] = jnp.concatenate([win_p[k, i] for i in range(6)], axis=1)
+
+    def project(k):
+        mixed = dot_nn(xg[k], w_in[...]) + z_bias
+        q_s[k] = (mixed[:, 0:192].astype(BF).astype(F32) * 0.125).astype(BF)
+        kv[c, pl.ds(pl.multiple_of(128 * k, 128), 128), :] = mixed[:, 192:576].astype(BF)
+
+    project(r)
+
+    def project_step(j, carry):
+        rank = peer_rank(j)
+        arrived(xg.at[rank], k_x + j)
+        project(rank)
+        return carry
+
+    lax.fori_loop(1, 4, project_step, 0)
+    k_kv = recvs(1)
+    send(kv.at[c], kv.at[c], k_kv, core_mate)
+
+    k_wout_y, k_wout_c = recvs(1), recvs(2)
+    k_wexp_y, k_wexp_c = recvs(1), recvs(2)
+    k_wshr_y, k_wshr_c = recvs(1), recvs(2)
+    for d in range(8):
+        arrived(wout_p.at[f, (ctx + 8 - d) % 8], k_wout + d)
+    send(wout_p.at[f], wout_p.at[f], k_wout_y, y_mate)
+    send(wout_p.at[f], wout_p.at[f], k_wout_c, core_mate)
+
+    arrived(kv.at[1 - c], k_kv)
+    for h in range(3):
+        for half in range(2):
+            kh[h, 512 * half : 512 * half + 512, :] = kv[half, :, 64 * h : 64 * h + 64]
+            vh[h, 512 * half : 512 * half + 512, :] = kv[half, :, 192 + 64 * h : 256 + 64 * h]
+
+    def attend(k, carry):
+        outs = []
+        for h in range(3):
+            scores = dot_nt(q_s[k, :, 64 * h : 64 * h + 64], kh[h]) + bias_s[k]
+            top = jnp.max(scores, axis=1, keepdims=True)
+            exps = jnp.exp(scores - top)
+            total = jnp.sum(exps, axis=1, keepdims=True)
+            weights = (exps * (1.0 / total)).astype(BF)
+            p_s[h, k] = weights
+            outs.append(dot_nn(weights, vh[h]))
+        both = jnp.concatenate(outs, axis=1)
+        a_f[k] = both
+        a_b[k] = both.astype(BF)
+        return carry
+
+    lax.fori_loop(0, 2, attend, 0)
+    for half in range(2):
+        at = pl.ds(pl.multiple_of(384 * half, 128), 384)
+        piece = wexp_f.at[f, :, at]
+        own = half == zh
+
+        @pl.when(own)
+        def _():
+            arrived(piece, k_wexp)
+
+        @pl.when(jnp.logical_not(own))
+        def _():
+            arrived(piece, k_wexp + 1)
+
+    send(wexp_f.at[f], wexp_f.at[f], k_wexp_y, y_mate)
+    send(wexp_f.at[f], wexp_f.at[f], k_wexp_c, core_mate)
+    for k in range(4):
+        arrived(wshr_p.at[y, c, k], k_wshr + k)
+    send(wshr_p.at[y, c], wshr_p.at[y, c], k_wshr_y, y_mate)
+    send(wshr_p.at[y, c], wshr_p.at[y, c], k_wshr_c, core_mate)
+    arrived(wout_p.at[f_y], k_wout_y)
+    send(wout_p.at[f_y], wout_p.at[f_y], k_wout_c + 1, core_mate)
+    lax.fori_loop(2, 4, attend, 0)
+
+    k_a = recvs(4)
+    for j in range(1, 4):
+        send(a_b.at[peer_rank(j)], a_all.at[r], k_a + j, peer(j))
+    a_all[r] = a_b[r]
+
+    arrived(wexp_f.at[f_y], k_wexp_y)
+    send(wexp_f.at[f_y], wexp_f.at[f_y], k_wexp_c + 1, core_mate)
+    arrived(wshr_p.at[1 - y, c], k_wshr_y)
+    send(wshr_p.at[1 - y, c], wshr_p.at[1 - y, c], k_wshr_c + 1, core_mate)
+    arrived(wout_p.at[2 * y + 1 - c], k_wout_c)
+    arrived(wout_p.at[2 * (1 - y) + 1 - c], k_wout_c + 1)
+    for k in range(4):
+        w_out[192 * k : 192 * k + 192, :] = jnp.concatenate([wout_p[k, b] for b in range(8)], axis=1)
+
+    for j in range(1, 4):
+        arrived(a_all.at[peer_rank(j)], k_a + j)
+    first = xg[r].astype(F32) + prm[2:3, :]
+    for k in range(4):
+        first += dot_nn(a_all[k], w_out[192 * k : 192 * k + 192, :])
+    centre = first - jnp.mean(first, axis=1, keepdims=True)
+    inverse = lax.rsqrt(jnp.mean(centre * centre, axis=1, keepdims=True) + 1e-05)
+    normed = centre * inverse
+    hidden_one = normed * prm[6:7, :] + prm[3:4, :]
+    n1_s[...] = normed
+    r1_s[...] = inverse
+    h1_s[...] = hidden_one
+    hg[r] = hidden_one.astype(BF)
+    k_h = recvs(4)
+    for j in range(1, 4):
+        send(hg.at[r], hg.at[r], k_h + j, peer(j))
+
+    arrived(wexp_f.at[2 * y + 1 - c], k_wexp_c)
+    arrived(wexp_f.at[2 * (1 - y) + 1 - c], k_wexp_c + 1)
+    arrived(wshr_p.at[y, 1 - c], k_wshr_c)
+    arrived(wshr_p.at[1 - y, 1 - c], k_wshr_c + 1)
+    for half in range(2):
+        w_shr[384 * half : 384 * half + 384, :] = jnp.concatenate(
+            [wshr_p[half, b % 2, b // 2] for b in range(8)], axis=1
+        )
+
+    def expand(k):
+        inner = dot_nn(hg[k], wexp_f[...].reshape(768, 768)) + be
+        below = 0.5 * (1.0 + lax.erf(inner * 0.7071067811865476))
+        dge[k] = below + inner * jnp.exp(-0.5 * inner * inner) * 0.3989422804014327
+        active = (inner * below).astype(BF)
+        g_s[k] = active
+        return dot_nn(active, w_shr[...])
+
+    ysum[...] = expand(r)
+    k_r1, s_r1 = recvs(4), sends(4)
+
+    def expand_step(j, carry):
+        rank = peer_rank(j)
+        arrived(hg.at[rank], k_h + j)
+        yb[j] = expand(rank).astype(BF)
+        copy_to(yb.at[j], rs1.at[j], s_r1 + j, k_r1 + j, peer(j)).start()
+        return carry
+
+    lax.fori_loop(1, 4, expand_step, 0)
+    for j in range(1, 4):
+        pending.append(copy_to(yb.at[j], rs1.at[j], s_r1 + j, k_r1 + j, peer(j)).wait_send)
+
+    arrived(eo, k_e)
+    upstream = eo[...].astype(F32)
+    second = h1_s[...] + prm[4:5, :] + ysum[...]
+    for j in range(1, 4):
+        arrived(rs1.at[j], k_r1 + j)
+        second += rs1[j].astype(F32)
+    centre = second - jnp.mean(second, axis=1, keepdims=True)
+    inverse = lax.rsqrt(jnp.mean(centre * centre, axis=1, keepdims=True) + 1e-05)
+    normed = centre * inverse
+    scaled = upstream * prm[7:8, :]
+    grad_two = inverse * (
+        scaled
+        - jnp.mean(scaled, axis=1, keepdims=True)
+        - normed * jnp.mean(scaled * normed, axis=1, keepdims=True)
+    )
+    d2_s[...] = grad_two
+    dg[r] = grad_two.astype(BF)
+    k_d = recvs(4)
+    for j in range(1, 4):
+        send(dg.at[r], dg.at[r], k_d + j, peer(j))
+    ob[...] = (normed * prm[7:8, :] + prm[5:6, :]).astype(BF)
+    k_o = recvs(1)
+    send_or_keep(ob, ohr, k_o, home)
+    row_gain_two = row_sum(upstream * normed)
+    row_shift_two = row_sum(upstream)
+    row_back = row_sum(grad_two)
+
+    def contract(k):
+        inner = dge[k] * dot_nt(dg[k], w_shr[...])
+        low = inner.astype(BF)
+        du_s[k] = low
+        beg[k] = row_sum(inner)
+        return dot_nt(low, wexp_f[...].reshape(768, 768))
+
+    ysum[...] = contract(r)
+    k_r2, s_r2 = recvs(4), sends(4)
+
+    def contract_step(j, carry):
+        rank = peer_rank(j)
+        arrived(dg.at[rank], k_d + j)
+        dh_b[j] = contract(rank).astype(BF)
+        copy_to(dh_b.at[j], rs2.at[j], s_r2 + j, k_r2 + j, peer(j)).start()
+        return carry
+
+    lax.fori_loop(1, 4, contract_step, 0)
+    for j in range(1, 4):
+        pending.append(copy_to(dh_b.at[j], rs2.at[j], s_r2 + j, k_r2 + j, peer(j)).wait_send)
+
+    def shrink_grad(half):
+        def step(i, carry):
+            at = pl.multiple_of(384 * half + 128 * i, 128)
+            rows = g_s[:, :, pl.ds(at, 128)].reshape(512, 128)
+            part = dot_tn(rows, dg[...].reshape(512, 768))
+            for b in range(8):
+                gs[half, b % 2, b // 2, pl.ds(pl.multiple_of(128 * i, 128), 128), :] = part[
+                    :, 96 * b : 96 * b + 96
+                ].astype(BF)
+            return carry
+
+        lax.fori_loop(0, 3, step, 0)
+
+    shrink_grad(0)
+    shrink_grad(1)
+    k_gs = recvs(2)
+    for half in range(2):
+        send(gs.at[half, 1 - c], rs_c.at[half], k_gs + half, core_mate)
+
+    def expand_grad(i, carry):
+        at = pl.ds(pl.multiple_of(128 * i, 128), 128)
+        rows = hg[:, :, at].reshape(512, 128)
+        ge[at, :] = dot_tn(rows, du_s[...].reshape(512, 768)).astype(BF)
+        return carry
+
+    lax.fori_loop(0, 6, expand_grad, 0)
+    k_ge = recvs(2)
+    for half in range(2):
+        at = pl.ds(pl.multiple_of(192 * (2 * half + 1 - c), 64), 192)
+        send(ge.at[at, :], re_c.at[half], k_ge + half, core_mate)
+
+    grad_hidden = d2_s[...] + ysum[...]
+    for j in range(1, 4):
+        arrived(rs2.at[j], k_r2 + j)
+        grad_hidden += rs2[j].astype(F32)
+    normed = n1_s[...]
+    scaled = grad_hidden * prm[6:7, :]
+    grad_one = r1_s[...] * (
+        scaled
+        - jnp.mean(scaled, axis=1, keepdims=True)
+        - normed * jnp.mean(scaled * normed, axis=1, keepdims=True)
+    )
+    d1_s[...] = grad_one
+    low_one = grad_one.astype(BF)
+    d1g[r] = low_one
+    for k in range(4):
+        dab[k] = dot_nt(low_one, w_out[192 * k : 192 * k + 192, :]).astype(BF)
+    k_da, k_d1 = recvs(4), recvs(4)
+    for j in range(1, 4):
+        send(dab.at[peer_rank(j)], da.at[r], k_da + j, peer(j))
+    da[r] = dab[r]
+    for j in range(1, 4):
+        send(d1g.at[r], d1g.at[r], k_d1 + j, peer(j))
+    row_gain_one = row_sum(grad_hidden * normed)
+    row_shift_one = row_sum(grad_hidden)
+    row_out = row_sum(grad_one)
+
+    k_gs_y, k_ge_y = recvs(1), recvs(1)
+    for half in range(2):
+        arrived(rs_c.at[half], k_gs + half)
+        arrived(re_c.at[half], k_ge + half)
+    t_shr[...] = (gs[1 - y, c].astype(F32) + rs_c[1 - y].astype(F32)).astype(BF)
+    send(t_shr, rs_y, k_gs_y, y_mate)
+    at_y = pl.ds(pl.multiple_of(192 * f_y, 64), 192)
+    at_own = pl.ds(pl.multiple_of(192 * f, 64), 192)
+    t_exp[...] = (ge[at_y, :].astype(F32) + re_c[1 - y].astype(F32)).astype(BF)
+    send(t_exp, re_y, k_ge_y, y_mate)
+
+    for j in range(1, 4):
+        arrived(da.at[peer_rank(j)], k_da + j)
+
+    def attend_back(k, carry):
+        outs = []
+        dots = da[k].astype(F32) * a_f[k]
+        for h in range(3):
+            at = slice(64 * h, 64 * h + 64)
+            delta = jnp.sum(dots[:, at], axis=1, keepdims=True)
+            slots = dot_nt(da[k, :, at], vh[h])
+            low = (p_s[h, k].astype(F32) * (slots - delta)).astype(BF)
+            ds_s[h, k] = low
+            outs.append(dot_nn(low, kh[h]) * 0.125)
+        queries = jnp.concatenate(outs, axis=1)
+        qb_s[k] = row_sum(queries)
+        dz[k, :, 0:192] = queries.astype(BF)
+        return carry
+
+    lax.fori_loop(0, 4, attend_back, 0)
+    sums = []
+    for h in range(3):
+        at = slice(64 * h, 64 * h + 64)
+        sums.append(dot_tn(q_s[...].reshape(512, 192)[:, at], ds_s[h].reshape(512, 1024)))
+    for h in range(3):
+        at = slice(64 * h, 64 * h + 64)
+        sums.append(dot_tn(da[...].reshape(512, 192)[:, at], p_s[h].reshape(512, 1024)))
+    sums = jnp.concatenate(sums, axis=0)
+    dkv[0] = sums[:, 0:512].T
+    dkv[1] = sums[:, 512:1024].T
+    dkb[...] = dkv[1 - c].astype(BF)
+    k_dk = recvs(1)
+    send(dkb, dkr, k_dk, core_mate)
+
+    for j in range(1, 4):
+        arrived(d1g.at[peer_rank(j)], k_d1 + j)
+    part = dot_tn(a_b[...].reshape(512, 192), d1g[...].reshape(512, 768))
+    for b in range(8):
+        go[b % 2, b // 2] = part[:, 96 * b : 96 * b + 96].astype(BF)
+    k_go = recvs(1)
+    send(go.at[1 - c], ro_c, k_go, core_mate)
+
+    arrived(dkr, k_dk)
+    keyvals = dkv[c] + dkr[...].astype(F32)
+    vb_s[...] = row_sum(keyvals[:, 192:384])
+    dz[:, :, 192:576] = keyvals.astype(BF).reshape(4, 128, 384)
+
+    def input_part(k):
+        return dot_nt(dz[k], w_in[...])
+
+    k_r3, s_r3 = recvs(4), sends(4)
+
+    def input_step(j, carry):
+        dx_b[j] = input_part(peer_rank(j)).astype(BF)
+        copy_to(dx_b.at[j], rs3.at[j], s_r3 + j, k_r3 + j, peer(j)).start()
+        return carry
+
+    lax.fori_loop(1, 4, input_step, 0)
+    for j in range(1, 4):
+        pending.append(copy_to(dx_b.at[j], rs3.at[j], s_r3 + j, k_r3 + j, peer(j)).wait_send)
+
+    def project_grad(i, carry):
+        at = pl.ds(pl.multiple_of(128 * i, 128), 128)
+        rows = xg[:, :, at].reshape(512, 128)
+        part = dot_tn(rows, dz[...].reshape(512, 576))
+        for slot in range(6):
+            gi[slot, at, :] = part[:, 96 * slot : 96 * slot + 96].astype(BF)
+        return carry
+
+    lax.fori_loop(0, 6, project_grad, 0)
+    k_gi = recvs(2)
+    for half in range(2):
+        at = pl.ds(pl.multiple_of(192 * (2 * half + 1 - c), 64), 192)
+        send(gi.at[:, at, :], ri_c.at[half], k_gi + half, core_mate)
+
+    vg[...] = jnp.zeros((8, 16, 128), F32)
+    rows = jnp.concatenate(
+        [row_out, row_shift_one, row_back, row_shift_two, row_gain_one, row_gain_two], axis=0
+    )
+    for b in range(8):
+        vg[b, 2:8, 0:96] = rows[:, 96 * b : 96 * b + 96]
+    q_row = row_sum(qb_s[:, 0, :])
+    v_row = vb_s[...]
+    for i in range(2):
+        vg[2 * r + i, 0:1, 0:96] = q_row[:, 96 * i : 96 * i + 96]
+        vg[2 * r + i, 1:2, 0:96] = v_row[:, 96 * i : 96 * i + 96]
+    inner_row = row_sum(beg[:, 0, :])
+    for i in range(3):
+        vg[r, 8 + i : 9 + i, :] = inner_row[:, 128 * i : 128 * i + 128]
+        vg[4 + r, 8 + i : 9 + i, :] = inner_row[:, 384 + 128 * i : 512 + 128 * i]
+    k_v = recvs(8)
+    for d in range(1, 8):
+        other = (ctx + d) % 8
+        send(vg.at[other], vr.at[d], k_v + d, (other, seq))
+
+    k_fs, k_re = recvs(4), recvs(1)
+    arrived(rs_y, k_gs_y)
+    fsb[...] = (gs[y, c].astype(F32) + rs_c[y].astype(F32) + rs_y[...].astype(F32)).astype(BF)
+    for k in range(4):
+        send_or_keep(fsb.at[k], fs.at[zh, x], k_fs + 2 * zh + x, dev(c, y, k, zl))
+    arrived(re_y, k_ge_y)
+    te_f[...] = ge[at_own, :].astype(F32) + re_c[y].astype(F32) + re_y[...].astype(F32)
+    te_b[...] = te_f[:, pl.ds(pl.multiple_of(384 * (1 - zh), 128), 384)].astype(BF)
+    send(te_b, re_z, k_re, z_mate)
+
+    k_gi_y = recvs(1)
+    for half in range(2):
+        arrived(ri_c.at[half], k_gi + half)
+    tib[...] = (gi[:, at_y, :].astype(F32) + ri_c[1 - y].astype(F32)).astype(BF)
+    send(tib, ri_y, k_gi_y, y_mate)
+
+    arrived(ro_c, k_go)
+    tob[...] = (go[c].astype(F32) + ro_c[...].astype(F32)).astype(BF)
+    k_go_y, k_fo = recvs(1), recvs(2)
+    s_go, s_fo = sends(1), sends(4)
+    stays = y == zl
+
+    @pl.when(jnp.logical_not(stays))
+    def _():
+        copy_to(tob, ro_y, s_go, k_go_y, y_mate).start()
+
+    @pl.when(stays)
+    def _():
+        arrived(ro_y, k_go_y)
+        tob2[...] = (tob[...].astype(F32) + ro_y[...].astype(F32)).astype(BF)
+        for k in range(4):
+            to = dev(c, y, k, x)
+            away = jnp.logical_or(to[0] != ctx, to[1] != seq)
+
+            @pl.when(away)
+            def _():
+                copy_to(tob2.at[k], fo.at[zh], s_fo + k, k_fo + zh, to).start()
+
+            @pl.when(jnp.logical_not(away))
+            def _():
+                pltpu.make_async_copy(tob2.at[k], fo.at[zh], rsem.at[k_fo + zh]).start()
+
+    def finish_out():
+        @pl.when(jnp.logical_not(stays))
+        def _():
+            copy_to(tob, ro_y, s_go, k_go_y, y_mate).wait_send()
+
+        @pl.when(stays)
+        def _():
+            for k in range(4):
+                to = dev(c, y, k, x)
+
+                @pl.when(jnp.logical_or(to[0] != ctx, to[1] != seq))
+                def _():
+                    copy_to(tob2.at[k], fo.at[zh], s_fo + k, k_fo + zh, to).wait_send()
+
+    pending.append(finish_out)
+
+    grad_in = d1_s[...] + input_part(r)
+    for j in range(1, 4):
+        arrived(rs3.at[j], k_r3 + j)
+        grad_in += rs3[j].astype(F32)
+    ghb[...] = grad_in.astype(BF)
+    k_gh = recvs(1)
+    send_or_keep(ghb, ghr, k_gh, home)
+
+    arrived(ri_y, k_gi_y)
+    ti2[...] = (gi[:, at_own, :].astype(F32) + ri_c[y].astype(F32) + ri_y[...].astype(F32)).astype(BF)
+    k_fi = recvs(6)
+    for slot in range(6):
+        unit = 8 * (slot // 2) + 2 * r + slot % 2
+        send_or_keep(
+            ti2.at[slot], fi.at[zh, unit % 3], k_fi + 3 * zh + unit % 3, (unit // 3, seq)
+        )
+
+    total = vg[ctx]
+    for d in range(1, 8):
+        arrived(vr.at[d], k_v + d)
+        total += vr[d]
+    vs1[...] = total
+    k_vc = recvs(2)
+    send(vs1, vc, k_vc, core_mate)
+    arrived(vc, k_vc)
+    vs2[...] = vs1[...] + vc[...]
+    send(vs2, vy, k_vc + 1, y_mate)
+
+    arrived(ohr, k_o)
+    o_out[...] = ohr[...]
+    for half in range(2):
+        for sub in range(2):
+            arrived(fs.at[half, sub], k_fs + 2 * half + sub)
+    for sub in range(2):
+        o_wshr[384 * sub : 384 * sub + 384, :] = fs[0, sub].astype(F32) + fs[1, sub].astype(F32)
+    arrived(re_z, k_re)
+    o_wexp[...] = te_f[:, pl.ds(pl.multiple_of(384 * zh, 128), 384)] + re_z[...].astype(F32)
+    for half in range(2):
+        arrived(fo.at[half], k_fo + half)
+    o_wout[...] = fo[0].astype(F32) + fo[1].astype(F32)
+    arrived(vy, k_vc + 1)
+    total = vs2[...] + vy[...]
+    o_gb[...] = total[0:6, 0:96]
+    o_gg[...] = total[6:8, 0:96]
+    o_ge[...] = total[8:11, :]
+    for half in range(2):
+        for j in range(3):
+            arrived(fi.at[half, j], k_fi + 3 * half + j)
+    o_win[...] = jnp.concatenate(
+        [fi[0, j].astype(F32) + fi[1, j].astype(F32) for j in range(3)], axis=1
+    )
+    arrived(ghr, k_gh)
+    o_gh[...] = ghr[...]
+    for finish in pending:
+        finish()
+
+
+def fast_shards(
+    hidden, project_in, project_out, expand_weight, shrink_weight, biases, gains, expand_bias,
+    random_blocks, global_blocks, document_lengths, cotangent,
+):
+    vm = lambda *dims: pltpu.VMEM(dims, BF)
+    vf = lambda *dims: pltpu.VMEM(dims, F32)
+    scratch = [
+        vm(3, 192, 96), vm(4, 128, 768), vm(128, 768), vf(8, 128), vf(4, 8, 128), vf(16, 128),
+        vf(8, 16, 128), vm(4, 6, 192, 96), vm(4, 8, 192, 96), vm(4, 192, 768), vm(2, 2, 4, 384, 96),
+        vm(768, 576), vm(768, 768), vm(768, 768), vf(8, 768),
+        vm(4, 128, 192), vm(2, 512, 384), vm(3, 1024, 64), vm(3, 1024, 64), vf(4, 128, 1024),
+        vm(3, 4, 128, 1024), vf(4, 128, 192), vm(4, 128, 192), vm(4, 128, 192), vm(4, 128, 768),
+        vf(128, 768), vf(128, 768), vf(128, 1), vf(4, 128, 768), vm(4, 128, 768), vf(128, 768),
+        vm(4, 128, 768),
+        vm(4, 128, 768), vf(128, 768), vm(4, 128, 768), vm(4, 128, 768), vm(4, 128, 768),
+        vm(4, 128, 768), vf(4, 1, 768), vf(128, 768), vm(4, 128, 768), vm(4, 128, 192),
+        vm(4, 128, 192), vm(3, 4, 128, 1024), vf(2, 512, 384), vm(512, 384), vm(512, 384),
+        vm(4, 128, 576), vm(4, 128, 768), vm(4, 128, 768),
+        vm(2, 2, 4, 384, 96), vm(2, 4, 384, 96), vm(4, 384, 96), vm(4, 384, 96), vm(4, 384, 96),
+        vm(2, 2, 384, 96), vm(768, 768), vm(2, 192, 768), vm(192, 768), vm(192, 768), vf(192, 768),
+        vm(192, 384), vm(192, 384),
+        vm(2, 4, 192, 96), vm(4, 192, 96), vm(4, 192, 96), vm(4, 192, 96), vm(4, 192, 96),
+        vm(2, 192, 96), vm(6, 768, 96), vm(2, 6, 192, 96), vm(6, 192, 96), vm(6, 192, 96),
+        vm(6, 192, 96), vm(2, 3, 192, 96),
+        vf(8, 16, 128), vf(8, 16, 128), vf(16, 128), vf(16, 128), vf(16, 128), vf(16, 128),
+        vf(4, 1, 192), vf(1, 192), vm(128, 768), vm(128, 768), vm(128, 768), vm(128, 768),
+        pltpu.SemaphoreType.DMA((SENDS,)), pltpu.SemaphoreType.DMA((RECVS,)),
+    ]
+    out = lambda kind, *dims: jax.ShapeDtypeStruct(dims, kind)
+    results = pl.pallas_call(
+        layer_kernel,
+        out_shape=(
+            out(BF, 128, 768), out(BF, 128, 768), out(F32, 192, 288), out(F32, 192, 96),
+            out(F32, 192, 384), out(F32, 768, 96), out(F32, 6, 96), out(F32, 2, 96), out(F32, 3, 128),
+        ),
+        in_specs=[pl.BlockSpec(memory_space=pltpu.SMEM)] * 3
+        + [pl.BlockSpec(memory_space=pltpu.VMEM)] * 9,
+        out_specs=tuple([pl.BlockSpec(memory_space=pltpu.VMEM)] * 9),
+        scratch_shapes=scratch,
+        compiler_params=pltpu.CompilerParams(
+            collective_id=0, has_side_effects=True, vmem_limit_bytes=62 * 1024 * 1024
+        ),
+    )(
+        random_blocks[0], global_blocks, document_lengths, hidden[0], cotangent[0], project_in,
+        project_out, expand_weight, shrink_weight.reshape(2, 384, 96), biases, gains,
+        expand_bias.reshape(3, 128),
+    )
+    return (
+        results[0][None], results[1][None], results[2], results[3], results[4], results[5],
+        results[6], results[7], results[8].reshape(-1),
+    )
+
+
 def solution(mesh):
+    small = tuple(mesh.shape[name] for name in ("ctx", "fsdp")) == (8, 4)
     return jax.shard_map(
-        shards,
+        fast_shards if small else shards,
         mesh=mesh,
         in_specs=(
             P("fsdp", "ctx", None),

time: 1380 us -> 179 us (0.13)
  waiting for transfers between devices: 1000 us -> 0 us
  Pallas kernels: 0 us -> 168 us
  blocking collectives: 144 us -> 0 us
  matrix products: 88.5 us -> 0 us
  local copies, waits for them, and re-layouts: 78.7 us -> 9.92 us
  other arithmetic: 43.3 us -> 0 us
  between operations: 14.9 us -> 0.67 us
    reduce_scatter x7 -> x0, waiting for transfers between devices: 644 us -> none  [the longest x1 164 us: over_cols(): lax.psum_scatter(shrink_grad, 'ctx', scatter_dimension=1, tiled=True)]
    unnamed x24 -> x0, waiting for transfers between devices: 230 us -> none
    pallas_call x0 -> x1, Pallas kernels: none -> 168 us  [fast_shards(): pl.pallas_call(layer_kernel, out_shape=(out(BF, 128, 768), out(BF, 128, 7...]
    all_gather x5 -> x0, blocking collectives: 138 us -> none  [the longest x1 35.3 us: shards(): lax.all_gather(project_in, 'ctx', axis=1, tiled=True)]
    all_gather x7 -> x0, waiting for transfers between devices: 126 us -> none  [the longest x1 42.5 us: shards(): lax.all_gather(shrink_weight, 'ctx', axis=1, tiled=True)]
    dot_general x18 -> x0, matrix products: 84 us -> none  [the longest x4 16.6 us: matmul(): return jnp.dot(left_side, right_side, preferred_element_type=jnp.float32)]
    concatenate x5 -> x0, local copies, waits for them, and re-layouts: 21.7 us -> none  [the longest x3 21.5 us: shards(): jnp.concatenate([grad_keys.reshape(blocks_here, link_count, BLOCK, width)...]
    scatter-add x1 -> x0, other arithmetic: 15.3 us -> none  [scatter_rows(): partial_value.at[target]]
  transfers between devices with their start and end apart: 19 -> 0, of which waited for: 18 -> 0; matrix products, arithmetic and copies ran while one was open for 7% -> 0% of each run, Pallas kernels for 0% -> 0%
where the time goes in v2:
time: 179 us
  Pallas kernels  168 us (94%)
  local copies, waits for them, and re-layouts  9.92 us (6%)
    pallas_call x1, Pallas kernels, fast_shards(): pl.pallas_call(layer_kernel, out_shape=(out(BF, 128, 768), out(BF, 128, 7...  168 us
    unnamed x26, local copies, waits for them, and re-layouts  9.92 us

profile of v2, /device:TPU:0, one launch (start us, length us, event | category | flops | bytes accessed | tf_op | source)
XLA Modules:
  0.0 178.7 jit_solution(18068397534331594351)
XLA Ops:
  0.6 1.7 copy.21
  2.4 168.1 %shard_map.187 = (bf16[128,768]{1,0:T(8,128)(2,1)}, bf16[128,768]{1,0:T(8,128)(2,1)}, f32[192,288]{1,0:T(8,128)}, f32[192,96]{1,0:T(8,128)}, f32[192,384]{1,0:T(...) custom-call(s32[2,3]{1,0:T(2,128)} %bitcast.14, s32[1,2]{1,0:T(1,128)} %glob_ref.1, ...), custom_call_target="tpu_custom_call" | custom-call | tf_op jit(solution)/shard_map/pallas_call | solution.py:1030
  170.5 0.0 copy-start.3
  170.5 1.9 %copy.22 = f32[768,96]{0,1:T(8,128)} copy(f32[768,96]{1,0:T(8,128)} %get-tuple-element.32) | data formatting | bytes 589824
  172.4 0.0 copy-done.3
  172.4 0.0 copy-start.2
  172.4 0.7 copy.31
  173.1 0.3 copy-done.2
  173.4 0.0 copy-start.1
  173.4 0.7 copy.32
  174.1 0.4 copy-done.1
  174.4 0.0 copy-start.4
  174.4 0.0 copy-start
  174.4 0.7 copy.33
  175.2 0.2 copy-done.4
  175.4 0.6 copy.34
  176.0 0.0 copy-done
  176.0 0.0 copy-start.5
  176.0 0.7 copy.35
  176.8 0.0 copy-done.5
  176.8 0.0 copy-start.7
  176.8 0.6 copy.36
  177.4 0.1 copy-done.7
  177.4 0.0 copy-start.6
  177.4 0.6 copy.37
  178.0 0.1 copy-done.6
  178.1 0.6 copy.38
Async XLA Ops:
  170.5 1.9 %copy-start.3 = (bf16[128,768]{1,0:T(8,128)(2,1)S(1)}, bf16[128,768]{1,0:T(8,128)(2,1)}, u32[]{:S(2)}) copy-start(bf16[128,768]{1,0:T(8,128)(2,1)} %get-tuple-element.18) | copy-start | bytes 589828
  172.4 1.0 copy-start.2
  173.4 1.0 copy-start.1
  174.4 1.0 copy-start.4
  174.4 1.6 copy-start
  176.0 0.7 copy-start.5
  176.8 0.7 copy-start.7
  177.4 0.7 copy-start.6

commit v3 on v2

--- a/solution.py
+++ b/solution.py
@@ -310,6 +310,7 @@
 F32 = jnp.float32
 SENDS = 128
 RECVS = 128
+LOCALS = 16
 NEG = -1e30
 
 
@@ -329,16 +330,21 @@
     return jnp.sum(values, axis=0, keepdims=True)
 
 
+def pack(piece):
+    return jnp.concatenate([piece[48 * q : 48 * q + 48] for q in range(4)], axis=1)
+
+
 def layer_kernel(
-    rand_ref, glob_ref, doc_ref, hid, cot, win, wout, wexp, wshr, bia, gai, ebi,
+    rand_ref, glob_ref, doc_ref, bia, gai, ebi, hid, cot, win, wout, wexp, wshr,
     o_out, o_gh, o_win, o_wout, o_wexp, o_wshr, o_gb, o_gg, o_ge,
-    win3, xg, eo, ms, mg, ps, par, win_p, wout_p, wexp_f, wshr_p, w_in, w_out, w_shr, prm,
-    q_s, kv, kh, vh, bias_s, p_s, a_f, a_b, a_all, hg, h1_s, n1_s, r1_s, dge, g_s, ysum, yb,
-    rs1, d2_s, dg, du_s, dh_b, rs2, beg, d1_s, d1g, dab, da, ds_s, dkv, dkb, dkr, dz, dx_b, rs3,
+    winv, woutv, win3, wout1, xg, eo, ms, mg, ps, par, win_p, wout_p, wexp_f, ws, w_in, w_out, prm,
+    mq, q_s, kv, kh, vh, e_s, l_s, a_f, a_b, a_all, hg, h1_s, n1_s, r1_s, dge, g_s, ysum, yb,
+    rs1, d2_s, dg, du_s, dh_b, rs2, beg, d1_s, d1g, dab, da, de, ds_s, dkv, dkb, dkr, dz, dx_b, rs3,
     gs, rs_c, t_shr, rs_y, fsb, fs, ge, re_c, t_exp, re_y, te_f, te_b, re_z,
     go, ro_c, tob, ro_y, tob2, fo, gi, ri_c, tib, ri_y, ti2, fi,
     vg, vr, vs1, vc, vs2, vy, qb_s, vb_s, ob, ohr, ghb, ghr,
-    ssem, rsem,
+    f_win, f_wout, f_wexp, f_wshr, f_gb, f_gg, f_ge,
+    ssem, rsem, lsem,
 ):
     ctx = lax.axis_index("ctx")
     seq = lax.axis_index("fsdp")
@@ -366,19 +372,24 @@
     home = dev(x, y, 2 * c + zl, zh)
 
     pending = []
-    counts = {"s": 0, "r": 0}
+    counts = {"s": 0, "r": 0, "l": 0}
+
+    def take(kind, n, most):
+        first = counts[kind]
+        counts[kind] = first + n
+        assert counts[kind] <= most
+        return first
 
     def recvs(n):
-        first = counts["r"]
-        counts["r"] = first + n
-        assert counts["r"] <= RECVS
-        return first
+        return take("r", n, RECVS)
 
     def sends(n):
-        first = counts["s"]
-        counts["s"] = first + n
-        assert counts["s"] <= SENDS
-        return first
+        return take("s", n, SENDS)
+
+    def local(src, dst):
+        cp = pltpu.make_async_copy(src, dst, lsem.at[take("l", 1, LOCALS)])
+        cp.start()
+        return cp
 
     def copy_to(src, dst, si, ri, to):
         return pltpu.make_async_remote_copy(
@@ -421,6 +432,7 @@
             barrier, inc=1, device_id=(other // 2, 2 * y + other % 2), device_id_type=MESH
         )
     pl.semaphore_signal(barrier, inc=1, device_id=y_mate, device_id_type=MESH)
+    in_win, in_wout = local(win, winv), local(wout, woutv)
 
     lane = lax.broadcasted_iota(jnp.int32, (1, 128), 1)
     for i in range(2):
@@ -429,7 +441,7 @@
         links += [rand_ref[i, k] for k in range(3)] + [glob_ref[0, k] for k in range(2)]
         count = jnp.zeros((1, 128), F32)
         for link in links:
-            count += jnp.where(lane == link, 1.0, 0.0)
+            count += jnp.where(jnp.logical_or(lane == link + 72, lane == link + 88), 1.0, 0.0)
         ms[i : i + 1, :] = count
     edge = doc_ref[0, 0]
     edges = jnp.zeros((1, 128), F32)
@@ -438,19 +450,19 @@
         edge = edge + doc_ref[0, k + 1]
     ms[2:3, :] = edges
     ms[3:8, :] = jnp.zeros((5, 128), F32)
-    for j in range(3):
-        win3[j] = win[:, 96 * j : 96 * j + 96]
     ps[...] = jnp.zeros((16, 128), F32)
     ps[0:6, 0:96] = bia[...].astype(F32)
     ps[6:8, 0:96] = gai[...].astype(F32)
     ps[8:11, :] = ebi[...].astype(F32)
+    in_win.wait()
+    for j in range(3):
+        win3[j] = pack(winv[:, 96 * j : 96 * j + 96])
 
     pl.semaphore_wait(barrier, 16)
 
     k_x, k_m, k_e = recvs(4), recvs(4), recvs(1)
     send_or_keep(hid, xg.at[r], k_x, home)
     send_or_keep(ms, mg.at[r], k_m, home)
-    k_par = recvs(8)
     k_win = recvs(6)
     for j in range(3):
         unit = 3 * ctx + j
@@ -460,67 +472,32 @@
             send_or_keep(
                 win3.at[j], win_p.at[f, slot], k_win + slot, dev(rank % 2, y, 2 * half + rank // 2, c)
             )
+    k_par = recvs(8)
     for d in range(1, 8):
         other = (ctx + d) % 8
         send(ps, par.at[ctx], k_par + d, (other, seq))
     par[ctx] = ps[...]
+    in_wout.wait()
+    wout1[...] = pack(woutv[...])
 
     arrived(xg.at[r], k_x)
     arrived(mg.at[r], k_m)
     for j in range(1, 4):
+        send(xg.at[r], xg.at[r], k_x + j, peer(j))
         send(mg.at[r], mg.at[r], k_m + j, peer(j))
-        send(xg.at[r], xg.at[r], k_x + j, peer(j))
-    send_or_keep(cot, eo, k_e, home)
-
-    k_wout = recvs(8)
-    for d in range(8):
-        other = (ctx + d) % 8
-        if d == 0:
-            pltpu.make_async_copy(wout, wout_p.at[f, ctx], rsem.at[k_wout]).start()
-        else:
-            send(wout, wout_p.at[f, ctx], k_wout + d, (other, seq))
-    k_wexp = recvs(2)
-    mine_exp = wexp_f.at[f, :, pl.ds(pl.multiple_of(384 * zh, 128), 384)]
-    pltpu.make_async_copy(wexp, mine_exp, rsem.at[k_wexp]).start()
-    send(wexp, mine_exp, k_wexp + 1, z_mate)
-    k_wshr = recvs(4)
-    for sub in range(2):
-        for half in range(2):
-            send_or_keep(
-                wshr.at[sub], wshr_p.at[y, x, 2 * zh + zl], k_wshr + 2 * zh + zl,
-                dev(sub, y, 2 * half + c, x),
-            )
 
     k_win_y, k_win_c = recvs(1), recvs(2)
     for slot in range(6):
         arrived(win_p.at[f, slot], k_win + slot)
     send(win_p.at[f], win_p.at[f], k_win_y, y_mate)
     send(win_p.at[f], win_p.at[f], k_win_c, core_mate)
-    f_y = 2 * (1 - y) + c
-    arrived(win_p.at[f_y], k_win_y)
-    send(win_p.at[f_y], win_p.at[f_y], k_win_c + 1, core_mate)
-
-    for j in range(1, 4):
-        arrived(mg.at[peer_rank(j)], k_m + j)
-    counted = jnp.concatenate([mg[k, 0:2, :] for k in range(4)], axis=0)
-    spread = (
-        lax.broadcasted_iota(jnp.int32, (128, 1024), 1) // 64
-        == lax.broadcasted_iota(jnp.int32, (128, 1024), 0)
-    ).astype(BF)
-    counted = dot_nn(counted.astype(BF), spread)
-    logs = jnp.where(counted > 0.5, jnp.log(jnp.maximum(counted, 1.0)), NEG)
-    key_pos = lax.broadcasted_iota(jnp.int32, (1, 1024), 1).astype(F32)
-    row_pos = (lax.broadcasted_iota(jnp.int32, (512, 1), 0) + 512 * c).astype(F32)
-    key_seg = jnp.zeros((1, 1024), F32)
-    row_seg = jnp.zeros((512, 1), F32)
-    for k in range(7):
-        at = mg[0, 2:3, k : k + 1]
-        key_seg += jnp.where(key_pos >= at, 1.0, 0.0)
-        row_seg += jnp.where(row_pos >= at, 1.0, 0.0)
-    for i in range(8):
-        bias_s[i // 2, 64 * (i % 2) : 64 * (i % 2) + 64, :] = jnp.where(
-            row_seg[64 * i : 64 * i + 64] == key_seg, logs[i : i + 1, :], NEG
-        )
+    k_wout = recvs(8)
+    for d in range(8):
+        other = (ctx + d) % 8
+        if d == 0:
+            pltpu.make_async_copy(wout1, wout_p.at[f, ctx], rsem.at[k_wout]).start()
+        else:
+            send(wout1, wout_p.at[f, ctx], k_wout + d, (other, seq))
 
     for d in range(1, 8):
         arrived(par.at[(ctx + 8 - d) % 8], k_par + d)
@@ -535,15 +512,65 @@
         axis=1,
     )
 
-
+    def sided(positions, rows):
+        segs = jnp.zeros((rows, 1), F32)
+        for k in range(7):
+            segs += jnp.where(positions >= mg[r, 2:3, k : k + 1], 1.0, 0.0)
+        return segs
+
+    wide = lax.broadcasted_iota(jnp.int32, (1024, 128), 1)
+    key_row = lax.broadcasted_iota(jnp.int32, (1024, 1), 0)
+    key_segs = sided(key_row.astype(F32), 1024).astype(jnp.int32) + 64
+    hot = jnp.logical_or(
+        jnp.logical_and(wide < 72, wide == key_segs),
+        jnp.logical_and(
+            wide >= 72,
+            jnp.logical_or(wide == key_row // 64 + 72, wide == key_row // 64 + 88),
+        ),
+    )
+    hot = jnp.where(hot, 1.0, 0.0).astype(BF)
+    ones = jnp.where(jnp.logical_or(wide == 64, wide == 65), 1.0, 0.0).astype(BF)
+    for h in range(3):
+        kh[h, :, 64:128] = hot[:, 64:128]
+        vh[h, :, 64:128] = ones[:, 64:128]
+    row_pos = lax.broadcasted_iota(jnp.int32, (512, 1), 0) + 512 * c
+    row_segs = sided(row_pos.astype(F32), 512).astype(jnp.int32) + 64
+    for j in range(1, 4):
+        arrived(mg.at[peer_rank(j)], k_m + j)
+    for i in range(8):
+        count = mg[i // 2, i % 2 : i % 2 + 1, :]
+        logs = jnp.log(jnp.maximum(count, 1.0))
+        high = logs.astype(BF).astype(F32)
+        line = jnp.where(lane < 88, jnp.where(count > 0.5, high, NEG), logs - high)
+        line = jnp.where(lane < 104, line, 0.0)
+        same = row_segs[64 * i : 64 * i + 64] == wide[0:64]
+        block = jnp.where(wide[0:64] < 72, jnp.where(same, 0.0, NEG), line)
+        mq[i // 2, 64 * (i % 2) : 64 * (i % 2) + 64, :] = block.astype(BF)
+    for h in range(3):
+        q_s[:, h, :, 64:128] = mq[:, :, 64:128]
+
+    f_y = 2 * (1 - y) + c
+    arrived(win_p.at[f_y], k_win_y)
+    send(win_p.at[f_y], win_p.at[f_y], k_win_c + 1, core_mate)
+
+    def place_in(k):
+        for q in range(4):
+            w_in[pl.ds(pl.multiple_of(192 * k + 48 * q, 16), 48), :] = jnp.concatenate(
+                [win_p[k, i, :, 96 * q : 96 * q + 96] for i in range(6)], axis=1
+            )
+
+    place_in(f)
+    place_in(f_y)
     arrived(win_p.at[2 * y + 1 - c], k_win_c)
+    place_in(2 * y + 1 - c)
     arrived(win_p.at[2 * (1 - y) + 1 - c], k_win_c + 1)
-    for k in range(4):
-        w_in[192 * k : 192 * k + 192, :] = jnp.concatenate([win_p[k, i] for i in range(6)], axis=1)
+    place_in(2 * (1 - y) + 1 - c)
 
     def project(k):
         mixed = dot_nn(xg[k], w_in[...]) + z_bias
-        q_s[k] = (mixed[:, 0:192].astype(BF).astype(F32) * 0.125).astype(BF)
+        queries = (mixed[:, 0:192].astype(BF).astype(F32) * 0.125).astype(BF)
+        for h in range(3):
+            q_s[k, h, :, 0:64] = queries[:, 64 * h : 64 * h + 64]
         kv[c, pl.ds(pl.multiple_of(128 * k, 128), 128), :] = mixed[:, 192:576].astype(BF)
 
     project(r)
@@ -558,6 +585,18 @@
     k_kv = recvs(1)
     send(kv.at[c], kv.at[c], k_kv, core_mate)
 
+    k_wexp = recvs(2)
+    mine_exp = wexp_f.at[f, :, pl.ds(pl.multiple_of(384 * zh, 128), 384)]
+    pltpu.make_async_copy(wexp, mine_exp, rsem.at[k_wexp]).start()
+    send(wexp, mine_exp, k_wexp + 1, z_mate)
+    k_wshr = recvs(4)
+    at_half = pl.ds(pl.multiple_of(384 * y, 128), 384)
+    for sub in range(2):
+        for half in range(2):
+            send_or_keep(
+                wshr.at[:, 384 * sub : 384 * sub + 384], ws.at[2 * zh + zl, x, :, at_half],
+                k_wshr + 2 * zh + zl, dev(sub, y, 2 * half + c, x),
+            )
     k_wout_y, k_wout_c = recvs(1), recvs(2)
     k_wexp_y, k_wexp_c = recvs(1), recvs(2)
     k_wshr_y, k_wshr_c = recvs(1), recvs(2)
@@ -566,64 +605,67 @@
     send(wout_p.at[f], wout_p.at[f], k_wout_y, y_mate)
     send(wout_p.at[f], wout_p.at[f], k_wout_c, core_mate)
 
+    def split_heads(half):
+        at = pl.ds(pl.multiple_of(512 * half, 512), 512)
+        for h in range(3):
+            kh[h, at, 0:64] = kv[half, :, 64 * h : 64 * h + 64]
+            vh[h, at, 0:64] = kv[half, :, 192 + 64 * h : 256 + 64 * h]
+
+    split_heads(c)
     arrived(kv.at[1 - c], k_kv)
-    for h in range(3):
-        for half in range(2):
-            kh[h, 512 * half : 512 * half + 512, :] = kv[half, :, 64 * h : 64 * h + 64]
-            vh[h, 512 * half : 512 * half + 512, :] = kv[half, :, 192 + 64 * h : 256 + 64 * h]
+    split_heads(1 - c)
 
     def attend(k, carry):
         outs = []
         for h in range(3):
-            scores = dot_nt(q_s[k, :, 64 * h : 64 * h + 64], kh[h]) + bias_s[k]
+            scores = dot_nt(q_s[k, h], kh[h])
             top = jnp.max(scores, axis=1, keepdims=True)
-            exps = jnp.exp(scores - top)
-            total = jnp.sum(exps, axis=1, keepdims=True)
-            weights = (exps * (1.0 / total)).astype(BF)
-            p_s[h, k] = weights
-            outs.append(dot_nn(weights, vh[h]))
+            exps = jnp.exp(scores - top).astype(BF)
+            e_s[h, k] = exps
+            sums = dot_nn(exps, vh[h])
+            scale = 1.0 / sums[:, 64:65]
+            l_s[h, k] = scale
+            outs.append(sums[:, 0:64] * scale)
         both = jnp.concatenate(outs, axis=1)
         a_f[k] = both
         a_b[k] = both.astype(BF)
         return carry
 
-    lax.fori_loop(0, 2, attend, 0)
-    for half in range(2):
-        at = pl.ds(pl.multiple_of(384 * half, 128), 384)
-        piece = wexp_f.at[f, :, at]
-        own = half == zh
-
-        @pl.when(own)
-        def _():
-            arrived(piece, k_wexp)
-
-        @pl.when(jnp.logical_not(own))
-        def _():
-            arrived(piece, k_wexp + 1)
-
+    lax.fori_loop(0, 1, attend, 0)
+    arrived(wout_p.at[f_y], k_wout_y)
+    send(wout_p.at[f_y], wout_p.at[f_y], k_wout_c + 1, core_mate)
+    lax.fori_loop(1, 2, attend, 0)
+    arrived(mine_exp, k_wexp)
+    arrived(wexp_f.at[f, :, pl.ds(pl.multiple_of(384 * (1 - zh), 128), 384)], k_wexp + 1)
     send(wexp_f.at[f], wexp_f.at[f], k_wexp_y, y_mate)
     send(wexp_f.at[f], wexp_f.at[f], k_wexp_c, core_mate)
+    lax.fori_loop(2, 3, attend, 0)
     for k in range(4):
-        arrived(wshr_p.at[y, c, k], k_wshr + k)
-    send(wshr_p.at[y, c], wshr_p.at[y, c], k_wshr_y, y_mate)
-    send(wshr_p.at[y, c], wshr_p.at[y, c], k_wshr_c, core_mate)
-    arrived(wout_p.at[f_y], k_wout_y)
-    send(wout_p.at[f_y], wout_p.at[f_y], k_wout_c + 1, core_mate)
-    lax.fori_loop(2, 4, attend, 0)
+        arrived(ws.at[k, c, :, at_half], k_wshr + k)
+    send(ws.at[:, c, :, at_half], ws.at[:, c, :, at_half], k_wshr_y, y_mate)
+    send(ws.at[:, c, :, at_half], ws.at[:, c, :, at_half], k_wshr_c, core_mate)
+    lax.fori_loop(3, 4, attend, 0)
 
     k_a = recvs(4)
     for j in range(1, 4):
         send(a_b.at[peer_rank(j)], a_all.at[r], k_a + j, peer(j))
     a_all[r] = a_b[r]
-
+    send_or_keep(cot, eo, k_e, home)
+
+    def place_out(k):
+        for q in range(4):
+            w_out[pl.ds(pl.multiple_of(192 * k + 48 * q, 16), 48), :] = jnp.concatenate(
+                [wout_p[k, b, :, 96 * q : 96 * q + 96] for b in range(8)], axis=1
+            )
+
+    place_out(f)
+    place_out(f_y)
+    arrived(wout_p.at[2 * y + 1 - c], k_wout_c)
+    place_out(2 * y + 1 - c)
+    arrived(wout_p.at[2 * (1 - y) + 1 - c], k_wout_c + 1)
+    place_out(2 * (1 - y) + 1 - c)
     arrived(wexp_f.at[f_y], k_wexp_y)
     send(wexp_f.at[f_y], wexp_f.at[f_y], k_wexp_c + 1, core_mate)
-    arrived(wshr_p.at[1 - y, c], k_wshr_y)
-    send(wshr_p.at[1 - y, c], wshr_p.at[1 - y, c], k_wshr_c + 1, core_mate)
-    arrived(wout_p.at[2 * y + 1 - c], k_wout_c)
-    arrived(wout_p.at[2 * (1 - y) + 1 - c], k_wout_c + 1)
-    for k in range(4):
-        w_out[192 * k : 192 * k + 192, :] = jnp.concatenate([wout_p[k, b] for b in range(8)], axis=1)
 
     for j in range(1, 4):
         arrived(a_all.at[peer_rank(j)], k_a + j)
@@ -634,22 +676,21 @@
     inverse = lax.rsqrt(jnp.mean(centre * centre, axis=1, keepdims=True) + 1e-05)
     normed = centre * inverse
     hidden_one = normed * prm[6:7, :] + prm[3:4, :]
+    hg[r] = hidden_one.astype(BF)
+    k_h = recvs(4)
+    for j in range(1, 4):
+        send(hg.at[r], hg.at[r], k_h + j, peer(j))
     n1_s[...] = normed
     r1_s[...] = inverse
     h1_s[...] = hidden_one
-    hg[r] = hidden_one.astype(BF)
-    k_h = recvs(4)
-    for j in range(1, 4):
-        send(hg.at[r], hg.at[r], k_h + j, peer(j))
-
+
+    other_half = pl.ds(pl.multiple_of(384 * (1 - y), 128), 384)
+    arrived(ws.at[:, c, :, other_half], k_wshr_y)
+    send(ws.at[:, c, :, other_half], ws.at[:, c, :, other_half], k_wshr_c + 1, core_mate)
     arrived(wexp_f.at[2 * y + 1 - c], k_wexp_c)
     arrived(wexp_f.at[2 * (1 - y) + 1 - c], k_wexp_c + 1)
-    arrived(wshr_p.at[y, 1 - c], k_wshr_c)
-    arrived(wshr_p.at[1 - y, 1 - c], k_wshr_c + 1)
-    for half in range(2):
-        w_shr[384 * half : 384 * half + 384, :] = jnp.concatenate(
-            [wshr_p[half, b % 2, b // 2] for b in range(8)], axis=1
-        )
+    arrived(ws.at[:, 1 - c, :, at_half], k_wshr_c)
+    arrived(ws.at[:, 1 - c, :, other_half], k_wshr_c + 1)
 
     def expand(k):
         inner = dot_nn(hg[k], wexp_f[...].reshape(768, 768)) + be
@@ -657,7 +698,7 @@
         dge[k] = below + inner * jnp.exp(-0.5 * inner * inner) * 0.3989422804014327
         active = (inner * below).astype(BF)
         g_s[k] = active
-        return dot_nn(active, w_shr[...])
+        return dot_nt(active, ws[...].reshape(768, 768))
 
     ysum[...] = expand(r)
     k_r1, s_r1 = recvs(4), sends(4)
@@ -675,6 +716,9 @@
 
     arrived(eo, k_e)
     upstream = eo[...].astype(F32)
+    scaled = upstream * prm[7:8, :]
+    scaled_mean = jnp.mean(scaled, axis=1, keepdims=True)
+    row_shift_two = row_sum(upstream)
     second = h1_s[...] + prm[4:5, :] + ysum[...]
     for j in range(1, 4):
         arrived(rs1.at[j], k_r1 + j)
@@ -682,26 +726,22 @@
     centre = second - jnp.mean(second, axis=1, keepdims=True)
     inverse = lax.rsqrt(jnp.mean(centre * centre, axis=1, keepdims=True) + 1e-05)
     normed = centre * inverse
-    scaled = upstream * prm[7:8, :]
     grad_two = inverse * (
-        scaled
-        - jnp.mean(scaled, axis=1, keepdims=True)
-        - normed * jnp.mean(scaled * normed, axis=1, keepdims=True)
-    )
-    d2_s[...] = grad_two
+        scaled - scaled_mean - normed * jnp.mean(scaled * normed, axis=1, keepdims=True)
+    )
     dg[r] = grad_two.astype(BF)
     k_d = recvs(4)
     for j in range(1, 4):
         send(dg.at[r], dg.at[r], k_d + j, peer(j))
+    d2_s[...] = grad_two
     ob[...] = (normed * prm[7:8, :] + prm[5:6, :]).astype(BF)
     k_o = recvs(1)
     send_or_keep(ob, ohr, k_o, home)
     row_gain_two = row_sum(upstream * normed)
-    row_shift_two = row_sum(upstream)
     row_back = row_sum(grad_two)
 
     def contract(k):
-        inner = dge[k] * dot_nt(dg[k], w_shr[...])
+        inner = dge[k] * dot_nn(dg[k], ws[...].reshape(768, 768))
         low = inner.astype(BF)
         du_s[k] = low
         beg[k] = row_sum(inner)
@@ -721,24 +761,11 @@
     for j in range(1, 4):
         pending.append(copy_to(dh_b.at[j], rs2.at[j], s_r2 + j, k_r2 + j, peer(j)).wait_send)
 
-    def shrink_grad(half):
-        def step(i, carry):
-            at = pl.multiple_of(384 * half + 128 * i, 128)
-            rows = g_s[:, :, pl.ds(at, 128)].reshape(512, 128)
-            part = dot_tn(rows, dg[...].reshape(512, 768))
-            for b in range(8):
-                gs[half, b % 2, b // 2, pl.ds(pl.multiple_of(128 * i, 128), 128), :] = part[
-                    :, 96 * b : 96 * b + 96
-                ].astype(BF)
-            return carry
-
-        lax.fori_loop(0, 3, step, 0)
-
-    shrink_grad(0)
-    shrink_grad(1)
-    k_gs = recvs(2)
-    for half in range(2):
-        send(gs.at[half, 1 - c], rs_c.at[half], k_gs + half, core_mate)
+    for k in range(4):
+        rows = dg[:, :, 192 * k : 192 * k + 192].reshape(512, 192)
+        gs[k] = dot_tn(rows, g_s[...].reshape(512, 768)).astype(BF).reshape(2, 96, 768)
+    k_gs = recvs(1)
+    send(gs.at[:, 1 - c], rs_c, k_gs, core_mate)
 
     def expand_grad(i, carry):
         at = pl.ds(pl.multiple_of(128 * i, 128), 128)
@@ -751,6 +778,12 @@
     for half in range(2):
         at = pl.ds(pl.multiple_of(192 * (2 * half + 1 - c), 64), 192)
         send(ge.at[at, :], re_c.at[half], k_ge + half, core_mate)
+    k_gs_y, k_ge_y = recvs(1), recvs(1)
+    arrived(rs_c, k_gs)
+    t_shr[...] = (
+        gs[:, c, :, other_half].astype(F32) + rs_c[:, :, other_half].astype(F32)
+    ).astype(BF)
+    send(t_shr, rs_y, k_gs_y, y_mate)
 
     grad_hidden = d2_s[...] + ysum[...]
     for j in range(1, 4):
@@ -763,7 +796,6 @@
         - jnp.mean(scaled, axis=1, keepdims=True)
         - normed * jnp.mean(scaled * normed, axis=1, keepdims=True)
     )
-    d1_s[...] = grad_one
     low_one = grad_one.astype(BF)
     d1g[r] = low_one
     for k in range(4):
@@ -772,18 +804,13 @@
     for j in range(1, 4):
         send(dab.at[peer_rank(j)], da.at[r], k_da + j, peer(j))
     da[r] = dab[r]
-    for j in range(1, 4):
-        send(d1g.at[r], d1g.at[r], k_d1 + j, peer(j))
+    d1_s[...] = grad_one
     row_gain_one = row_sum(grad_hidden * normed)
     row_shift_one = row_sum(grad_hidden)
     row_out = row_sum(grad_one)
 
-    k_gs_y, k_ge_y = recvs(1), recvs(1)
     for half in range(2):
-        arrived(rs_c.at[half], k_gs + half)
         arrived(re_c.at[half], k_ge + half)
-    t_shr[...] = (gs[1 - y, c].astype(F32) + rs_c[1 - y].astype(F32)).astype(BF)
-    send(t_shr, rs_y, k_gs_y, y_mate)
     at_y = pl.ds(pl.multiple_of(192 * f_y, 64), 192)
     at_own = pl.ds(pl.multiple_of(192 * f, 64), 192)
     t_exp[...] = (ge[at_y, :].astype(F32) + re_c[1 - y].astype(F32)).astype(BF)
@@ -791,30 +818,50 @@
 
     for j in range(1, 4):
         arrived(da.at[peer_rank(j)], k_da + j)
+        send(d1g.at[r], d1g.at[r], k_d1 + j, peer(j))
 
     def attend_back(k, carry):
         outs = []
-        dots = da[k].astype(F32) * a_f[k]
+        grads = da[k].astype(F32)
+        dots = grads * a_f[k]
         for h in range(3):
             at = slice(64 * h, 64 * h + 64)
-            delta = jnp.sum(dots[:, at], axis=1, keepdims=True)
-            slots = dot_nt(da[k, :, at], vh[h])
-            low = (p_s[h, k].astype(F32) * (slots - delta)).astype(BF)
+            scale = l_s[h, k]
+            delta = jnp.sum(dots[:, at], axis=1, keepdims=True) * scale
+            high = delta.astype(BF).astype(F32)
+            side = jnp.where(wide[0:128, 0:64] == 0, -high, 0.0)
+            side = jnp.where(wide[0:128, 0:64] == 1, high - delta, side)
+            both = jnp.concatenate([grads[:, at] * scale, side], axis=1).astype(BF)
+            de[k, h] = both
+            low = (e_s[h, k].astype(F32) * dot_nt(both, vh[h])).astype(BF)
             ds_s[h, k] = low
-            outs.append(dot_nn(low, kh[h]) * 0.125)
+            outs.append(dot_nn(low, kh[h])[:, 0:64] * 0.125)
         queries = jnp.concatenate(outs, axis=1)
         qb_s[k] = row_sum(queries)
         dz[k, :, 0:192] = queries.astype(BF)
         return carry
 
-    lax.fori_loop(0, 4, attend_back, 0)
+    lax.fori_loop(0, 1, attend_back, 0)
+    k_fs, k_re = recvs(4), recvs(1)
+    arrived(rs_y, k_gs_y)
+    fsb[...] = (
+        gs[:, c, :, at_half].astype(F32) + rs_c[:, :, at_half].astype(F32) + rs_y[...].astype(F32)
+    ).astype(BF)
+    for k in range(4):
+        send_or_keep(fsb.at[k], fs.at[zh, x], k_fs + 2 * zh + x, dev(c, y, k, zl))
+    lax.fori_loop(1, 2, attend_back, 0)
+    arrived(re_y, k_ge_y)
+    te_f[...] = ge[at_own, :].astype(F32) + re_c[y].astype(F32) + re_y[...].astype(F32)
+    te_b[...] = te_f[:, pl.ds(pl.multiple_of(384 * (1 - zh), 128), 384)].astype(BF)
+    send(te_b, re_z, k_re, z_mate)
+    lax.fori_loop(2, 4, attend_back, 0)
     sums = []
     for h in range(3):
-        at = slice(64 * h, 64 * h + 64)
-        sums.append(dot_tn(q_s[...].reshape(512, 192)[:, at], ds_s[h].reshape(512, 1024)))
+        rows = q_s[:, h, :, 0:64].reshape(512, 64)
+        sums.append(dot_tn(rows, ds_s[h].reshape(512, 1024)))
     for h in range(3):
-        at = slice(64 * h, 64 * h + 64)
-        sums.append(dot_tn(da[...].reshape(512, 192)[:, at], p_s[h].reshape(512, 1024)))
+        rows = de[:, h, :, 0:64].reshape(512, 64)
+        sums.append(dot_tn(rows, e_s[h].reshape(512, 1024)))
     sums = jnp.concatenate(sums, axis=0)
     dkv[0] = sums[:, 0:512].T
     dkv[1] = sums[:, 512:1024].T
@@ -826,7 +873,7 @@
         arrived(d1g.at[peer_rank(j)], k_d1 + j)
     part = dot_tn(a_b[...].reshape(512, 192), d1g[...].reshape(512, 768))
     for b in range(8):
-        go[b % 2, b // 2] = part[:, 96 * b : 96 * b + 96].astype(BF)
+        go[b % 2, b // 2] = pack(part[:, 96 * b : 96 * b + 96].astype(BF))
     k_go = recvs(1)
     send(go.at[1 - c], ro_c, k_go, core_mate)
 
@@ -849,19 +896,14 @@
     for j in range(1, 4):
         pending.append(copy_to(dx_b.at[j], rs3.at[j], s_r3 + j, k_r3 + j, peer(j)).wait_send)
 
-    def project_grad(i, carry):
-        at = pl.ds(pl.multiple_of(128 * i, 128), 128)
-        rows = xg[:, :, at].reshape(512, 128)
-        part = dot_tn(rows, dz[...].reshape(512, 576))
+    for k in range(4):
+        rows = xg[:, :, 192 * k : 192 * k + 192].reshape(512, 192)
+        part = dot_tn(rows, dz[...].reshape(512, 576)).astype(BF)
         for slot in range(6):
-            gi[slot, at, :] = part[:, 96 * slot : 96 * slot + 96].astype(BF)
-        return carry
-
-    lax.fori_loop(0, 6, project_grad, 0)
+            gi[k, slot] = pack(part[:, 96 * slot : 96 * slot + 96])
     k_gi = recvs(2)
     for half in range(2):
-        at = pl.ds(pl.multiple_of(192 * (2 * half + 1 - c), 64), 192)
-        send(gi.at[:, at, :], ri_c.at[half], k_gi + half, core_mate)
+        send(gi.at[2 * half + 1 - c], ri_c.at[half], k_gi + half, core_mate)
 
     vg[...] = jnp.zeros((8, 16, 128), F32)
     rows = jnp.concatenate(
@@ -883,20 +925,10 @@
         other = (ctx + d) % 8
         send(vg.at[other], vr.at[d], k_v + d, (other, seq))
 
-    k_fs, k_re = recvs(4), recvs(1)
-    arrived(rs_y, k_gs_y)
-    fsb[...] = (gs[y, c].astype(F32) + rs_c[y].astype(F32) + rs_y[...].astype(F32)).astype(BF)
-    for k in range(4):
-        send_or_keep(fsb.at[k], fs.at[zh, x], k_fs + 2 * zh + x, dev(c, y, k, zl))
-    arrived(re_y, k_ge_y)
-    te_f[...] = ge[at_own, :].astype(F32) + re_c[y].astype(F32) + re_y[...].astype(F32)
-    te_b[...] = te_f[:, pl.ds(pl.multiple_of(384 * (1 - zh), 128), 384)].astype(BF)
-    send(te_b, re_z, k_re, z_mate)
-
     k_gi_y = recvs(1)
     for half in range(2):
         arrived(ri_c.at[half], k_gi + half)
-    tib[...] = (gi[:, at_y, :].astype(F32) + ri_c[1 - y].astype(F32)).astype(BF)
+    tib[...] = (gi[f_y].astype(F32) + ri_c[1 - y].astype(F32)).astype(BF)
     send(tib, ri_y, k_gi_y, y_mate)
 
     arrived(ro_c, k_go)
@@ -908,6 +940,35 @@
     @pl.when(jnp.logical_not(stays))
     def _():
         copy_to(tob, ro_y, s_go, k_go_y, y_mate).start()
+
+    done = []
+
+    for half in range(2):
+        for sub in range(2):
+            arrived(fs.at[half, sub], k_fs + 2 * half + sub)
+    for sub in range(2):
+        f_wshr[:, 384 * sub : 384 * sub + 384] = fs[0, sub].astype(F32) + fs[1, sub].astype(F32)
+    done.append(local(f_wshr, o_wshr))
+    arrived(re_z, k_re)
+    f_wexp[...] = te_f[:, pl.ds(pl.multiple_of(384 * zh, 128), 384)] + re_z[...].astype(F32)
+    done.append(local(f_wexp, o_wexp))
+
+    grad_in = d1_s[...] + input_part(r)
+    for j in range(1, 4):
+        arrived(rs3.at[j], k_r3 + j)
+        grad_in += rs3[j].astype(F32)
+    ghb[...] = grad_in.astype(BF)
+    k_gh = recvs(1)
+    send_or_keep(ghb, ghr, k_gh, home)
+
+    arrived(ri_y, k_gi_y)
+    ti2[...] = (gi[f].astype(F32) + ri_c[y].astype(F32) + ri_y[...].astype(F32)).astype(BF)
+    k_fi = recvs(6)
+    for slot in range(6):
+        unit = 8 * (slot // 2) + 2 * r + slot % 2
+        send_or_keep(
+            ti2.at[slot], fi.at[zh, unit % 3], k_fi + 3 * zh + unit % 3, (unit // 3, seq)
+        )
 
     @pl.when(stays)
     def _():
@@ -940,23 +1001,6 @@
                     copy_to(tob2.at[k], fo.at[zh], s_fo + k, k_fo + zh, to).wait_send()
 
     pending.append(finish_out)
-
-    grad_in = d1_s[...] + input_part(r)
-    for j in range(1, 4):
-        arrived(rs3.at[j], k_r3 + j)
-        grad_in += rs3[j].astype(F32)
-    ghb[...] = grad_in.astype(BF)
-    k_gh = recvs(1)
-    send_or_keep(ghb, ghr, k_gh, home)
-
-    arrived(ri_y, k_gi_y)
-    ti2[...] = (gi[:, at_own, :].astype(F32) + ri_c[y].astype(F32) + ri_y[...].astype(F32)).astype(BF)
-    k_fi = recvs(6)
-    for slot in range(6):
-        unit = 8 * (slot // 2) + 2 * r + slot % 2
-        send_or_keep(
-            ti2.at[slot], fi.at[zh, unit % 3], k_fi + 3 * zh + unit % 3, (unit // 3, seq)
-        )
 
     total = vg[ctx]
     for d in range(1, 8):
@@ -970,32 +1014,47 @@
     send(vs2, vy, k_vc + 1, y_mate)
 
     arrived(ohr, k_o)
-    o_out[...] = ohr[...]
-    for half in range(2):
-        for sub in range(2):
-            arrived(fs.at[half, sub], k_fs + 2 * half + sub)
-    for sub in range(2):
-        o_wshr[384 * sub : 384 * sub + 384, :] = fs[0, sub].astype(F32) + fs[1, sub].astype(F32)
-    arrived(re_z, k_re)
-    o_wexp[...] = te_f[:, pl.ds(pl.multiple_of(384 * zh, 128), 384)] + re_z[...].astype(F32)
+    done.append(local(ohr, o_out))
+    arrived(vy, k_vc + 1)
+    total = vs2[...] + vy[...]
+    f_gb[...] = total[0:6, 0:96]
+    f_gg[...] = total[6:8, 0:96]
+    f_ge[...] = total[8:11, :]
+    done += [local(f_gb, o_gb), local(f_gg, o_gg), local(f_ge, o_ge)]
     for half in range(2):
         arrived(fo.at[half], k_fo + half)
-    o_wout[...] = fo[0].astype(F32) + fo[1].astype(F32)
-    arrived(vy, k_vc + 1)
-    total = vs2[...] + vy[...]
-    o_gb[...] = total[0:6, 0:96]
-    o_gg[...] = total[6:8, 0:96]
-    o_ge[...] = total[8:11, :]
+    part = fo[0].astype(F32) + fo[1].astype(F32)
+    for q in range(4):
+        f_wout[48 * q : 48 * q + 48, :] = part[:, 96 * q : 96 * q + 96]
+    done.append(local(f_wout, o_wout))
     for half in range(2):
         for j in range(3):
             arrived(fi.at[half, j], k_fi + 3 * half + j)
-    o_win[...] = jnp.concatenate(
-        [fi[0, j].astype(F32) + fi[1, j].astype(F32) for j in range(3)], axis=1
-    )
+    parts = [fi[0, j].astype(F32) + fi[1, j].astype(F32) for j in range(3)]
+    for q in range(4):
+        f_win[48 * q : 48 * q + 48, :] = jnp.concatenate(
+            [part[:, 96 * q : 96 * q + 96] for part in parts], axis=1
+        )
+    done.append(local(f_win, o_win))
     arrived(ghr, k_gh)
-    o_gh[...] = ghr[...]
+    done.append(local(ghr, o_gh))
     for finish in pending:
         finish()
+    for copy in done:
+        copy.wait()
+
+
+def hand_over(*refs):
+    ins, outs, held, into, out_of = refs[0:9], refs[9:18], refs[18:27], refs[27], refs[28]
+    loads = [pltpu.make_async_copy(ins[i], held[i], into.at[i]) for i in range(9)]
+    stores = [pltpu.make_async_copy(held[i], outs[i], out_of.at[i]) for i in range(9)]
+    for load in loads:
+        load.start()
+    for load, store in zip(loads, stores):
+        load.wait()
+        store.start()
+    for store in stores:
+        store.wait()
 
 
 def fast_shards(
@@ -1005,48 +1064,61 @@
     vm = lambda *dims: pltpu.VMEM(dims, BF)
     vf = lambda *dims: pltpu.VMEM(dims, F32)
     scratch = [
-        vm(3, 192, 96), vm(4, 128, 768), vm(128, 768), vf(8, 128), vf(4, 8, 128), vf(16, 128),
-        vf(8, 16, 128), vm(4, 6, 192, 96), vm(4, 8, 192, 96), vm(4, 192, 768), vm(2, 2, 4, 384, 96),
-        vm(768, 576), vm(768, 768), vm(768, 768), vf(8, 768),
-        vm(4, 128, 192), vm(2, 512, 384), vm(3, 1024, 64), vm(3, 1024, 64), vf(4, 128, 1024),
-        vm(3, 4, 128, 1024), vf(4, 128, 192), vm(4, 128, 192), vm(4, 128, 192), vm(4, 128, 768),
-        vf(128, 768), vf(128, 768), vf(128, 1), vf(4, 128, 768), vm(4, 128, 768), vf(128, 768),
-        vm(4, 128, 768),
+        vm(192, 288), vm(192, 96), vm(3, 48, 384), vm(48, 384), vm(4, 128, 768), vm(128, 768),
+        vf(8, 128), vf(4, 8, 128), vf(16, 128), vf(8, 16, 128), vm(4, 6, 48, 384), vm(4, 8, 48, 384),
+        vm(4, 192, 768), vm(4, 2, 96, 768), vm(768, 576), vm(768, 768), vf(8, 768),
+        vm(4, 128, 128), vm(4, 3, 128, 128), vm(2, 512, 384), vm(3, 1024, 128), vm(3, 1024, 128),
+        vm(3, 4, 128, 1024), vf(3, 4, 128, 1), vf(4, 128, 192), vm(4, 128, 192), vm(4, 128, 192),
+        vm(4, 128, 768), vf(128, 768), vf(128, 768), vf(128, 1), vf(4, 128, 768), vm(4, 128, 768),
+        vf(128, 768), vm(4, 128, 768),
         vm(4, 128, 768), vf(128, 768), vm(4, 128, 768), vm(4, 128, 768), vm(4, 128, 768),
         vm(4, 128, 768), vf(4, 1, 768), vf(128, 768), vm(4, 128, 768), vm(4, 128, 192),
-        vm(4, 128, 192), vm(3, 4, 128, 1024), vf(2, 512, 384), vm(512, 384), vm(512, 384),
-        vm(4, 128, 576), vm(4, 128, 768), vm(4, 128, 768),
-        vm(2, 2, 4, 384, 96), vm(2, 4, 384, 96), vm(4, 384, 96), vm(4, 384, 96), vm(4, 384, 96),
-        vm(2, 2, 384, 96), vm(768, 768), vm(2, 192, 768), vm(192, 768), vm(192, 768), vf(192, 768),
+        vm(4, 128, 192), vm(4, 3, 128, 128), vm(3, 4, 128, 1024), vf(2, 512, 384), vm(512, 384),
+        vm(512, 384), vm(4, 128, 576), vm(4, 128, 768), vm(4, 128, 768),
+        vm(4, 2, 96, 768), vm(4, 96, 768), vm(4, 96, 384), vm(4, 96, 384), vm(4, 96, 384),
+        vm(2, 2, 96, 384), vm(768, 768), vm(2, 192, 768), vm(192, 768), vm(192, 768), vf(192, 768),
         vm(192, 384), vm(192, 384),
-        vm(2, 4, 192, 96), vm(4, 192, 96), vm(4, 192, 96), vm(4, 192, 96), vm(4, 192, 96),
-        vm(2, 192, 96), vm(6, 768, 96), vm(2, 6, 192, 96), vm(6, 192, 96), vm(6, 192, 96),
-        vm(6, 192, 96), vm(2, 3, 192, 96),
+        vm(2, 4, 48, 384), vm(4, 48, 384), vm(4, 48, 384), vm(4, 48, 384), vm(4, 48, 384),
+        vm(2, 48, 384), vm(4, 6, 48, 384), vm(2, 6, 48, 384), vm(6, 48, 384), vm(6, 48, 384),
+        vm(6, 48, 384), vm(2, 3, 48, 384),
         vf(8, 16, 128), vf(8, 16, 128), vf(16, 128), vf(16, 128), vf(16, 128), vf(16, 128),
         vf(4, 1, 192), vf(1, 192), vm(128, 768), vm(128, 768), vm(128, 768), vm(128, 768),
+        vf(192, 288), vf(192, 96), vf(192, 384), vf(96, 768), vf(6, 96), vf(2, 96), vf(3, 128),
         pltpu.SemaphoreType.DMA((SENDS,)), pltpu.SemaphoreType.DMA((RECVS,)),
+        pltpu.SemaphoreType.DMA((LOCALS,)),
     ]
     out = lambda kind, *dims: jax.ShapeDtypeStruct(dims, kind)
+    shapes = (
+        out(BF, 128, 768), out(BF, 128, 768), out(F32, 192, 288), out(F32, 192, 96),
+        out(F32, 192, 384), out(F32, 96, 768), out(F32, 6, 96), out(F32, 2, 96), out(F32, 3, 128),
+    )
+    anywhere = pl.BlockSpec(memory_space=pl.ANY)
     results = pl.pallas_call(
         layer_kernel,
-        out_shape=(
-            out(BF, 128, 768), out(BF, 128, 768), out(F32, 192, 288), out(F32, 192, 96),
-            out(F32, 192, 384), out(F32, 768, 96), out(F32, 6, 96), out(F32, 2, 96), out(F32, 3, 128),
-        ),
+        out_shape=shapes,
         in_specs=[pl.BlockSpec(memory_space=pltpu.SMEM)] * 3
-        + [pl.BlockSpec(memory_space=pltpu.VMEM)] * 9,
-        out_specs=tuple([pl.BlockSpec(memory_space=pltpu.VMEM)] * 9),
+        + [pl.BlockSpec(memory_space=pltpu.VMEM)] * 3
+        + [anywhere] * 6,
+        out_specs=(anywhere,) * 9,
         scratch_shapes=scratch,
         compiler_params=pltpu.CompilerParams(
-            collective_id=0, has_side_effects=True, vmem_limit_bytes=62 * 1024 * 1024
+            collective_id=0, has_side_effects=True, vmem_limit_bytes=58 * 1024 * 1024
         ),
     )(
-        random_blocks[0], global_blocks, document_lengths, hidden[0], cotangent[0], project_in,
-        project_out, expand_weight, shrink_weight.reshape(2, 384, 96), biases, gains,
-        expand_bias.reshape(3, 128),
-    )
+        random_blocks[0], global_blocks, document_lengths, biases, gains,
+        expand_bias.reshape(3, 128), hidden[0], cotangent[0], project_in, project_out,
+        expand_weight, shrink_weight.T,
+    )
+    results = pl.pallas_call(
+        hand_over,
+        out_shape=shapes,
+        in_specs=[anywhere] * 9,
+        out_specs=(anywhere,) * 9,
+        scratch_shapes=[pltpu.VMEM(one.shape, one.dtype) for one in shapes]
+        + [pltpu.SemaphoreType.DMA((9,))] * 2,
+    )(*results)
     return (
-        results[0][None], results[1][None], results[2], results[3], results[4], results[5],
+        results[0][None], results[1][None], results[2], results[3], results[4], results[5].T,
         results[6], results[7], results[8].reshape(-1),
     )
 

time: 179 us -> 144 us (0.80)
  Pallas kernels: 168 us -> 143 us
  local copies, waits for them, and re-layouts: 9.92 us -> 0 us
    pallas_call x1 -> x2, Pallas kernels: 168 us -> 143 us  [the longest x1 141 us: fast_shards(): pl.pallas_call(layer_kernel, out_shape=shapes, in_specs=[pl.BlockSpec(mem...]
    unnamed x26 -> x0, local copies, waits for them, and re-layouts: 9.92 us -> none
where the time goes in v3:
time: 144 us
  Pallas kernels  143 us (99%)
    pallas_call x1, Pallas kernels, fast_shards(): pl.pallas_call(layer_kernel, out_shape=shapes, in_specs=[pl.BlockSpec(mem...  141 us

profile of v3, /device:TPU:0, one launch (start us, length us, event | category | flops | bytes accessed | tf_op | source)
XLA Modules:
  0.0 144.1 jit_solution(5601428624231486421)
XLA Ops:
  0.6 141.0 %shard_map.187 = (bf16[128,768]{1,0:T(8,128)(2,1)}, bf16[128,768]{1,0:T(8,128)(2,1)}, f32[192,288]{1,0:T(8,128)}, f32[192,96]{1,0:T(8,128)}, f32[192,384]{1,0:T(...) custom-call(s32[2,3]{1,0:T(2,128)} %bitcast.12, s32[1,2]{1,0:T(1,128)} %glob_ref.1, ...), custom_call_target="tpu_custom_call" | custom-call | tf_op jit(solution)/shard_map/pallas_call | solution.py:1096
  141.6 2.3 %shard_map.188 = (bf16[128,768]{1,0:T(8,128)(2,1)}, bf16[128,768]{1,0:T(8,128)(2,1)}, f32[192,288]{1,0:T(8,128)}, f32[192,96]{1,0:T(8,128)}, f32[192,384]{1,0:T(...) custom-call(bf16[128,768]{1,0:T(8,128)(2,1)} %get-tuple-element.27.refs_0_, ...), custom_call_target="tpu_custom_call" | custom-call | tf_op jit(solution)/shard_map/pallas_call | solution.py:1112

commit v4 on v3

--- a/solution.py
+++ b/solution.py
@@ -308,8 +308,8 @@
 MESH = pl.DeviceIdType.MESH
 BF = jnp.bfloat16
 F32 = jnp.float32
-SENDS = 128
-RECVS = 128
+SENDS = 160
+RECVS = 160
 LOCALS = 16
 NEG = -1e30
 
@@ -338,7 +338,7 @@
     rand_ref, glob_ref, doc_ref, bia, gai, ebi, hid, cot, win, wout, wexp, wshr,
     o_out, o_gh, o_win, o_wout, o_wexp, o_wshr, o_gb, o_gg, o_ge,
     winv, woutv, win3, wout1, xg, eo, ms, mg, ps, par, win_p, wout_p, wexp_f, ws, w_in, w_out, prm,
-    mq, q_s, kv, kh, vh, e_s, l_s, a_f, a_b, a_all, hg, h1_s, n1_s, r1_s, dge, g_s, ysum, yb,
+    mq, q_s, kv, kh, vh, e_s, l_s, a_f, a_b, a_all, hg, h1_s, n1_s, r1_s, u_s, dge, g_s, ysum, yb,
     rs1, d2_s, dg, du_s, dh_b, rs2, beg, d1_s, d1g, dab, da, de, ds_s, dkv, dkb, dkr, dz, dx_b, rs3,
     gs, rs_c, t_shr, rs_y, fsb, fs, ge, re_c, t_exp, re_y, te_f, te_b, re_z,
     go, ro_c, tob, ro_y, tob2, fo, gi, ri_c, tib, ri_y, ti2, fi,
@@ -423,6 +423,17 @@
 
     def arrived(dst, ri):
         pltpu.make_async_copy(dst, dst, rsem.at[ri]).wait()
+
+    def pass_on(buf, first):
+        for j, at in ((1, pl.ds(0, 64)), (2, pl.ds(64, 64))):
+            rank = peer_rank(j)
+            arrived(buf.at[rank], first + j)
+            send(buf.at[rank, at], buf.at[rank, at], first + 3 * (2 - j), peer(3 - j))
+
+    def far_arrived(buf, first):
+        rank = peer_rank(3)
+        arrived(buf.at[rank, pl.ds(0, 64)], first + 3)
+        arrived(buf.at[rank, pl.ds(64, 64)], first)
 
     barrier = pltpu.get_barrier_semaphore()
     place = 2 * ctx + c
@@ -460,8 +471,8 @@
 
     pl.semaphore_wait(barrier, 16)
 
-    k_x, k_m, k_e = recvs(4), recvs(4), recvs(1)
-    send_or_keep(hid, xg.at[r], k_x, home)
+    k_h, k_x, k_m, k_e = recvs(1), recvs(4), recvs(4), recvs(1)
+    send_or_keep(hid, xg.at[r], k_h, home)
     send_or_keep(ms, mg.at[r], k_m, home)
     k_win = recvs(6)
     for j in range(3):
@@ -480,17 +491,15 @@
     in_wout.wait()
     wout1[...] = pack(woutv[...])
 
-    arrived(xg.at[r], k_x)
+    arrived(xg.at[r], k_h)
     arrived(mg.at[r], k_m)
     for j in range(1, 4):
-        send(xg.at[r], xg.at[r], k_x + j, peer(j))
+        if j < 3:
+            send(xg.at[r], xg.at[r], k_x + j, peer(j))
         send(mg.at[r], mg.at[r], k_m + j, peer(j))
-
-    k_win_y, k_win_c = recvs(1), recvs(2)
-    for slot in range(6):
-        arrived(win_p.at[f, slot], k_win + slot)
-    send(win_p.at[f], win_p.at[f], k_win_y, y_mate)
-    send(win_p.at[f], win_p.at[f], k_win_c, core_mate)
+    k_wout_y, k_wout_c = recvs(1), recvs(2)
+    k_wexp_y, k_wexp_c = recvs(1), recvs(2)
+    k_wshr_y, k_wshr_c = recvs(1), recvs(2)
     k_wout = recvs(8)
     for d in range(8):
         other = (ctx + d) % 8
@@ -499,18 +508,6 @@
         else:
             send(wout1, wout_p.at[f, ctx], k_wout + d, (other, seq))
 
-    for d in range(1, 8):
-        arrived(par.at[(ctx + 8 - d) % 8], k_par + d)
-    prm[...] = jnp.concatenate([par[b, 0:8, 0:96] for b in range(8)], axis=1)
-    be = jnp.concatenate(
-        [par[r, 8 + i : 9 + i, :] for i in range(3)] + [par[4 + r, 8 + i : 9 + i, :] for i in range(3)],
-        axis=1,
-    )
-    zrow = jnp.zeros((1, 192), F32)
-    z_bias = jnp.concatenate(
-        [par[2 * r, 0:1, 0:96], par[2 * r + 1, 0:1, 0:96], zrow, par[2 * r, 1:2, 0:96], par[2 * r + 1, 1:2, 0:96]],
-        axis=1,
-    )
 
     def sided(positions, rows):
         segs = jnp.zeros((rows, 1), F32)
@@ -533,6 +530,31 @@
     for h in range(3):
         kh[h, :, 64:128] = hot[:, 64:128]
         vh[h, :, 64:128] = ones[:, 64:128]
+
+    k_win_y, k_win_c = recvs(1), recvs(2)
+    for slot in range(6):
+        arrived(win_p.at[f, slot], k_win + slot)
+    send(win_p.at[f], win_p.at[f], k_win_y, y_mate)
+    send(win_p.at[f], win_p.at[f], k_win_c, core_mate)
+    pass_on(xg, k_x)
+    k_wexp = recvs(2)
+    mine_exp = wexp_f.at[f, :, pl.ds(pl.multiple_of(384 * zh, 128), 384)]
+    pltpu.make_async_copy(wexp, mine_exp, rsem.at[k_wexp]).start()
+    send(wexp, mine_exp, k_wexp + 1, z_mate)
+
+    for d in range(1, 8):
+        arrived(par.at[(ctx + 8 - d) % 8], k_par + d)
+    prm[...] = jnp.concatenate([par[b, 0:8, 0:96] for b in range(8)], axis=1)
+    be = jnp.concatenate(
+        [par[r, 8 + i : 9 + i, :] for i in range(3)] + [par[4 + r, 8 + i : 9 + i, :] for i in range(3)],
+        axis=1,
+    )
+    zrow = jnp.zeros((1, 192), F32)
+    z_bias = jnp.concatenate(
+        [par[2 * r, 0:1, 0:96], par[2 * r + 1, 0:1, 0:96], zrow, par[2 * r, 1:2, 0:96], par[2 * r + 1, 1:2, 0:96]],
+        axis=1,
+    )
+
     row_pos = lax.broadcasted_iota(jnp.int32, (512, 1), 0) + 512 * c
     row_segs = sided(row_pos.astype(F32), 512).astype(jnp.int32) + 64
     for j in range(1, 4):
@@ -552,43 +574,10 @@
     f_y = 2 * (1 - y) + c
     arrived(win_p.at[f_y], k_win_y)
     send(win_p.at[f_y], win_p.at[f_y], k_win_c + 1, core_mate)
-
-    def place_in(k):
-        for q in range(4):
-            w_in[pl.ds(pl.multiple_of(192 * k + 48 * q, 16), 48), :] = jnp.concatenate(
-                [win_p[k, i, :, 96 * q : 96 * q + 96] for i in range(6)], axis=1
-            )
-
-    place_in(f)
-    place_in(f_y)
-    arrived(win_p.at[2 * y + 1 - c], k_win_c)
-    place_in(2 * y + 1 - c)
-    arrived(win_p.at[2 * (1 - y) + 1 - c], k_win_c + 1)
-    place_in(2 * (1 - y) + 1 - c)
-
-    def project(k):
-        mixed = dot_nn(xg[k], w_in[...]) + z_bias
-        queries = (mixed[:, 0:192].astype(BF).astype(F32) * 0.125).astype(BF)
-        for h in range(3):
-            q_s[k, h, :, 0:64] = queries[:, 64 * h : 64 * h + 64]
-        kv[c, pl.ds(pl.multiple_of(128 * k, 128), 128), :] = mixed[:, 192:576].astype(BF)
-
-    project(r)
-
-    def project_step(j, carry):
-        rank = peer_rank(j)
-        arrived(xg.at[rank], k_x + j)
-        project(rank)
-        return carry
-
-    lax.fori_loop(1, 4, project_step, 0)
-    k_kv = recvs(1)
-    send(kv.at[c], kv.at[c], k_kv, core_mate)
-
-    k_wexp = recvs(2)
-    mine_exp = wexp_f.at[f, :, pl.ds(pl.multiple_of(384 * zh, 128), 384)]
-    pltpu.make_async_copy(wexp, mine_exp, rsem.at[k_wexp]).start()
-    send(wexp, mine_exp, k_wexp + 1, z_mate)
+    for d in range(8):
+        arrived(wout_p.at[f, (ctx + 8 - d) % 8], k_wout + d)
+    send(wout_p.at[f], wout_p.at[f], k_wout_y, y_mate)
+    send(wout_p.at[f], wout_p.at[f], k_wout_c, core_mate)
     k_wshr = recvs(4)
     at_half = pl.ds(pl.multiple_of(384 * y, 128), 384)
     for sub in range(2):
@@ -597,13 +586,40 @@
                 wshr.at[:, 384 * sub : 384 * sub + 384], ws.at[2 * zh + zl, x, :, at_half],
                 k_wshr + 2 * zh + zl, dev(sub, y, 2 * half + c, x),
             )
-    k_wout_y, k_wout_c = recvs(1), recvs(2)
-    k_wexp_y, k_wexp_c = recvs(1), recvs(2)
-    k_wshr_y, k_wshr_c = recvs(1), recvs(2)
-    for d in range(8):
-        arrived(wout_p.at[f, (ctx + 8 - d) % 8], k_wout + d)
-    send(wout_p.at[f], wout_p.at[f], k_wout_y, y_mate)
-    send(wout_p.at[f], wout_p.at[f], k_wout_c, core_mate)
+
+
+    def place_in(k):
+        for q in range(4):
+            w_in[pl.ds(pl.multiple_of(192 * k + 48 * q, 16), 48), :] = jnp.concatenate(
+                [win_p[k, i, :, 96 * q : 96 * q + 96] for i in range(6)], axis=1
+            )
+
+    place_in(f)
+    place_in(f_y)
+    arrived(win_p.at[2 * y + 1 - c], k_win_c)
+    place_in(2 * y + 1 - c)
+    arrived(win_p.at[2 * (1 - y) + 1 - c], k_win_c + 1)
+    place_in(2 * (1 - y) + 1 - c)
+
+    def project(k):
+        mixed = dot_nn(xg[k], w_in[...]) + z_bias
+        queries = (mixed[:, 0:192].astype(BF).astype(F32) * 0.125).astype(BF)
+        for h in range(3):
+            q_s[k, h, :, 0:64] = queries[:, 64 * h : 64 * h + 64]
+        kv[c, pl.ds(pl.multiple_of(128 * k, 128), 128), :] = mixed[:, 192:576].astype(BF)
+
+    project(r)
+
+    def project_step(j, carry):
+        rank = peer_rank(j)
+        project(rank)
+        return carry
+
+    lax.fori_loop(1, 3, project_step, 0)
+    far_arrived(xg, k_x)
+    lax.fori_loop(3, 4, project_step, 0)
+    k_kv = recvs(1)
+    send(kv.at[c], kv.at[c], k_kv, core_mate)
 
     def split_heads(half):
         at = pl.ds(pl.multiple_of(512 * half, 512), 512)
@@ -612,8 +628,14 @@
             vh[h, at, 0:64] = kv[half, :, 192 + 64 * h : 256 + 64 * h]
 
     split_heads(c)
+    arrived(mine_exp, k_wexp)
+    arrived(wexp_f.at[f, :, pl.ds(pl.multiple_of(384 * (1 - zh), 128), 384)], k_wexp + 1)
+    send(wexp_f.at[f], wexp_f.at[f], k_wexp_y, y_mate)
+    send(wexp_f.at[f], wexp_f.at[f], k_wexp_c, core_mate)
     arrived(kv.at[1 - c], k_kv)
     split_heads(1 - c)
+
+    k_a, s_a = recvs(16), sends(16)
 
     def attend(k, carry):
         outs = []
@@ -628,30 +650,33 @@
             outs.append(sums[:, 0:64] * scale)
         both = jnp.concatenate(outs, axis=1)
         a_f[k] = both
-        a_b[k] = both.astype(BF)
+        low = both.astype(BF)
+        a_b[k] = low
+        a_all[r, k] = jnp.concatenate([low[0:64], low[64:128]], axis=1)
+        for j in range(1, 4):
+            at = 4 * j + k
+            copy_to(a_all.at[r, k], a_all.at[r, k], s_a + at, k_a + at, peer(j)).start()
         return carry
 
     lax.fori_loop(0, 1, attend, 0)
     arrived(wout_p.at[f_y], k_wout_y)
     send(wout_p.at[f_y], wout_p.at[f_y], k_wout_c + 1, core_mate)
     lax.fori_loop(1, 2, attend, 0)
-    arrived(mine_exp, k_wexp)
-    arrived(wexp_f.at[f, :, pl.ds(pl.multiple_of(384 * (1 - zh), 128), 384)], k_wexp + 1)
-    send(wexp_f.at[f], wexp_f.at[f], k_wexp_y, y_mate)
-    send(wexp_f.at[f], wexp_f.at[f], k_wexp_c, core_mate)
-    lax.fori_loop(2, 3, attend, 0)
     for k in range(4):
         arrived(ws.at[k, c, :, at_half], k_wshr + k)
     send(ws.at[:, c, :, at_half], ws.at[:, c, :, at_half], k_wshr_y, y_mate)
     send(ws.at[:, c, :, at_half], ws.at[:, c, :, at_half], k_wshr_c, core_mate)
+    lax.fori_loop(2, 3, attend, 0)
+    arrived(wexp_f.at[f_y], k_wexp_y)
+    send(wexp_f.at[f_y], wexp_f.at[f_y], k_wexp_c + 1, core_mate)
     lax.fori_loop(3, 4, attend, 0)
-
-    k_a = recvs(4)
     for j in range(1, 4):
-        send(a_b.at[peer_rank(j)], a_all.at[r], k_a + j, peer(j))
-    a_all[r] = a_b[r]
+        for k in range(4):
+            at = 4 * j + k
+            pending.append(
+                copy_to(a_all.at[r, k], a_all.at[r, k], s_a + at, k_a + at, peer(j)).wait_send
+            )
     send_or_keep(cot, eo, k_e, home)
-
     def place_out(k):
         for q in range(4):
             w_out[pl.ds(pl.multiple_of(192 * k + 48 * q, 16), 48), :] = jnp.concatenate(
@@ -664,55 +689,67 @@
     place_out(2 * y + 1 - c)
     arrived(wout_p.at[2 * (1 - y) + 1 - c], k_wout_c + 1)
     place_out(2 * (1 - y) + 1 - c)
-    arrived(wexp_f.at[f_y], k_wexp_y)
-    send(wexp_f.at[f_y], wexp_f.at[f_y], k_wexp_c + 1, core_mate)
-
-    for j in range(1, 4):
-        arrived(a_all.at[peer_rank(j)], k_a + j)
-    first = xg[r].astype(F32) + prm[2:3, :]
-    for k in range(4):
-        first += dot_nn(a_all[k], w_out[192 * k : 192 * k + 192, :])
-    centre = first - jnp.mean(first, axis=1, keepdims=True)
-    inverse = lax.rsqrt(jnp.mean(centre * centre, axis=1, keepdims=True) + 1e-05)
-    normed = centre * inverse
-    hidden_one = normed * prm[6:7, :] + prm[3:4, :]
-    hg[r] = hidden_one.astype(BF)
-    k_h = recvs(4)
-    for j in range(1, 4):
-        send(hg.at[r], hg.at[r], k_h + j, peer(j))
-    n1_s[...] = normed
-    r1_s[...] = inverse
-    h1_s[...] = hidden_one
-
     other_half = pl.ds(pl.multiple_of(384 * (1 - y), 128), 384)
     arrived(ws.at[:, c, :, other_half], k_wshr_y)
     send(ws.at[:, c, :, other_half], ws.at[:, c, :, other_half], k_wshr_c + 1, core_mate)
+    for j in range(1, 4):
+        for k in range(4):
+            arrived(a_all.at[peer_rank(j), k], k_a + 4 * j + k)
     arrived(wexp_f.at[2 * y + 1 - c], k_wexp_c)
     arrived(wexp_f.at[2 * (1 - y) + 1 - c], k_wexp_c + 1)
     arrived(ws.at[:, 1 - c, :, at_half], k_wshr_c)
     arrived(ws.at[:, 1 - c, :, other_half], k_wshr_c + 1)
 
+    def first_norm(k):
+        rows = jnp.concatenate(
+            [
+                jnp.concatenate([a_all[src, k, :, 192 * i : 192 * i + 192] for src in range(4)], axis=1)
+                for i in range(2)
+            ],
+            axis=0,
+        )
+        first = xg[k].astype(F32) + prm[2:3, :] + dot_nn(rows, w_out[...])
+        centre = first - jnp.mean(first, axis=1, keepdims=True)
+        inverse = lax.rsqrt(jnp.mean(centre * centre, axis=1, keepdims=True) + 1e-05)
+        normed = centre * inverse
+        hidden_one = normed * prm[6:7, :] + prm[3:4, :]
+        hg[k] = hidden_one.astype(BF)
+        return normed, inverse, hidden_one
+
     def expand(k):
         inner = dot_nn(hg[k], wexp_f[...].reshape(768, 768)) + be
         below = 0.5 * (1.0 + lax.erf(inner * 0.7071067811865476))
-        dge[k] = below + inner * jnp.exp(-0.5 * inner * inner) * 0.3989422804014327
+        u_s[k] = inner
+        dge[k] = below
         active = (inner * below).astype(BF)
         g_s[k] = active
         return dot_nt(active, ws[...].reshape(768, 768))
 
-    ysum[...] = expand(r)
     k_r1, s_r1 = recvs(4), sends(4)
 
-    def expand_step(j, carry):
+    def expand_step(i, carry):
+        j = 3 - i
         rank = peer_rank(j)
-        arrived(hg.at[rank], k_h + j)
+        first_norm(rank)
         yb[j] = expand(rank).astype(BF)
         copy_to(yb.at[j], rs1.at[j], s_r1 + j, k_r1 + j, peer(j)).start()
         return carry
 
-    lax.fori_loop(1, 4, expand_step, 0)
+    lax.fori_loop(0, 3, expand_step, 0)
     for j in range(1, 4):
         pending.append(copy_to(yb.at[j], rs1.at[j], s_r1 + j, k_r1 + j, peer(j)).wait_send)
+    normed, inverse, hidden_one = first_norm(r)
+    n1_s[...] = normed
+    r1_s[...] = inverse
+    h1_s[...] = hidden_one
+    ysum[...] = expand(r)
+
+    def slope(k, carry):
+        inner = u_s[k]
+        dge[k] = dge[k] + inner * jnp.exp(-0.5 * inner * inner) * 0.3989422804014327
+        return carry
+
+    lax.fori_loop(0, 4, slope, 0)
 
     arrived(eo, k_e)
     upstream = eo[...].astype(F32)
@@ -731,7 +768,7 @@
     )
     dg[r] = grad_two.astype(BF)
     k_d = recvs(4)
-    for j in range(1, 4):
+    for j in range(1, 3):
         send(dg.at[r], dg.at[r], k_d + j, peer(j))
     d2_s[...] = grad_two
     ob[...] = (normed * prm[7:8, :] + prm[5:6, :]).astype(BF)
@@ -752,12 +789,14 @@
 
     def contract_step(j, carry):
         rank = peer_rank(j)
-        arrived(dg.at[rank], k_d + j)
         dh_b[j] = contract(rank).astype(BF)
         copy_to(dh_b.at[j], rs2.at[j], s_r2 + j, k_r2 + j, peer(j)).start()
         return carry
 
-    lax.fori_loop(1, 4, contract_step, 0)
+    pass_on(dg, k_d)
+    lax.fori_loop(1, 3, contract_step, 0)
+    far_arrived(dg, k_d)
+    lax.fori_loop(3, 4, contract_step, 0)
     for j in range(1, 4):
         pending.append(copy_to(dh_b.at[j], rs2.at[j], s_r2 + j, k_r2 + j, peer(j)).wait_send)
 
@@ -818,6 +857,7 @@
 
     for j in range(1, 4):
         arrived(da.at[peer_rank(j)], k_da + j)
+    for j in range(1, 3):
         send(d1g.at[r], d1g.at[r], k_d1 + j, peer(j))
 
     def attend_back(k, carry):
@@ -854,7 +894,9 @@
     te_f[...] = ge[at_own, :].astype(F32) + re_c[y].astype(F32) + re_y[...].astype(F32)
     te_b[...] = te_f[:, pl.ds(pl.multiple_of(384 * (1 - zh), 128), 384)].astype(BF)
     send(te_b, re_z, k_re, z_mate)
-    lax.fori_loop(2, 4, attend_back, 0)
+    lax.fori_loop(2, 3, attend_back, 0)
+    pass_on(d1g, k_d1)
+    lax.fori_loop(3, 4, attend_back, 0)
     sums = []
     for h in range(3):
         rows = q_s[:, h, :, 0:64].reshape(512, 64)
@@ -869,8 +911,48 @@
     k_dk = recvs(1)
     send(dkb, dkr, k_dk, core_mate)
 
-    for j in range(1, 4):
-        arrived(d1g.at[peer_rank(j)], k_d1 + j)
+    def project_grad(first, count):
+        for k in range(4):
+            rows = xg[:, :, 192 * k : 192 * k + 192].reshape(512, 192)
+            cols = dz[:, :, 96 * first : 96 * first + 96 * count].reshape(512, 96 * count)
+            part = dot_tn(rows, cols).astype(BF)
+            for slot in range(count):
+                gi[k, first + slot] = pack(part[:, 96 * slot : 96 * slot + 96])
+
+    some = {"q": pl.ds(0, 2), "kv": pl.ds(2, 4)}
+    k_gi = {"q": recvs(2), "kv": recvs(2)}
+    k_gi_y = {"q": recvs(1), "kv": recvs(1)}
+
+    def over_cores(which):
+        at = some[which]
+        for half in range(2):
+            send(gi.at[2 * half + 1 - c, at], ri_c.at[half, at], k_gi[which] + half, core_mate)
+
+    def over_y(which):
+        at = some[which]
+        for half in range(2):
+            arrived(ri_c.at[half, at], k_gi[which] + half)
+        tib[at] = (gi[f_y, at].astype(F32) + ri_c[1 - y, at].astype(F32)).astype(BF)
+        send(tib.at[at], ri_y.at[at], k_gi_y[which], y_mate)
+
+    k_fi = recvs(6)
+
+    def to_owners(which):
+        at = some[which]
+        arrived(ri_y.at[at], k_gi_y[which])
+        ti2[at] = (
+            gi[f, at].astype(F32) + ri_c[y, at].astype(F32) + ri_y[at].astype(F32)
+        ).astype(BF)
+        for slot in range(2) if which == "q" else range(2, 6):
+            unit = 8 * (slot // 2) + 2 * r + slot % 2
+            send_or_keep(
+                ti2.at[slot], fi.at[zh, unit % 3], k_fi + 3 * zh + unit % 3, (unit // 3, seq)
+            )
+
+    project_grad(0, 2)
+    over_cores("q")
+
+    far_arrived(d1g, k_d1)
     part = dot_tn(a_b[...].reshape(512, 192), d1g[...].reshape(512, 768))
     for b in range(8):
         go[b % 2, b // 2] = pack(part[:, 96 * b : 96 * b + 96].astype(BF))
@@ -885,25 +967,30 @@
     def input_part(k):
         return dot_nt(dz[k], w_in[...])
 
-    k_r3, s_r3 = recvs(4), sends(4)
-
-    def input_step(j, carry):
+    k_r3, s_r3 = recvs(8), sends(8)
+
+    def near(buf, j, i):
+        return buf.at[j, pl.ds(64 * i, 64)]
+
+    def input_copy(j, i):
+        at = 2 * j + i
+        return copy_to(near(dx_b, j, i), near(rs3, j, i), s_r3 + at, k_r3 + at, peer(j))
+
+    def input_step(i, carry):
+        j = 3 - i
         dx_b[j] = input_part(peer_rank(j)).astype(BF)
-        copy_to(dx_b.at[j], rs3.at[j], s_r3 + j, k_r3 + j, peer(j)).start()
+        input_copy(j, 0).start()
         return carry
 
-    lax.fori_loop(1, 4, input_step, 0)
+    lax.fori_loop(0, 3, input_step, 0)
+    for j in (3, 2, 1):
+        input_copy(j, 1).start()
     for j in range(1, 4):
-        pending.append(copy_to(dx_b.at[j], rs3.at[j], s_r3 + j, k_r3 + j, peer(j)).wait_send)
-
-    for k in range(4):
-        rows = xg[:, :, 192 * k : 192 * k + 192].reshape(512, 192)
-        part = dot_tn(rows, dz[...].reshape(512, 576)).astype(BF)
-        for slot in range(6):
-            gi[k, slot] = pack(part[:, 96 * slot : 96 * slot + 96])
-    k_gi = recvs(2)
-    for half in range(2):
-        send(gi.at[2 * half + 1 - c], ri_c.at[half], k_gi + half, core_mate)
+        for i in range(2):
+            pending.append(input_copy(j, i).wait_send)
+    over_y("q")
+    project_grad(2, 4)
+    over_cores("kv")
 
     vg[...] = jnp.zeros((8, 16, 128), F32)
     rows = jnp.concatenate(
@@ -925,12 +1012,7 @@
         other = (ctx + d) % 8
         send(vg.at[other], vr.at[d], k_v + d, (other, seq))
 
-    k_gi_y = recvs(1)
-    for half in range(2):
-        arrived(ri_c.at[half], k_gi + half)
-    tib[...] = (gi[f_y].astype(F32) + ri_c[1 - y].astype(F32)).astype(BF)
-    send(tib, ri_y, k_gi_y, y_mate)
-
+    over_y("kv")
     arrived(ro_c, k_go)
     tob[...] = (go[c].astype(F32) + ro_c[...].astype(F32)).astype(BF)
     k_go_y, k_fo = recvs(1), recvs(2)
@@ -940,6 +1022,21 @@
     @pl.when(jnp.logical_not(stays))
     def _():
         copy_to(tob, ro_y, s_go, k_go_y, y_mate).start()
+
+    k_gh = recvs(2)
+    ysum[...] = d1_s[...] + input_part(r)
+
+    def finish_input(i):
+        at = pl.ds(64 * i, 64)
+        grad_in = ysum[at, :]
+        for j in range(1, 4):
+            arrived(near(rs3, j, i), k_r3 + 2 * j + i)
+            grad_in += rs3[j, at, :].astype(F32)
+        ghb[at, :] = grad_in.astype(BF)
+        send_or_keep(ghb.at[at, :], ghr.at[at, :], k_gh + i, home)
+
+    to_owners("q")
+    finish_input(0)
 
     done = []
 
@@ -953,22 +1050,8 @@
     f_wexp[...] = te_f[:, pl.ds(pl.multiple_of(384 * zh, 128), 384)] + re_z[...].astype(F32)
     done.append(local(f_wexp, o_wexp))
 
-    grad_in = d1_s[...] + input_part(r)
-    for j in range(1, 4):
-        arrived(rs3.at[j], k_r3 + j)
-        grad_in += rs3[j].astype(F32)
-    ghb[...] = grad_in.astype(BF)
-    k_gh = recvs(1)
-    send_or_keep(ghb, ghr, k_gh, home)
-
-    arrived(ri_y, k_gi_y)
-    ti2[...] = (gi[f].astype(F32) + ri_c[y].astype(F32) + ri_y[...].astype(F32)).astype(BF)
-    k_fi = recvs(6)
-    for slot in range(6):
-        unit = 8 * (slot // 2) + 2 * r + slot % 2
-        send_or_keep(
-            ti2.at[slot], fi.at[zh, unit % 3], k_fi + 3 * zh + unit % 3, (unit // 3, seq)
-        )
+    finish_input(1)
+    to_owners("kv")
 
     @pl.when(stays)
     def _():
@@ -1036,7 +1119,8 @@
             [part[:, 96 * q : 96 * q + 96] for part in parts], axis=1
         )
     done.append(local(f_win, o_win))
-    arrived(ghr, k_gh)
+    for i in range(2):
+        arrived(ghr.at[pl.ds(64 * i, 64), :], k_gh + i)
     done.append(local(ghr, o_gh))
     for finish in pending:
         finish()
@@ -1068,8 +1152,8 @@
         vf(8, 128), vf(4, 8, 128), vf(16, 128), vf(8, 16, 128), vm(4, 6, 48, 384), vm(4, 8, 48, 384),
         vm(4, 192, 768), vm(4, 2, 96, 768), vm(768, 576), vm(768, 768), vf(8, 768),
         vm(4, 128, 128), vm(4, 3, 128, 128), vm(2, 512, 384), vm(3, 1024, 128), vm(3, 1024, 128),
-        vm(3, 4, 128, 1024), vf(3, 4, 128, 1), vf(4, 128, 192), vm(4, 128, 192), vm(4, 128, 192),
-        vm(4, 128, 768), vf(128, 768), vf(128, 768), vf(128, 1), vf(4, 128, 768), vm(4, 128, 768),
+        vm(3, 4, 128, 1024), vf(3, 4, 128, 1), vf(4, 128, 192), vm(4, 128, 192), vm(4, 4, 64, 384),
+        vm(4, 128, 768), vf(128, 768), vf(128, 768), vf(128, 1), vf(4, 128, 768), vf(4, 128, 768), vm(4, 128, 768),
         vf(128, 768), vm(4, 128, 768),
         vm(4, 128, 768), vf(128, 768), vm(4, 128, 768), vm(4, 128, 768), vm(4, 128, 768),
         vm(4, 128, 768), vf(4, 1, 768), vf(128, 768), vm(4, 128, 768), vm(4, 128, 192),

time: 144 us -> 130 us (0.903)
  Pallas kernels: 143 us -> 129 us
    pallas_call x1, Pallas kernels: 141 us -> 126 us  [fast_shards(): pl.pallas_call(layer_kernel, out_shape=shapes, in_specs=[pl.BlockSpec(mem...]
where the time goes in v4:
time: 130 us; the launch traced here: 129 us
  Pallas kernels  129 us (99%)
    pallas_call x1, Pallas kernels, fast_shards(): pl.pallas_call(layer_kernel, out_shape=shapes, in_specs=[pl.BlockSpec(mem...  126 us

profile of v4, /device:TPU:0, one launch (start us, length us, event | category | flops | bytes accessed | tf_op | source)
XLA Modules:
  0.0 129.5 jit_solution(14292102294486864674)
XLA Ops:
  0.6 126.4 %shard_map.187 = (bf16[128,768]{1,0:T(8,128)(2,1)}, bf16[128,768]{1,0:T(8,128)(2,1)}, f32[192,288]{1,0:T(8,128)}, f32[192,96]{1,0:T(8,128)}, f32[192,384]{1,0:T(...) custom-call(s32[2,3]{1,0:T(2,128)} %bitcast.12, s32[1,2]{1,0:T(1,128)} %glob_ref.1, ...), custom_call_target="tpu_custom_call" | custom-call | tf_op jit(solution)/shard_map/pallas_call | solution.py:1180
  127.0 2.3 %shard_map.188 = (bf16[128,768]{1,0:T(8,128)(2,1)}, bf16[128,768]{1,0:T(8,128)(2,1)}, f32[192,288]{1,0:T(8,128)}, f32[192,96]{1,0:T(8,128)}, f32[192,384]{1,0:T(...) custom-call(bf16[128,768]{1,0:T(8,128)(2,1)} %get-tuple-element.27.refs_0_, ...), custom_call_target="tpu_custom_call" | custom-call | tf_op jit(solution)/shard_map/pallas_call | solution.py:1196

commit v5 on v4

--- a/solution.py
+++ b/solution.py
@@ -308,9 +308,9 @@
 MESH = pl.DeviceIdType.MESH
 BF = jnp.bfloat16
 F32 = jnp.float32
-SENDS = 160
-RECVS = 160
-LOCALS = 16
+SENDS = 176
+RECVS = 176
+LOCALS = 24
 NEG = -1e30
 
 
@@ -335,7 +335,7 @@
 
 
 def layer_kernel(
-    rand_ref, glob_ref, doc_ref, bia, gai, ebi, hid, cot, win, wout, wexp, wshr,
+    rand_hbm, glob_hbm, doc_hbm, bia_hbm, gai_hbm, ebi_hbm, hid, cot, win, wout, wexp, wshr,
     o_out, o_gh, o_win, o_wout, o_wexp, o_wshr, o_gb, o_gg, o_ge,
     winv, woutv, win3, wout1, xg, eo, ms, mg, ps, par, win_p, wout_p, wexp_f, ws, w_in, w_out, prm,
     mq, q_s, kv, kh, vh, e_s, l_s, a_f, a_b, a_all, hg, h1_s, n1_s, r1_s, u_s, dge, g_s, ysum, yb,
@@ -344,6 +344,7 @@
     go, ro_c, tob, ro_y, tob2, fo, gi, ri_c, tib, ri_y, ti2, fi,
     vg, vr, vs1, vc, vs2, vy, qb_s, vb_s, ob, ohr, ghb, ghr,
     f_win, f_wout, f_wexp, f_wshr, f_gb, f_gg, f_ge,
+    rand_ref, glob_ref, doc_ref, bia, gai, ebi,
     ssem, rsem, lsem,
 ):
     ctx = lax.axis_index("ctx")
@@ -366,6 +367,8 @@
     def peer_rank(j):
         return 2 * flip(zl, j // 2) + flip(x, j % 2)
 
+    peers = [peer(j) for j in range(4)]
+    ranks = [peer_rank(j) for j in range(4)]
     core_mate = dev(x, y, z, 1 - c)
     y_mate = dev(x, 1 - y, z, c)
     z_mate = dev(x, y, 2 * (1 - zh) + zl, c)
@@ -398,9 +401,9 @@
         )
 
     def send(src, dst, ri, to):
-        cp = copy_to(src, dst, sends(1), ri, to)
-        cp.start()
-        pending.append(cp.wait_send)
+        si = sends(1)
+        copy_to(src, dst, si, ri, to).start()
+        pending.append(lambda: copy_to(src, dst, si, ri, to).wait_send())
 
     def send_or_keep(src, dst, ri, to):
         si = sends(1)
@@ -415,7 +418,7 @@
             pltpu.make_async_copy(src, dst, rsem.at[ri]).start()
 
         def finish():
-            @pl.when(away)
+            @pl.when(jnp.logical_or(to[0] != ctx, to[1] != seq))
             def _():
                 copy_to(src, dst, si, ri, to).wait_send()
 
@@ -424,16 +427,38 @@
     def arrived(dst, ri):
         pltpu.make_async_copy(dst, dst, rsem.at[ri]).wait()
 
-    def pass_on(buf, first):
-        for j, at in ((1, pl.ds(0, 64)), (2, pl.ds(64, 64))):
-            rank = peer_rank(j)
-            arrived(buf.at[rank], first + j)
-            send(buf.at[rank, at], buf.at[rank, at], first + 3 * (2 - j), peer(3 - j))
-
-    def far_arrived(buf, first):
-        rank = peer_rank(3)
-        arrived(buf.at[rank, pl.ds(0, 64)], first + 3)
-        arrived(buf.at[rank, pl.ds(64, 64)], first)
+    def split(rows):
+        return [(1, 0, rows), (2, rows, 128 - rows)]
+
+    def near_parts(buf, rows):
+        return [
+            (j, buf.at[ranks[j]], buf.at[ranks[j], pl.ds(at, size)] if size else None)
+            for j, at, size in split(rows)
+        ]
+
+    def pass_on(parts, first):
+        for j, block, part in parts:
+            arrived(block, first + j)
+            if part is not None:
+                send(part, part, first + 3 * (2 - j), peers[3 - j])
+
+    def far_arrived(buf, first, rows):
+        for j, at, size in split(rows):
+            if size:
+                arrived(buf.at[ranks[3], pl.ds(at, size)], first + 3 * (2 - j))
+
+    def served(step, services):
+        def run(k, carry):
+            for at, before, serve in services:
+                if before:
+                    pl.when(k == at)(serve)
+            step(k)
+            for at, before, serve in services:
+                if not before:
+                    pl.when(k == at)(serve)
+            return carry
+
+        return run
 
     barrier = pltpu.get_barrier_semaphore()
     place = 2 * ctx + c
@@ -443,7 +468,14 @@
             barrier, inc=1, device_id=(other // 2, 2 * y + other % 2), device_id_type=MESH
         )
     pl.semaphore_signal(barrier, inc=1, device_id=y_mate, device_id_type=MESH)
+    small = [
+        local(*pair)
+        for pair in ((rand_hbm, rand_ref), (glob_hbm, glob_ref), (doc_hbm, doc_ref), (bia_hbm, bia), (gai_hbm, gai), (ebi_hbm, ebi))
+    ]
     in_win, in_wout = local(win, winv), local(wout, woutv)
+
+    for copy in small:
+        copy.wait()
 
     lane = lax.broadcasted_iota(jnp.int32, (1, 128), 1)
     for i in range(2):
@@ -536,7 +568,7 @@
         arrived(win_p.at[f, slot], k_win + slot)
     send(win_p.at[f], win_p.at[f], k_win_y, y_mate)
     send(win_p.at[f], win_p.at[f], k_win_c, core_mate)
-    pass_on(xg, k_x)
+    pass_on(near_parts(xg, 64), k_x)
     k_wexp = recvs(2)
     mine_exp = wexp_f.at[f, :, pl.ds(pl.multiple_of(384 * zh, 128), 384)]
     pltpu.make_async_copy(wexp, mine_exp, rsem.at[k_wexp]).start()
@@ -608,16 +640,10 @@
             q_s[k, h, :, 0:64] = queries[:, 64 * h : 64 * h + 64]
         kv[c, pl.ds(pl.multiple_of(128 * k, 128), 128), :] = mixed[:, 192:576].astype(BF)
 
-    project(r)
-
-    def project_step(j, carry):
-        rank = peer_rank(j)
-        project(rank)
-        return carry
-
-    lax.fori_loop(1, 3, project_step, 0)
-    far_arrived(xg, k_x)
-    lax.fori_loop(3, 4, project_step, 0)
+    lax.fori_loop(
+        0, 4,
+        served(lambda j: project(peer_rank(j)), [(3, True, lambda: far_arrived(xg, k_x, 64))]), 0,
+    )
     k_kv = recvs(1)
     send(kv.at[c], kv.at[c], k_kv, core_mate)
 
@@ -637,7 +663,7 @@
 
     k_a, s_a = recvs(16), sends(16)
 
-    def attend(k, carry):
+    def attend(k):
         outs = []
         for h in range(3):
             scores = dot_nt(q_s[k, h], kh[h])
@@ -655,21 +681,26 @@
         a_all[r, k] = jnp.concatenate([low[0:64], low[64:128]], axis=1)
         for j in range(1, 4):
             at = 4 * j + k
-            copy_to(a_all.at[r, k], a_all.at[r, k], s_a + at, k_a + at, peer(j)).start()
-        return carry
-
-    lax.fori_loop(0, 1, attend, 0)
-    arrived(wout_p.at[f_y], k_wout_y)
-    send(wout_p.at[f_y], wout_p.at[f_y], k_wout_c + 1, core_mate)
-    lax.fori_loop(1, 2, attend, 0)
-    for k in range(4):
-        arrived(ws.at[k, c, :, at_half], k_wshr + k)
-    send(ws.at[:, c, :, at_half], ws.at[:, c, :, at_half], k_wshr_y, y_mate)
-    send(ws.at[:, c, :, at_half], ws.at[:, c, :, at_half], k_wshr_c, core_mate)
-    lax.fori_loop(2, 3, attend, 0)
-    arrived(wexp_f.at[f_y], k_wexp_y)
-    send(wexp_f.at[f_y], wexp_f.at[f_y], k_wexp_c + 1, core_mate)
-    lax.fori_loop(3, 4, attend, 0)
+            copy_to(a_all.at[r, k], a_all.at[r, k], s_a + at, k_a + at, peers[j]).start()
+
+    wout_there, wexp_there = wout_p.at[f_y], wexp_f.at[f_y]
+    ws_mine = ws.at[:, c, :, at_half]
+
+    def relay_0():
+        arrived(wout_there, k_wout_y)
+        send(wout_there, wout_there, k_wout_c + 1, core_mate)
+
+    def relay_1():
+        for k in range(4):
+            arrived(ws.at[k, c, :, at_half], k_wshr + k)
+        send(ws_mine, ws_mine, k_wshr_y, y_mate)
+        send(ws_mine, ws_mine, k_wshr_c, core_mate)
+
+    def relay_2():
+        arrived(wexp_there, k_wexp_y)
+        send(wexp_there, wexp_there, k_wexp_c + 1, core_mate)
+
+    lax.fori_loop(0, 4, served(attend, [(0, False, relay_0), (1, False, relay_1), (2, False, relay_2)]), 0)
     for j in range(1, 4):
         for k in range(4):
             at = 4 * j + k
@@ -697,8 +728,6 @@
             arrived(a_all.at[peer_rank(j), k], k_a + 4 * j + k)
     arrived(wexp_f.at[2 * y + 1 - c], k_wexp_c)
     arrived(wexp_f.at[2 * (1 - y) + 1 - c], k_wexp_c + 1)
-    arrived(ws.at[:, 1 - c, :, at_half], k_wshr_c)
-    arrived(ws.at[:, 1 - c, :, other_half], k_wshr_c + 1)
 
     def first_norm(k):
         rows = jnp.concatenate(
@@ -723,26 +752,43 @@
         dge[k] = below
         active = (inner * below).astype(BF)
         g_s[k] = active
-        return dot_nt(active, ws[...].reshape(768, 768))
-
+
+    def widen(k):
+        normed, inverse, hidden_one = first_norm(k)
+        n1_s[...] = normed
+        r1_s[...] = inverse
+        h1_s[...] = hidden_one
+        expand(k)
+
+    widen(ranks[3])
+    arrived(ws.at[:, 1 - c, :, at_half], k_wshr_c)
+    arrived(ws.at[:, 1 - c, :, other_half], k_wshr_c + 1)
     k_r1, s_r1 = recvs(4), sends(4)
 
     def expand_step(i, carry):
         j = 3 - i
         rank = peer_rank(j)
-        first_norm(rank)
-        yb[j] = expand(rank).astype(BF)
-        copy_to(yb.at[j], rs1.at[j], s_r1 + j, k_r1 + j, peer(j)).start()
+
+        @pl.when(i > 0)
+        def _():
+            widen(rank)
+
+        value = dot_nt(g_s[rank], ws[...].reshape(768, 768))
+
+        @pl.when(i < 3)
+        def _():
+            yb[j] = value.astype(BF)
+            copy_to(yb.at[j], rs1.at[j], s_r1 + j, k_r1 + j, peer(j)).start()
+
+        @pl.when(i == 3)
+        def _():
+            ysum[...] = value
+
         return carry
 
-    lax.fori_loop(0, 3, expand_step, 0)
+    lax.fori_loop(0, 4, expand_step, 0)
     for j in range(1, 4):
         pending.append(copy_to(yb.at[j], rs1.at[j], s_r1 + j, k_r1 + j, peer(j)).wait_send)
-    normed, inverse, hidden_one = first_norm(r)
-    n1_s[...] = normed
-    r1_s[...] = inverse
-    h1_s[...] = hidden_one
-    ysum[...] = expand(r)
 
     def slope(k, carry):
         inner = u_s[k]
@@ -784,19 +830,26 @@
         beg[k] = row_sum(inner)
         return dot_nt(low, wexp_f[...].reshape(768, 768))
 
-    ysum[...] = contract(r)
     k_r2, s_r2 = recvs(4), sends(4)
 
-    def contract_step(j, carry):
-        rank = peer_rank(j)
-        dh_b[j] = contract(rank).astype(BF)
-        copy_to(dh_b.at[j], rs2.at[j], s_r2 + j, k_r2 + j, peer(j)).start()
-        return carry
-
-    pass_on(dg, k_d)
-    lax.fori_loop(1, 3, contract_step, 0)
-    far_arrived(dg, k_d)
-    lax.fori_loop(3, 4, contract_step, 0)
+    def contract_step(j):
+        value = contract(peer_rank(j))
+
+        @pl.when(j == 0)
+        def _():
+            ysum[...] = value
+
+        @pl.when(j > 0)
+        def _():
+            dh_b[j] = value.astype(BF)
+            copy_to(dh_b.at[j], rs2.at[j], s_r2 + j, k_r2 + j, peer(j)).start()
+
+    dg_parts = near_parts(dg, 64)
+    gathered = [
+        (1, True, lambda: pass_on(dg_parts, k_d)),
+        (3, True, lambda: far_arrived(dg, k_d, 64)),
+    ]
+    lax.fori_loop(0, 4, served(contract_step, gathered), 0)
     for j in range(1, 4):
         pending.append(copy_to(dh_b.at[j], rs2.at[j], s_r2 + j, k_r2 + j, peer(j)).wait_send)
 
@@ -860,7 +913,7 @@
     for j in range(1, 3):
         send(d1g.at[r], d1g.at[r], k_d1 + j, peer(j))
 
-    def attend_back(k, carry):
+    def attend_back(k):
         outs = []
         grads = da[k].astype(F32)
         dots = grads * a_f[k]
@@ -879,24 +932,33 @@
         queries = jnp.concatenate(outs, axis=1)
         qb_s[k] = row_sum(queries)
         dz[k, :, 0:192] = queries.astype(BF)
-        return carry
-
-    lax.fori_loop(0, 1, attend_back, 0)
+
     k_fs, k_re = recvs(4), recvs(1)
-    arrived(rs_y, k_gs_y)
-    fsb[...] = (
-        gs[:, c, :, at_half].astype(F32) + rs_c[:, :, at_half].astype(F32) + rs_y[...].astype(F32)
-    ).astype(BF)
-    for k in range(4):
-        send_or_keep(fsb.at[k], fs.at[zh, x], k_fs + 2 * zh + x, dev(c, y, k, zl))
-    lax.fori_loop(1, 2, attend_back, 0)
-    arrived(re_y, k_ge_y)
-    te_f[...] = ge[at_own, :].astype(F32) + re_c[y].astype(F32) + re_y[...].astype(F32)
-    te_b[...] = te_f[:, pl.ds(pl.multiple_of(384 * (1 - zh), 128), 384)].astype(BF)
-    send(te_b, re_z, k_re, z_mate)
-    lax.fori_loop(2, 3, attend_back, 0)
-    pass_on(d1g, k_d1)
-    lax.fori_loop(3, 4, attend_back, 0)
+    shrink_owners = [dev(c, y, k, zl) for k in range(4)]
+    fs_at = fs.at[zh, x]
+    fsb_at = [fsb.at[k] for k in range(4)]
+    k_own = k_fs + 2 * zh + x
+
+    def pass_0():
+        arrived(rs_y, k_gs_y)
+        fsb[...] = (
+            gs[:, c, :, at_half].astype(F32) + rs_c[:, :, at_half].astype(F32) + rs_y[...].astype(F32)
+        ).astype(BF)
+        for k in range(4):
+            send_or_keep(fsb_at[k], fs_at, k_own, shrink_owners[k])
+
+    def pass_1():
+        arrived(re_y, k_ge_y)
+        te_f[...] = ge[at_own, :].astype(F32) + re_c[y].astype(F32) + re_y[...].astype(F32)
+        te_b[...] = te_f[:, pl.ds(pl.multiple_of(384 * (1 - zh), 128), 384)].astype(BF)
+        send(te_b, re_z, k_re, z_mate)
+
+    d1g_parts = near_parts(d1g, 0)
+
+    def pass_2():
+        pass_on(d1g_parts, k_d1)
+
+    lax.fori_loop(0, 4, served(attend_back, [(0, False, pass_0), (1, False, pass_1), (2, False, pass_2)]), 0)
     sums = []
     for h in range(3):
         rows = q_s[:, h, :, 0:64].reshape(512, 64)
@@ -952,13 +1014,6 @@
     project_grad(0, 2)
     over_cores("q")
 
-    far_arrived(d1g, k_d1)
-    part = dot_tn(a_b[...].reshape(512, 192), d1g[...].reshape(512, 768))
-    for b in range(8):
-        go[b % 2, b // 2] = pack(part[:, 96 * b : 96 * b + 96].astype(BF))
-    k_go = recvs(1)
-    send(go.at[1 - c], ro_c, k_go, core_mate)
-
     arrived(dkr, k_dk)
     keyvals = dkv[c] + dkr[...].astype(F32)
     vb_s[...] = row_sum(keyvals[:, 192:384])
@@ -991,6 +1046,13 @@
     over_y("q")
     project_grad(2, 4)
     over_cores("kv")
+
+    far_arrived(d1g, k_d1, 0)
+    part = dot_tn(a_b[...].reshape(512, 192), d1g[...].reshape(512, 768))
+    for b in range(8):
+        go[b % 2, b // 2] = pack(part[:, 96 * b : 96 * b + 96].astype(BF))
+    k_go = recvs(1)
+    send(go.at[1 - c], ro_c, k_go, core_mate)
 
     vg[...] = jnp.zeros((8, 16, 128), F32)
     rows = jnp.concatenate(
@@ -1168,6 +1230,8 @@
         vf(8, 16, 128), vf(8, 16, 128), vf(16, 128), vf(16, 128), vf(16, 128), vf(16, 128),
         vf(4, 1, 192), vf(1, 192), vm(128, 768), vm(128, 768), vm(128, 768), vm(128, 768),
         vf(192, 288), vf(192, 96), vf(192, 384), vf(96, 768), vf(6, 96), vf(2, 96), vf(3, 128),
+        pltpu.SMEM((2, 3), jnp.int32), pltpu.SMEM((1, 2), jnp.int32), pltpu.SMEM((1, 8), jnp.int32),
+        vm(6, 96), vm(2, 96), vm(3, 128),
         pltpu.SemaphoreType.DMA((SENDS,)), pltpu.SemaphoreType.DMA((RECVS,)),
         pltpu.SemaphoreType.DMA((LOCALS,)),
     ]
@@ -1180,9 +1244,7 @@
     results = pl.pallas_call(
         layer_kernel,
         out_shape=shapes,
-        in_specs=[pl.BlockSpec(memory_space=pltpu.SMEM)] * 3
-        + [pl.BlockSpec(memory_space=pltpu.VMEM)] * 3
-        + [anywhere] * 6,
+        in_specs=[anywhere] * 12,
         out_specs=(anywhere,) * 9,
         scratch_shapes=scratch,
         compiler_params=pltpu.CompilerParams(

time: 130 us -> 127 us (0.977)
  Pallas kernels: 129 us -> 126 us
    pallas_call x1, Pallas kernels: 126 us -> 124 us  [fast_shards(): pl.pallas_call(layer_kernel, out_shape=shapes, in_specs=[anywhere] * 12,...]
where the time goes in v5:
time: 127 us
  Pallas kernels  126 us (99%)
    pallas_call x1, Pallas kernels, fast_shards(): pl.pallas_call(layer_kernel, out_shape=shapes, in_specs=[anywhere] * 12,...  124 us

profile of v5, /device:TPU:0, one launch (start us, length us, event | category | flops | bytes accessed | tf_op | source)
XLA Modules:
  0.0 126.6 jit_solution(10058303962709574968)
XLA Ops:
  0.6 123.6 %shard_map.187 = (bf16[128,768]{1,0:T(8,128)(2,1)}, bf16[128,768]{1,0:T(8,128)(2,1)}, f32[192,288]{1,0:T(8,128)}, f32[192,96]{1,0:T(8,128)}, f32[192,384]{1,0:T(...) custom-call(s32[2,3]{1,0:T(2,128)} %bitcast.12, s32[1,2]{1,0:T(1,128)} %glob_hbm.1, ...), custom_call_target="tpu_custom_call" | custom-call | tf_op jit(solution)/shard_map/pallas_call | solution.py:1244
  124.2 2.3 %shard_map.188 = (bf16[128,768]{1,0:T(8,128)(2,1)}, bf16[128,768]{1,0:T(8,128)(2,1)}, f32[192,288]{1,0:T(8,128)}, f32[192,96]{1,0:T(8,128)}, f32[192,384]{1,0:T(...) custom-call(bf16[128,768]{1,0:T(8,128)(2,1)} %get-tuple-element.27.refs_0_, ...), custom_call_target="tpu_custom_call" | custom-call | tf_op jit(solution)/shard_map/pallas_call | solution.py:1258

commit v6 on v5

--- a/solution.py
+++ b/solution.py
@@ -308,8 +308,8 @@
 MESH = pl.DeviceIdType.MESH
 BF = jnp.bfloat16
 F32 = jnp.float32
-SENDS = 176
-RECVS = 176
+SENDS = 192
+RECVS = 192
 LOCALS = 24
 NEG = -1e30
 
@@ -339,7 +339,7 @@
     o_out, o_gh, o_win, o_wout, o_wexp, o_wshr, o_gb, o_gg, o_ge,
     winv, woutv, win3, wout1, xg, eo, ms, mg, ps, par, win_p, wout_p, wexp_f, ws, w_in, w_out, prm,
     mq, q_s, kv, kh, vh, e_s, l_s, a_f, a_b, a_all, hg, h1_s, n1_s, r1_s, u_s, dge, g_s, ysum, yb,
-    rs1, d2_s, dg, du_s, dh_b, rs2, beg, d1_s, d1g, dab, da, de, ds_s, dkv, dkb, dkr, dz, dx_b, rs3,
+    rd1, rd3, rs1, d2_s, dg, du_s, dh_b, rs2, beg, d1_s, d1g, dab, da, de, ds_s, dkv, dkb, dkr, dz, dx_b, rs3,
     gs, rs_c, t_shr, rs_y, fsb, fs, ge, re_c, t_exp, re_y, te_f, te_b, re_z,
     go, ro_c, tob, ro_y, tob2, fo, gi, ri_c, tib, ri_y, ti2, fi,
     vg, vr, vs1, vc, vs2, vy, qb_s, vb_s, ob, ohr, ghb, ghr,
@@ -446,6 +446,42 @@
         for j, at, size in split(rows):
             if size:
                 arrived(buf.at[ranks[3], pl.ds(at, size)], first + 3 * (2 - j))
+
+    def merging(out, rs, rd):
+        k_rs, s_rs, k_rd, s_rd = recvs(4), sends(4), recvs(2), sends(2)
+
+        def to_near(i):
+            return copy_to(
+                out.at[3, pl.ds(64 * i, 64)], rd.at[i], s_rd + i, k_rd + i, peers[1 + i]
+            )
+
+        def to_peer(j, i):
+            at = 2 * (j - 1) + i
+            rows = pl.ds(64 * i, 64)
+            return copy_to(out.at[j, rows], rs.at[j, rows], s_rs + at, k_rs + at, peers[j])
+
+        def far_done():
+            for i in range(2):
+                to_near(i).start()
+
+        def merge():
+            for j, i in ((2, 0), (1, 1)):
+                arrived(rd.at[i], k_rd + i)
+                rows = pl.ds(64 * i, 64)
+                out[j, rows] = (out[j, rows].astype(F32) + rd[i].astype(F32)).astype(BF)
+                to_peer(j, i).start()
+
+        def finish():
+            for i in range(2):
+                to_near(i).wait_send()
+                for j in (1, 2):
+                    to_peer(j, i).wait_send()
+
+        def here(j, i):
+            arrived(rs.at[j, pl.ds(64 * i, 64)], k_rs + 2 * (j - 1) + i)
+
+        pending.append(finish)
+        return far_done, lambda: to_peer(2, 1).start(), lambda: to_peer(1, 0).start(), merge, here
 
     def served(step, services):
         def run(k, carry):
@@ -763,7 +799,7 @@
     widen(ranks[3])
     arrived(ws.at[:, 1 - c, :, at_half], k_wshr_c)
     arrived(ws.at[:, 1 - c, :, other_half], k_wshr_c + 1)
-    k_r1, s_r1 = recvs(4), sends(4)
+    far_1, second_1, third_1, merge_1, here_1 = merging(yb, rs1, rd1)
 
     def expand_step(i, carry):
         j = 3 - i
@@ -778,7 +814,14 @@
         @pl.when(i < 3)
         def _():
             yb[j] = value.astype(BF)
-            copy_to(yb.at[j], rs1.at[j], s_r1 + j, k_r1 + j, peer(j)).start()
+
+        pl.when(i == 0)(far_1)
+        pl.when(i == 1)(second_1)
+
+        @pl.when(i == 2)
+        def _():
+            third_1()
+            merge_1()
 
         @pl.when(i == 3)
         def _():
@@ -787,9 +830,6 @@
         return carry
 
     lax.fori_loop(0, 4, expand_step, 0)
-    for j in range(1, 4):
-        pending.append(copy_to(yb.at[j], rs1.at[j], s_r1 + j, k_r1 + j, peer(j)).wait_send)
-
     def slope(k, carry):
         inner = u_s[k]
         dge[k] = dge[k] + inner * jnp.exp(-0.5 * inner * inner) * 0.3989422804014327
@@ -803,8 +843,9 @@
     scaled_mean = jnp.mean(scaled, axis=1, keepdims=True)
     row_shift_two = row_sum(upstream)
     second = h1_s[...] + prm[4:5, :] + ysum[...]
-    for j in range(1, 4):
-        arrived(rs1.at[j], k_r1 + j)
+    for j in range(1, 3):
+        for i in range(2):
+            here_1(j, i)
         second += rs1[j].astype(F32)
     centre = second - jnp.mean(second, axis=1, keepdims=True)
     inverse = lax.rsqrt(jnp.mean(centre * centre, axis=1, keepdims=True) + 1e-05)
@@ -1022,30 +1063,21 @@
     def input_part(k):
         return dot_nt(dz[k], w_in[...])
 
-    k_r3, s_r3 = recvs(8), sends(8)
-
-    def near(buf, j, i):
-        return buf.at[j, pl.ds(64 * i, 64)]
-
-    def input_copy(j, i):
-        at = 2 * j + i
-        return copy_to(near(dx_b, j, i), near(rs3, j, i), s_r3 + at, k_r3 + at, peer(j))
+    far_3, second_3, third_3, merge_3, here_3 = merging(dx_b, rs3, rd3)
 
     def input_step(i, carry):
         j = 3 - i
         dx_b[j] = input_part(peer_rank(j)).astype(BF)
-        input_copy(j, 0).start()
+        pl.when(i == 0)(far_3)
+        pl.when(i == 1)(second_3)
+        pl.when(i == 2)(third_3)
         return carry
 
     lax.fori_loop(0, 3, input_step, 0)
-    for j in (3, 2, 1):
-        input_copy(j, 1).start()
-    for j in range(1, 4):
-        for i in range(2):
-            pending.append(input_copy(j, i).wait_send)
     over_y("q")
     project_grad(2, 4)
     over_cores("kv")
+    merge_3()
 
     far_arrived(d1g, k_d1, 0)
     part = dot_tn(a_b[...].reshape(512, 192), d1g[...].reshape(512, 768))
@@ -1053,6 +1085,8 @@
         go[b % 2, b // 2] = pack(part[:, 96 * b : 96 * b + 96].astype(BF))
     k_go = recvs(1)
     send(go.at[1 - c], ro_c, k_go, core_mate)
+
+    over_y("kv")
 
     vg[...] = jnp.zeros((8, 16, 128), F32)
     rows = jnp.concatenate(
@@ -1074,7 +1108,6 @@
         other = (ctx + d) % 8
         send(vg.at[other], vr.at[d], k_v + d, (other, seq))
 
-    over_y("kv")
     arrived(ro_c, k_go)
     tob[...] = (go[c].astype(F32) + ro_c[...].astype(F32)).astype(BF)
     k_go_y, k_fo = recvs(1), recvs(2)
@@ -1091,8 +1124,8 @@
     def finish_input(i):
         at = pl.ds(64 * i, 64)
         grad_in = ysum[at, :]
-        for j in range(1, 4):
-            arrived(near(rs3, j, i), k_r3 + 2 * j + i)
+        for j in range(1, 3):
+            here_3(j, i)
             grad_in += rs3[j, at, :].astype(F32)
         ghb[at, :] = grad_in.astype(BF)
         send_or_keep(ghb.at[at, :], ghr.at[at, :], k_gh + i, home)
@@ -1112,8 +1145,8 @@
     f_wexp[...] = te_f[:, pl.ds(pl.multiple_of(384 * zh, 128), 384)] + re_z[...].astype(F32)
     done.append(local(f_wexp, o_wexp))
 
+    to_owners("kv")
     finish_input(1)
-    to_owners("kv")
 
     @pl.when(stays)
     def _():
@@ -1217,7 +1250,8 @@
         vm(3, 4, 128, 1024), vf(3, 4, 128, 1), vf(4, 128, 192), vm(4, 128, 192), vm(4, 4, 64, 384),
         vm(4, 128, 768), vf(128, 768), vf(128, 768), vf(128, 1), vf(4, 128, 768), vf(4, 128, 768), vm(4, 128, 768),
         vf(128, 768), vm(4, 128, 768),
-        vm(4, 128, 768), vf(128, 768), vm(4, 128, 768), vm(4, 128, 768), vm(4, 128, 768),
+        vm(2, 64, 768), vm(2, 64, 768), vm(4, 128, 768), vf(128, 768), vm(4, 128, 768),
+        vm(4, 128, 768), vm(4, 128, 768),
         vm(4, 128, 768), vf(4, 1, 768), vf(128, 768), vm(4, 128, 768), vm(4, 128, 192),
         vm(4, 128, 192), vm(4, 3, 128, 128), vm(3, 4, 128, 1024), vf(2, 512, 384), vm(512, 384),
         vm(512, 384), vm(4, 128, 576), vm(4, 128, 768), vm(4, 128, 768),

time: 127 us -> 124 us (0.976)
  Pallas kernels: 126 us -> 123 us
    pallas_call x1, Pallas kernels: 124 us -> 121 us  [fast_shards(): pl.pallas_call(layer_kernel, out_shape=shapes, in_specs=[anywhere] * 12,...]
where the time goes in v6:
time: 124 us
  Pallas kernels  123 us (99%)
    pallas_call x1, Pallas kernels, fast_shards(): pl.pallas_call(layer_kernel, out_shape=shapes, in_specs=[anywhere] * 12,...  121 us

profile of v6, /device:TPU:0, one launch (start us, length us, event | category | flops | bytes accessed | tf_op | source)
XLA Modules:
  0.0 123.6 jit_solution(16495140505593264178)
XLA Ops:
  0.6 120.5 %shard_map.187 = (bf16[128,768]{1,0:T(8,128)(2,1)}, bf16[128,768]{1,0:T(8,128)(2,1)}, f32[192,288]{1,0:T(8,128)}, f32[192,96]{1,0:T(8,128)}, f32[192,384]{1,0:T(...) custom-call(s32[2,3]{1,0:T(2,128)} %bitcast.12, s32[1,2]{1,0:T(1,128)} %glob_hbm.1, ...), custom_call_target="tpu_custom_call" | custom-call | tf_op jit(solution)/shard_map/pallas_call | solution.py:1278
  121.2 2.3 %shard_map.188 = (bf16[128,768]{1,0:T(8,128)(2,1)}, bf16[128,768]{1,0:T(8,128)(2,1)}, f32[192,288]{1,0:T(8,128)}, f32[192,96]{1,0:T(8,128)}, f32[192,384]{1,0:T(...) custom-call(bf16[128,768]{1,0:T(8,128)(2,1)} %get-tuple-element.27.refs_0_, ...), custom_call_target="tpu_custom_call" | custom-call | tf_op jit(solution)/shard_map/pallas_call | solution.py:1292

commit v7 on v6

--- a/solution.py
+++ b/solution.py
@@ -949,12 +949,20 @@
     t_exp[...] = (ge[at_y, :].astype(F32) + re_c[1 - y].astype(F32)).astype(BF)
     send(t_exp, re_y, k_ge_y, y_mate)
 
-    for j in range(1, 4):
-        arrived(da.at[peer_rank(j)], k_da + j)
-    for j in range(1, 3):
-        send(d1g.at[r], d1g.at[r], k_d1 + j, peer(j))
-
-    def attend_back(k):
+
+    d1g_mine = d1g.at[r]
+
+    def send_d1():
+        for j in range(1, 3):
+            send(d1g_mine, d1g_mine, k_d1 + j, peers[j])
+
+    def attend_back(j):
+        k = peer_rank(j)
+
+        @pl.when(j > 0)
+        def _():
+            arrived(da.at[k], k_da + j)
+
         outs = []
         grads = da[k].astype(F32)
         dots = grads * a_f[k]
@@ -999,7 +1007,7 @@
     def pass_2():
         pass_on(d1g_parts, k_d1)
 
-    lax.fori_loop(0, 4, served(attend_back, [(0, False, pass_0), (1, False, pass_1), (2, False, pass_2)]), 0)
+    lax.fori_loop(0, 4, served(attend_back, [(0, False, send_d1), (1, False, pass_0), (2, False, pass_1), (3, False, pass_2)]), 0)
     sums = []
     for h in range(3):
         rows = q_s[:, h, :, 0:64].reshape(512, 64)

time: 124 us -> 122 us (0.984)
  Pallas kernels: 123 us -> 121 us
    pallas_call x1, Pallas kernels: 121 us -> 119 us  [fast_shards(): pl.pallas_call(layer_kernel, out_shape=shapes, in_specs=[anywhere] * 12,...]
where the time goes in v7:
time: 122 us
  Pallas kernels  121 us (99%)
    pallas_call x1, Pallas kernels, fast_shards(): pl.pallas_call(layer_kernel, out_shape=shapes, in_specs=[anywhere] * 12,...  119 us

profile of v7, /device:TPU:0, one launch (start us, length us, event | category | flops | bytes accessed | tf_op | source)
XLA Modules:
  0.0 121.8 jit_solution(8122063307092421548)
XLA Ops:
  0.6 118.8 %shard_map.187 = (bf16[128,768]{1,0:T(8,128)(2,1)}, bf16[128,768]{1,0:T(8,128)(2,1)}, f32[192,288]{1,0:T(8,128)}, f32[192,96]{1,0:T(8,128)}, f32[192,384]{1,0:T(...) custom-call(s32[2,3]{1,0:T(2,128)} %bitcast.12, s32[1,2]{1,0:T(1,128)} %glob_hbm.1, ...), custom_call_target="tpu_custom_call" | custom-call | tf_op jit(solution)/shard_map/pallas_call | solution.py:1286
  119.4 2.3 %shard_map.188 = (bf16[128,768]{1,0:T(8,128)(2,1)}, bf16[128,768]{1,0:T(8,128)(2,1)}, f32[192,288]{1,0:T(8,128)}, f32[192,96]{1,0:T(8,128)}, f32[192,384]{1,0:T(...) custom-call(bf16[128,768]{1,0:T(8,128)(2,1)} %get-tuple-element.27.refs_0_, ...), custom_call_target="tpu_custom_call" | custom-call | tf_op jit(solution)/shard_map/pallas_call | solution.py:1300

commit v8 on v7

--- a/solution.py
+++ b/solution.py
@@ -604,11 +604,12 @@
         arrived(win_p.at[f, slot], k_win + slot)
     send(win_p.at[f], win_p.at[f], k_win_y, y_mate)
     send(win_p.at[f], win_p.at[f], k_win_c, core_mate)
-    pass_on(near_parts(xg, 64), k_x)
     k_wexp = recvs(2)
     mine_exp = wexp_f.at[f, :, pl.ds(pl.multiple_of(384 * zh, 128), 384)]
     pltpu.make_async_copy(wexp, mine_exp, rsem.at[k_wexp]).start()
     send(wexp, mine_exp, k_wexp + 1, z_mate)
+
+    pass_on(near_parts(xg, 64), k_x)
 
     for d in range(1, 8):
         arrived(par.at[(ctx + 8 - d) % 8], k_par + d)

time: 122 us -> 121 us (level)
  no operation moved by 1% of the time
where the time goes in v8:
time: 121 us
  Pallas kernels  120 us (99%)
    pallas_call x1, Pallas kernels, fast_shards(): pl.pallas_call(layer_kernel, out_shape=shapes, in_specs=[anywhere] * 12,...  118 us

profile of v8, /device:TPU:0, one launch (start us, length us, event | category | flops | bytes accessed | tf_op | source)
XLA Modules:
  0.0 121.3 jit_solution(14732257028616820075)
XLA Ops:
  0.6 118.2 %shard_map.187 = (bf16[128,768]{1,0:T(8,128)(2,1)}, bf16[128,768]{1,0:T(8,128)(2,1)}, f32[192,288]{1,0:T(8,128)}, f32[192,96]{1,0:T(8,128)}, f32[192,384]{1,0:T(...) custom-call(s32[2,3]{1,0:T(2,128)} %bitcast.12, s32[1,2]{1,0:T(1,128)} %glob_hbm.1, ...), custom_call_target="tpu_custom_call" | custom-call | tf_op jit(solution)/shard_map/pallas_call | solution.py:1287
  118.8 2.3 %shard_map.188 = (bf16[128,768]{1,0:T(8,128)(2,1)}, bf16[128,768]{1,0:T(8,128)(2,1)}, f32[192,288]{1,0:T(8,128)}, f32[192,96]{1,0:T(8,128)}, f32[192,384]{1,0:T(...) custom-call(bf16[128,768]{1,0:T(8,128)(2,1)} %get-tuple-element.27.refs_0_, ...), custom_call_target="tpu_custom_call" | custom-call | tf_op jit(solution)/shard_map/pallas_call | solution.py:1301
